TPU v7x, 512 devices: a whole 4x8x8 slice. The times are simulated.
512 devices in a mesh: expert: 16 (over y_hi, z), tensor: 32 (over y_lo, x, core).
Axes of the slice: x: 4, y: 8 (y_hi: 2, y_lo: 4; y = y_hi * 4 + y_lo), z: 8, core: 2. Of those that a mesh axis runs over, the one named last changes fastest.
Arguments:
- residual: bfloat16 [2048, 2048], P('expert', 'tensor'), may hold values from -6 to 6
- heads_out: bfloat16 [2048, 2048], P('expert', 'tensor'), may hold values from -6 to 6
- out_weight: bfloat16 [2048, 2048], P(None, 'tensor'), may hold values from -0.125 to 0.125
- norm_gain: float32 [2048], P('tensor'), may hold values from 0.5 to 1.5
- up_weight: bfloat16 [32, 2048, 8192], P('expert', None, 'tensor'), may hold values from -0.125 to 0.125
- down_weight: bfloat16 [32, 8192, 2048], P('expert', 'tensor'), may hold values from -0.0625 to 0.0625
- routes: int32 [2048, 2], P('expert'), may hold values from 0 to 31, all different within a row; in each aligned block of 128 rows (0 to 127, 128 to 255, ...) at most 9 rows name the same one
- gate_values: float32 [2048, 2], P('expert'), may hold values from 0.2 to 1
- cotangent: bfloat16 [2048, 2048], P('expert', 'tensor'), may hold values from -6 to 6
Outputs:
- result: bfloat16 [2048, 2048], P('expert', 'tensor')
- grad_residual: bfloat16 [2048, 2048], P('expert', 'tensor')
- grad_heads: bfloat16 [2048, 2048], P('expert', 'tensor')
- grad_out_weight: bfloat16 [2048, 2048], P(None, 'tensor')
Inputs may be any that keep to these rules, and one draw needn't show every extreme that they name: `routes`: each row names two different experts. Among the 128 rows of one index of expert (aligned blocks), no expert is named by more than 9 rows, a bound that some block reaches.
All inputs are finite; a program needn't handle non-finite values.
Results may differ from a plain program's by a relative error of at most 0.019.
Values may be sent and summed in bfloat16 or wider, within the bound.
No kernel may reach another device: no remote copies, remote signals or barrier semaphores. Data moves between devices by JAX's collectives and lax.ppermute only.
A program may use at most 128 MiB of HBM per device.

v0:
```python
import jax
import jax.numpy as jnp
from jax import lax
from jax.sharding import PartitionSpec as P


def activate(value):
    return jax.nn.gelu(value, approximate=True)


def route_tables(routes, gate_values, experts, capacity):
    rows_here = routes.shape[0]
    flat_ids = routes.reshape(-1)
    onehot = (flat_ids[:, None] == jnp.arange(experts, dtype=jnp.int32)[None, :]).astype(jnp.int32)
    earlier = jnp.cumsum(onehot, axis=0) - onehot
    places = jnp.sum(earlier * onehot, axis=1)
    target = (flat_ids * capacity + places).reshape(rows_here, 2)
    slot_ids = jnp.arange(experts * capacity, dtype=jnp.int32)
    matches = (slot_ids[:, None, None] == target[None, :, :]).astype(jnp.float32)
    slot_placement = jnp.sum(matches, axis=2)
    gate_weighted = jnp.sum(matches * gate_values[None, :, :], axis=2)
    return (slot_placement, gate_weighted)


def local(
    residual,
    heads_out,
    out_weight,
    norm_gain,
    up_weight,
    down_weight,
    routes,
    gate_values,
    cotangent,
):
    highest_precision = lax.Precision.HIGHEST
    groups = lax.axis_size("expert")
    local_experts = up_weight.shape[0]
    experts = groups * local_experts
    rows_here = residual.shape[0]
    part_width = residual.shape[1]
    full_width = out_weight.shape[0]
    capacity = 9 * rows_here // (4 * experts)
    slot_placement, gate_weighted = route_tables(routes, gate_values, experts, capacity)
    heads_whole = lax.all_gather(heads_out, "tensor", axis=1, tiled=True)
    mixed = jnp.dot(heads_whole, out_weight, preferred_element_type=jnp.float32)
    stream = residual.astype(jnp.float32) + mixed
    row_sums, squares = lax.psum(
        (jnp.sum(stream, axis=1), jnp.sum(stream * stream, axis=1)), "tensor"
    )
    center = row_sums / full_width
    inv_scale = lax.rsqrt(squares / full_width - center * center + 1e-05)
    normal = (stream - center[:, None]) * inv_scale[:, None]
    normed = (normal * norm_gain[None, :]).astype(jnp.bfloat16)
    placing_low = slot_placement.astype(jnp.bfloat16)
    outgoing = jnp.dot(placing_low, normed, preferred_element_type=jnp.float32).astype(jnp.bfloat16)
    outgoing = outgoing.reshape(groups, local_experts, capacity, part_width)
    arrived = lax.all_to_all(outgoing, "expert", split_axis=0, concat_axis=0, tiled=True)
    slot_rows = lax.all_gather(arrived, "tensor", axis=3, tiled=True)
    pre_act = jnp.einsum("becd,edf->ebcf", slot_rows, up_weight, preferred_element_type=jnp.float32)
    hidden_f, pullback = jax.vjp(activate, pre_act)
    hidden = hidden_f.astype(jnp.bfloat16)
    matrix = down_weight
    expert_part = lax.psum_scatter(
        jnp.einsum("ebcf,efd->dbec", hidden, matrix, preferred_element_type=jnp.float32).astype(
            jnp.bfloat16
        ),
        "tensor",
        scatter_dimension=0,
        tiled=True,
    )
    returned = lax.all_to_all(expert_part, "expert", split_axis=1, concat_axis=1, tiled=True)
    returned = returned.reshape(part_width, experts * capacity).astype(jnp.float32)
    expert_mixture = jnp.einsum("qt,fq->tf", gate_weighted, returned, precision=highest_precision)
    result = (stream + expert_mixture).astype(jnp.bfloat16)
    cot_wide = cotangent.astype(jnp.float32)
    grad_out = jnp.dot(gate_weighted, cot_wide, precision=highest_precision).astype(jnp.bfloat16)
    grad_out = grad_out.reshape(groups, local_experts, capacity, part_width)
    grad_arrived = lax.all_to_all(grad_out, "expert", split_axis=0, concat_axis=0, tiled=True)
    grad_rows = lax.all_gather(grad_arrived, "tensor", axis=3, tiled=True)
    grad_hidden = jnp.einsum(
        "becd,efd->ebcf", grad_rows, down_weight, preferred_element_type=jnp.float32
    )
    grad_act = pullback(grad_hidden)[0].astype(jnp.bfloat16)
    matrix = up_weight
    grad_part = lax.psum_scatter(
        jnp.einsum("ebcf,edf->dbec", grad_act, matrix, preferred_element_type=jnp.float32).astype(
            jnp.bfloat16
        ),
        "tensor",
        scatter_dimension=0,
        tiled=True,
    )
    grad_back = lax.all_to_all(grad_part, "expert", split_axis=1, concat_axis=1, tiled=True)
    grad_back = grad_back.reshape(part_width, experts * capacity).astype(jnp.float32)
    normed_gradient = jnp.einsum(
        "qt,fq->tf", slot_placement, grad_back, precision=highest_precision
    )
    grad_scaled = normed_gradient * norm_gain[None, :]
    sum_first, sum_second = lax.psum(
        (jnp.sum(grad_scaled, axis=1), jnp.sum(grad_scaled * normal, axis=1)), "tensor"
    )
    grad_stream = cot_wide + inv_scale[:, None] * (
        grad_scaled - sum_first[:, None] / full_width - normal * (sum_second[:, None] / full_width)
    )
    grad_residual = grad_stream.astype(jnp.bfloat16)
    matrix = out_weight
    grad_heads = lax.psum_scatter(
        lax.dot_general(
            matrix, grad_residual, (((1,), (1,)), ((), ())), preferred_element_type=jnp.float32
        ),
        "tensor",
        scatter_dimension=0,
        tiled=True,
    ).T.astype(jnp.bfloat16)
    weight_terms = lax.dot_general(
        heads_whole, grad_residual, (((0,), (0,)), ((), ())), preferred_element_type=jnp.float32
    )
    grad_out_weight = lax.psum(weight_terms, "expert").astype(jnp.bfloat16)
    return (result, grad_residual, grad_heads, grad_out_weight)


def solution(mesh):
    return jax.shard_map(
        local,
        mesh=mesh,
        in_specs=(
            P("expert", "tensor"),
            P("expert", "tensor"),
            P(None, "tensor"),
            P("tensor"),
            P("expert", None, "tensor"),
            P("expert", "tensor", None),
            P("expert", None),
            P("expert", None),
            P("expert", "tensor"),
        ),
        out_specs=(
            P("expert", "tensor"),
            P("expert", "tensor"),
            P("expert", "tensor"),
            P(None, "tensor"),
        ),
        check_vma=False,
    )
```

profile of v0, /device:TPU:63, one launch (start us, length us, event | category | flops | bytes accessed | tf_op | source)
XLA Modules:
  0.0 786.3 jit_solution(15927243014625623555)
XLA Ops:
  7.2 0.0 all-gather.3.cloned.1.call-start
  7.2 0.9 copy.84
  8.2 0.1 eq.43
  8.3 0.1 eq.39
  8.5 38.9 %all_gather.9 = bf16[128,2048]{0,1:T(8,128)(2,1)S(1)} all-gather(bf16[128,64]{0,1:T(8,128)(2,1)} %param.10), channel_id=1, replica_groups=mesh['expert'=16,'tensor'=32] {'tensor'}, dimensions={1}, use_global_device_ids=true | all-gather | bytes 540672 | tf_op jit(solution)/shard_map/all_gather | solution.py:45
  47.3 0.6 reduce-window.6
  47.9 0.2 slice_reduce_fusion
  48.2 0.1 fusion.42
  48.3 0.1 reduce_sum.66
  48.4 0.1 copy.87
  48.5 0.7 multiply_add_fusion
  49.2 1.2 fusion.58
  50.4 68.1 %all-reduce.1 = (f32[128]{0:T(128)S(1)}, f32[128]{0:T(128)S(1)}) all-reduce(f32[128]{0:T(128)S(1)} %get-tuple-element.31, f32[128]{0:T(128)S(1)} %get-tuple-element.30), channel_id=1, replica_groups=mesh['expert'=16,'tensor'=32] {'tensor'}, use_global_device_ids=true, to_apply=%region_8.9 | all-reduce | flops 256 | bytes 2048 | tf_op jit(solution)/shard_map/psum | solution.py:48
  118.5 0.8 convert_reduce_fusion
  119.2 0.2 convolution_convert_fusion.3
  119.5 0.1 copy.88
  119.6 0.1 copy.124
  119.7 0.1 reshape.66
  119.8 21.6 %all_to_all.20 = bf16[16,2,576]{2,1,0:T(2,128)(2,1)S(1)} all-to-all(bf16[16,2,576]{2,1,0:T(2,128)(2,1)S(1)} %reshape.66), channel_id=1, replica_groups=mesh['expert'=16,'tensor'=32] {'expert'}, dimensions={0} | all-to-all | bytes 73728 | tf_op jit(solution)/shard_map/all_to_all | solution.py:58
  141.4 0.1 reshape.67
  141.6 0.9 copy.90
  142.5 0.0 all-gather.5.cloned.1.call-start
  142.6 0.2 convolution_convert_fusion.2
  142.8 0.1 copy.94
  142.9 0.1 copy.123
  143.0 0.1 reshape.70
  143.1 13.7 %all_to_all.21 = bf16[16,2,576]{2,1,0:T(2,128)(2,1)S(1)} all-to-all(bf16[16,2,576]{2,1,0:T(2,128)(2,1)S(1)} %reshape.70), channel_id=1, replica_groups=mesh['expert'=16,'tensor'=32] {'expert'}, dimensions={0} | all-to-all | bytes 73728 | tf_op jit(solution)/shard_map/all_to_all | solution.py:79
  156.8 0.1 reshape.71
  157.0 0.9 copy.96
  157.9 0.0 reduce-scatter.12.cloned.1.call-start
  158.0 54.5 %all-gather.3.cloned.1.call-done = bf16[16,2,9,2048]{0,1,2,3:T(2,128)(2,1)} async-done(((bf16[16,2,9,64]{0,1,2,3:T(2,128)(2,1)}), bf16[16,2,9,2048]{0,1,2,3:T(2,128)(2,1)}) %all-gather.3.cloned.1.call-update) | async-done | bytes 1179664 | tf_op jit(solution)/shard_map/all_gather | solution.py:59
  212.5 7.6 fusion.2
  220.1 66.6 %all-gather.5.cloned.1.call-done = bf16[16,2,9,2048]{0,1,2,3:T(2,128)(2,1)} async-done(((bf16[16,2,9,64]{0,1,2,3:T(2,128)(2,1)}), bf16[16,2,9,2048]{0,1,2,3:T(2,128)(2,1)}) %all-gather.5.cloned.1.call-update) | async-done | bytes 1179664 | tf_op jit(solution)/shard_map/all_gather | solution.py:80
  286.7 7.5 fusion.5
  294.3 22.8 %copy.105 = bf16[2048,16,2,9]{1,3,2,0:T(8,128)(2,1)} copy(bf16[2048,16,2,9]{0,1,3,2:T(8,128)(2,1)S(1)} %fusion.5) | data formatting | bytes 2359296
  317.1 18.8 %reshape.61 = bf16[2048,288]{1,0:T(8,128)(2,1)} reshape(bf16[2048,2,9,16]{3,2,1,0:T(8,128)(2,1)} %bitcast.83) | data formatting | bytes 2359296
  335.9 0.2 reduce-scatter.10.cloned.1.call-start
  336.2 1.5 fusion.4
  337.7 22.8 %copy.103 = bf16[2048,16,2,9]{1,3,2,0:T(8,128)(2,1)} copy(bf16[2048,16,2,9]{0,1,3,2:T(8,128)(2,1)S(1)} %fusion.4) | data formatting | bytes 2359296
  360.5 18.9 %reshape.59 = bf16[2048,288]{1,0:T(8,128)(2,1)} reshape(bf16[2048,2,9,16]{3,2,1,0:T(8,128)(2,1)} %bitcast.84) | data formatting | bytes 2359296
  379.4 0.0 reduce-scatter.14.cloned.1.call-start
  379.4 103.3 %reduce-scatter.12.cloned.1.call-done = bf16[64,288]{1,0:T(8,128)(2,1)} async-done(((bf16[2048,288]{1,0:T(8,128)(2,1)}), bf16[64,288]{1,0:T(8,128)(2,1)}) %reduce-scatter.12.cloned.1.call-update) | async-done | bytes 36880
  482.7 1.2 reshape.62
  484.0 0.4 copy.98
  484.4 0.1 reshape.72
  484.5 18.1 %all_to_all.22 = bf16[16,2,576]{2,1,0:T(2,128)(2,1)S(1)} all-to-all(bf16[16,2,576]{2,1,0:T(2,128)(2,1)S(1)} %reshape.72), channel_id=1, replica_groups=mesh['expert'=16,'tensor'=32] {'expert'}, dimensions={0} | all-to-all | bytes 73728 | tf_op jit(solution)/shard_map/all_to_all | solution.py:94
  502.6 0.1 reshape.73
  502.8 0.3 fusion.57
  503.1 66.9 %all-reduce = (f32[128]{0:T(128)S(1)}, f32[128]{0:T(128)S(1)}) all-reduce(f32[128]{0:T(128)S(1)} %get-tuple-element.29, f32[128]{0:T(128)S(1)} %get-tuple-element.28), channel_id=1, replica_groups=mesh['expert'=16,'tensor'=32] {'tensor'}, use_global_device_ids=true, to_apply=%region_14.15 | all-reduce | flops 256 | bytes 2048 | tf_op jit(solution)/shard_map/psum | solution.py:100
  570.0 1.3 convolution_bitcast_fusion
  571.3 2.6 copy.107
  573.9 55.9 %reduce-scatter.10.cloned.1.call-done = bf16[64,288]{1,0:T(8,128)(2,1)} async-done(((bf16[2048,288]{1,0:T(8,128)(2,1)}), bf16[64,288]{1,0:T(8,128)(2,1)}) %reduce-scatter.10.cloned.1.call-update) | async-done | bytes 36880
  629.8 1.2 reshape.60
  631.0 0.4 copy.92
  631.5 0.7 reshape.68
  632.2 12.5 %all-to-all-start.1 = ((bf16[16,2,576]{2,1,0:T(2,128)(2,1)}), bf16[16,2,576]{2,1,0:T(2,128)(2,1)S(1)}, u32[]{:S(2)}, u32[]{:S(2)}) async-start(bf16[16,2,576]{2,1,0:T(2,128)(2,1)} %reshape.68), calls=%async_computation.1 | async-start | bytes 81920 | tf_op jit(solution)/shard_map/all_to_all | solution.py:72
  644.7 0.3 convolution_bitcast_fusion.1
  645.0 6.0 all-to-all-done.1
  651.0 0.1 reshape.69
  651.2 0.9 fusion.10
  652.1 91.8 %all-reduce.3 = bf16[2048,64]{0,1:T(8,128)(2,1)} all-reduce(f32[2048,64]{0,1:T(8,128)S(1)} %convolution_bitcast_fusion.1), channel_id=1, replica_groups=mesh['expert'=16,'tensor'=32] {'expert'}, use_global_device_ids=true, to_apply=%region_16.17 | all-reduce | flops 131072 | bytes 786432 | tf_op jit(solution)/shard_map/psum | solution.py:119
  743.8 34.4 %reduce-scatter.14.cloned.1.call-done = f32[64,128]{1,0:T(8,128)} async-done(((f32[2048,128]{1,0:T(8,128)}), f32[64,128]{1,0:T(8,128)}) %reduce-scatter.14.cloned.1.call-update) | async-done | bytes 32784
  778.2 0.9 copy.108
  779.1 0.7 copy.100
  (35 shorter events, 0.4 us)
Async XLA Ops:
  7.2 279.6 %copy-start = (bf16[2,256,2048]{2,1,0:T(8,128)(2,1)S(1)}, bf16[2,256,2048]{2,1,0:T(8,128)(2,1)}, u32[]{:S(2)}) copy-start(bf16[2,256,2048]{2,1,0:T(8,128)(2,1)} %param.14) | copy-start | bytes 6291460
  7.2 112.1 %copy-start.8 = (f32[64]{0:T(128)S(1)}, f32[64]{0:T(128)}, u32[]{:S(2)}) copy-start(f32[64]{0:T(128)} %param.12) | copy-start | bytes 772
  7.2 135.4 %copy-start.7 = (bf16[128,64]{0,1:T(8,128)(2,1)S(1)}, bf16[128,64]{0,1:T(8,128)(2,1)}, u32[]{:S(2)}) copy-start(bf16[128,64]{0,1:T(8,128)(2,1)} %param.17) | copy-start | bytes 49156
  7.2 205.3 %all-gather.3.cloned.1.call-start = ((), (), s32[]{:S(2)}) async-start(), calls=%async_computation.7 | async-start | bytes 9732096 | tf_op jit(solution)/shard_map/all_gather | solution.py:59
  47.3 109.7 %copy-start.1 = (bf16[128,2048]{0,1:T(8,128)(2,1)}, bf16[128,2048]{0,1:T(8,128)(2,1)S(1)}, u32[]{:S(2)}) copy-start(bf16[128,2048]{0,1:T(8,128)(2,1)S(1)} %all_gather.9) | copy-start | bytes 1572868
  119.2 100.9 %copy-start.3 = (f32[288,128]{1,0:T(8,128)}, f32[288,128]{1,0:T(8,128)S(1)}, u32[]{:S(2)}) copy-start(f32[288,128]{1,0:T(8,128)S(1)} %get-tuple-element.33) | copy-start | bytes 442372
  142.5 144.2 %all-gather.5.cloned.1.call-start = ((), (), s32[]{:S(2)}) async-start(), calls=%async_computation.8 | async-start | bytes 9732096 | tf_op jit(solution)/shard_map/all_gather | solution.py:80
  157.9 324.8 %reduce-scatter.12.cloned.1.call-start = ((), (), s32[]{:S(2)}) async-start(), calls=%async_computation.10 | async-start | bytes 1622016
  335.9 293.9 %reduce-scatter.10.cloned.1.call-start = ((), (), s32[]{:S(2)}) async-start(), calls=%async_computation.9 | async-start | bytes 1622016
  379.3 190.7 %copy-start.5 = (bf16[2048,64]{0,1:T(8,128)(2,1)S(1)}, bf16[2048,64]{0,1:T(8,128)(2,1)}, u32[]{:S(2)}) copy-start(bf16[2048,64]{0,1:T(8,128)(2,1)} %param.11) | copy-start | bytes 786436
  379.4 398.9 %reduce-scatter.14.cloned.1.call-start = ((), (), s32[]{:S(2)}) async-start(), calls=%async_computation.11 | async-start | bytes 1081344
  570.0 74.7 %copy-start.6 = (bf16[128,64]{0,1:T(8,128)(2,1)}, bf16[128,64]{0,1:T(8,128)(2,1)S(1)}, u32[]{:S(2)}) copy-start(bf16[128,64]{0,1:T(8,128)(2,1)S(1)} %add_convert_fusion) | copy-start | bytes 49156
  571.3 73.4 %copy-start.2 = (bf16[128,2048]{0,1:T(8,128)(2,1)S(1)}, bf16[128,2048]{0,1:T(8,128)(2,1)}, u32[]{:S(2)}) copy-start(bf16[128,2048]{0,1:T(8,128)(2,1)} %copy-done.1) | copy-start | bytes 1572868
  573.9 77.3 %copy-start.4 = (f32[288,128]{1,0:T(8,128)S(1)}, f32[288,128]{1,0:T(8,128)}, u32[]{:S(2)}) copy-start(f32[288,128]{1,0:T(8,128)} %copy-done.3) | copy-start | bytes 442372
  632.2 18.8 %all-to-all-start.1 = ((bf16[16,2,576]{2,1,0:T(2,128)(2,1)}), bf16[16,2,576]{2,1,0:T(2,128)(2,1)S(1)}, u32[]{:S(2)}, u32[]{:S(2)}) async-start(bf16[16,2,576]{2,1,0:T(2,128)(2,1)} %reshape.68), calls=%async_computation.1 | async-start | bytes 81920 | tf_op jit(solution)/shard_map/all_to_all | solution.py:72
Sparse Core Ops, SparseCore 0:
  142.6 69.8 all-gather.2
  214.7 72.0 all-gather.4
  336.0 146.6 reduce-scatter.11
  485.6 144.1 reduce-scatter.9
  632.5 145.7 reduce-scatter.13
where the time goes:
time: 788 us; the launch traced here: 786 us
  waiting for transfers between devices  321 us (41%)
  blocking collectives  319 us (40%)
  local copies, waits for them, and re-layouts  96.3 us (12%)
  matrix products  21 us (3%)
  between operations  14 us (2%)
  starting transfers between devices  12.9 us (2%)
    unnamed x8, waiting for transfers between devices  194 us
    unnamed x36, local copies, waits for them, and re-layouts  92.4 us
    psum x1, blocking collectives, local(): grad_out_weight = lax.psum(weight_terms, 'expert').astype(jnp.bfloat16)  91.8 us
    psum x1, blocking collectives, local(): lax.psum((jnp.sum(stream, axis=1), jnp.sum(stream * stream, axis=1)), 'te...  68.1 us
    psum x1, blocking collectives, local(): lax.psum((jnp.sum(grad_scaled, axis=1), jnp.sum(grad_scaled * normal, axi...  66.9 us
    all_gather x1, waiting for transfers between devices, local(): grad_rows = lax.all_gather(grad_arrived, 'tensor', axis=3, tiled=True)  66.6 us
    all_gather x1, waiting for transfers between devices, local(): slot_rows = lax.all_gather(arrived, 'tensor', axis=3, tiled=True)  54.5 us
    all_gather x1, blocking collectives, local(): heads_whole = lax.all_gather(heads_out, 'tensor', axis=1, tiled=True)  38.9 us
  transfers between devices with their start and end apart: 6, of which 6 were waited for; matrix products, arithmetic and copies ran while one was open for 8% of the time, Pallas kernels for 0%

commit v1 on v0

v1 whole, which is shorter than its diff:
```python
import jax
import jax.numpy as jnp
from jax import lax
from jax.experimental import pallas as pl
from jax.experimental.pallas import tpu as pltpu
from jax.sharding import Mesh, PartitionSpec as P

AXES = ("yh", "z", "yl", "x", "c")
EXPERT = ("yh", "z")
TENSOR = ("yl", "x", "c")
SPLIT = (2, 8, 4, 4, 2)
BLOCKS = 16
CAP = 9
MSG = 24
PACK = 320
SLOTS = BLOCKS * CAP
ROWS = BLOCKS * MSG
WIDTH = 2048
HID = 256
F32 = jnp.float32
BF16 = jnp.bfloat16
HIGHEST = lax.Precision.HIGHEST
ROOT = 0.7978845608028654
CUBIC = 0.044715


def iota(shape, axis):
    return lax.broadcasted_iota(jnp.int32, shape, axis)


def div(value, by):
    scale = -(-(1 << 14) // by)
    return lax.shift_right_logical(value * scale, 14)


def dot_nn(a, b, **kw):
    return lax.dot_general(a, b, (((1,), (0,)), ((), ())), preferred_element_type=F32, **kw)


def dot_nt(a, b, **kw):
    return lax.dot_general(a, b, (((1,), (1,)), ((), ())), preferred_element_type=F32, **kw)


def dot_tn(a, b, **kw):
    return lax.dot_general(a, b, (((0,), (0,)), ((), ())), preferred_element_type=F32, **kw)


def eye(n):
    return (iota((n, n), 0) == iota((n, n), 1)).astype(F32).astype(BF16)


def call(kernel, outs, name, n_smem=0, n_in=0):
    return pl.pallas_call(
        kernel,
        out_shape=outs,
        in_specs=[pl.BlockSpec(memory_space=pltpu.SMEM)] * n_smem
        + [pl.BlockSpec(memory_space=pltpu.VMEM)] * n_in,
        name=name,
        compiler_params=pltpu.CompilerParams(vmem_limit_bytes=48 * 1024 * 1024),
    )


def shape(dims, dtype):
    return jax.ShapeDtypeStruct(dims, dtype)


def split_two(value):
    high = value.astype(BF16)
    low = (value - high.astype(F32)).astype(BF16)
    return high, low


def prepare(core_ref, heads_ref, routes_ref, gates_ref, heads_t_ref, place_ref, gate_ref):
    turned = dot_nt(eye(64), heads_ref[...]).astype(BF16)
    for i in range(16):
        heads_t_ref[i] = turned
    core = core_ref[0]
    row = iota((ROWS, 128), 0)
    group = div(row, MSG)
    local = row - group * MSG
    slot = jnp.where(local < CAP, local, local - CAP)
    used = local < 2 * CAP
    expert = 2 * group + core
    first = (routes_ref[0:1, :] == expert) & used
    second = (routes_ref[1:2, :] == expert) & used
    named = jnp.where(first | second, 1.0, 0.0)
    before = (iota((128, 128), 0) < iota((128, 128), 1)).astype(F32).astype(BF16)
    earlier = dot_nn(named.astype(BF16), before)
    taken = (earlier == slot.astype(F32)) & (named > 0.5)
    place_ref[...] = jnp.where(taken, 1.0, 0.0).astype(BF16)
    gate = jnp.where(first, gates_ref[0:1, :], gates_ref[1:2, :])
    gate_ref[...] = jnp.where(taken, gate, 0.0)


def project(core_ref, heads_ref, weight_ref, residual_ref, cotangent_ref, gain_ref, out_ref):
    parts = []
    for chip in range(16):
        parts.append(heads_ref[0, chip])
        parts.append(heads_ref[1, chip])
    heads_t = jnp.concatenate(parts, axis=0)
    mixed = dot_tn(weight_ref[...], heads_t)
    out_ref[0:64] = dot_nt(eye(64), residual_ref[...]) + mixed
    out_ref[64:128] = dot_nt(eye(64), cotangent_ref[...])
    mine = div(iota((8, 128), 1), 64) == core_ref[0]
    out_ref[128:136] = jnp.where(mine, jnp.broadcast_to(gain_ref[...], (8, 128)), 0.0)


def dispatch(both_ref, place_ref, gate_ref, out_ref):
    stream = jnp.concatenate([both_ref[0, 0:64], both_ref[1, 0:64]], axis=0)
    cot = jnp.concatenate([both_ref[0, 64:128], both_ref[1, 64:128]], axis=0)
    gain = both_ref[0, 128:129] + both_ref[1, 128:129]
    shift = jnp.mean(stream, axis=0, keepdims=True)
    centered = (stream - shift).astype(BF16)
    place = place_ref[...]
    placed = place.astype(F32)
    rows_x = dot_nt(place, centered)
    rows_c = dot_nt(place, cot.astype(BF16))
    gate_col = jnp.sum(gate_ref[...], axis=1, keepdims=True)
    shift_col = jnp.sum(placed * shift, axis=1, keepdims=True)
    row = iota((ROWS, 128), 0)
    lane = iota((ROWS, 128), 1)
    local = row - div(row, MSG) * MSG
    high, low = split_two(shift_col)
    spread = jnp.where(lane == local, high.astype(F32), 0.0)
    spread = spread + jnp.where(lane == local + 16, low.astype(F32), 0.0)
    spread = jnp.where(local < CAP, spread, 0.0).astype(BF16)
    to = iota((ROWS, ROWS), 0)
    come = iota((ROWS, ROWS), 1)
    to_group = div(to, MSG)
    gather = (to - to_group * MSG == 18) & (to_group == div(come, MSG))
    stats = dot_nn(jnp.where(gather, 1.0, 0.0).astype(BF16), spread)
    gain_high, gain_low = split_two(gain)
    rest = gain - gain_high.astype(F32) - gain_low.astype(F32)
    value = jnp.where(local < CAP, rows_x, jnp.where(local < 2 * CAP, rows_c * gate_col, stats))
    value = jnp.where(local == 19, gain_high.astype(F32), value)
    value = jnp.where(local == 20, gain_low.astype(F32), value)
    value = jnp.where(local == 21, rest, value)
    value = value.astype(BF16)
    for e in range(BLOCKS):
        piece = value[e * MSG : (e + 1) * MSG]
        for y in range(4):
            out_ref[e, y] = piece


def repack(in_ref, out_ref):
    to = iota((PACK, ROWS), 0)
    come = iota((PACK, ROWS), 1)
    group = div(come, MSG)
    local = come - group * MSG
    pick = (local < CAP) & (to == group * CAP + local)
    pick |= (local >= CAP) & (local < 2 * CAP) & (to == SLOTS + group * CAP + local - CAP)
    pick |= (local == 18) & (to == 2 * SLOTS + group)
    pick |= (group == 0) & (local >= 19) & (local < 22) & (to == 304 + local - 19)
    pick = jnp.where(pick, 1.0, 0.0).astype(BF16)
    for y in range(4):
        rows = in_ref[:, y].astype(F32).reshape(ROWS, 128).astype(BF16)
        packed = dot_nn(pick, rows).astype(BF16)
        for x in range(4):
            out_ref[x, y] = packed


def experts(which_ref, in_ref, up_ref, down_ref, out_ref):
    slot = iota((SLOTS, 128), 0)
    lane = iota((SLOTS, 128), 1)
    block = div(slot, CAP)
    local = slot - block * CAP
    expand = (div(iota((SLOTS, 16), 0), CAP) == iota((SLOTS, 16), 1)).astype(F32).astype(BF16)
    shift_lane = (lane == local) | (lane == local + 16)
    chunks = [None] * 16
    cots = [None] * 16
    gains = [None] * 16
    total = jnp.zeros((SLOTS, 128), F32)
    for x in range(4):
        for y in range(4):
            shift = dot_nn(expand, in_ref[x, y, 288:304])
            shift = jnp.sum(jnp.where(shift_lane, shift, 0.0), axis=1, keepdims=True)
            chunk = in_ref[x, y, 0:144].astype(F32) + shift
            total = total + chunk
            chunks[y * 4 + x] = chunk
            cots[y * 4 + x] = in_ref[x, y, 144:288]
            gains[y * 4 + x] = in_ref[x, y, 304:320]
    center = jnp.sum(total, axis=1, keepdims=True) / WIDTH
    squares = jnp.zeros((SLOTS, 128), F32)
    for i in range(16):
        chunks[i] = chunks[i] - center
        squares = squares + chunks[i] * chunks[i]
    inv_scale = lax.rsqrt(jnp.sum(squares, axis=1, keepdims=True) / WIDTH + 1e-05)
    rows = []
    for i in range(16):
        parts = gains[i].astype(F32)
        gain = parts[0:1] + parts[1:2] + parts[2:3]
        rows.append((chunks[i] * inv_scale * gain).astype(BF16))
    rows = jnp.concatenate(
        [jnp.concatenate(rows, axis=1), jnp.concatenate(gains, axis=1)], axis=0
    )
    up = up_ref[0]
    down = down_ref[0]
    product = dot_nn(rows, up)
    pre = product[0:SLOTS]
    weigh = product[SLOTS : SLOTS + 1] + product[SLOTS + 1 : SLOTS + 2]
    weigh = weigh + product[SLOTS + 2 : SLOTS + 3]
    grad_hidden = dot_nt(jnp.concatenate(cots, axis=1), down)
    bend = jnp.tanh(ROOT * (pre + CUBIC * pre * pre * pre))
    hidden = (0.5 * pre * (1.0 + bend)).astype(BF16)
    slope = 0.5 * (1.0 + bend) + 0.5 * pre * (1.0 - bend * bend) * (
        ROOT * (1.0 + 3.0 * CUBIC * pre * pre)
    )
    grad_act = (grad_hidden * slope).astype(BF16)
    value = dot_nn(hidden, down).astype(BF16)
    grad_in = dot_nt(grad_act, up).astype(BF16)
    wide = grad_act.astype(F32)
    sum_first = jnp.sum(wide * weigh, axis=1, keepdims=True)
    sum_second = jnp.sum(wide * pre, axis=1, keepdims=True)
    spread = jnp.where(lane == local, sum_first, 0.0)
    spread = spread + jnp.where(lane == local + 16, sum_second, 0.0)
    spread = spread + jnp.where(lane == local + 32, center * (1.0 / 32), 0.0)
    spread = spread + jnp.where(lane == local + 48, inv_scale * (1.0 / 32), 0.0)
    high, low = split_two(spread)
    collect = (iota((16, SLOTS), 0) == div(iota((16, SLOTS), 1), CAP)).astype(F32).astype(BF16)
    high = dot_nn(collect, high).astype(BF16)
    low = dot_nn(collect, low).astype(BF16)
    for x in range(4):
        for y in range(4):
            at = (y * 4 + x) * 128
            out_ref[x, y, 0:144] = value[:, at : at + 128]
            out_ref[x, y, 144:288] = grad_in[:, at : at + 128]
            out_ref[x, y, 288:304] = high
            out_ref[x, y, 304:320] = low


def run_experts(which, rows, up, down):
    return pl.pallas_call(
        experts,
        out_shape=shape((4, 4, PACK, 128), BF16),
        grid_spec=pltpu.PrefetchScalarGridSpec(
            num_scalar_prefetch=1,
            grid=(1,),
            in_specs=[
                pl.BlockSpec((4, 4, PACK, 128), lambda i, j: (0, 0, 0, 0)),
                pl.BlockSpec((1, WIDTH, HID), lambda i, j: (j[0], 0, 0)),
                pl.BlockSpec((1, HID, WIDTH), lambda i, j: (j[0], 0, 0)),
            ],
            out_specs=pl.BlockSpec((4, 4, PACK, 128), lambda i, j: (0, 0, 0, 0)),
        ),
        name="experts",
        compiler_params=pltpu.CompilerParams(vmem_limit_bytes=48 * 1024 * 1024),
    )(which, rows, up, down)


def add_pair(a_ref, b_ref, out_ref):
    for x in range(4):
        for y in range(4):
            value = a_ref[x, y].astype(F32) + b_ref[x, y].astype(F32)
            out_ref[x, y, 0:288] = value[0:288].astype(BF16)
            high, low = split_two(value[288:304] + value[304:320])
            out_ref[x, y, 288:304] = high
            out_ref[x, y, 304:320] = low


def add_four(in_ref, out_ref):
    to = iota((ROWS, PACK), 0)
    come = iota((ROWS, PACK), 1)
    group = div(to, MSG)
    local = to - group * MSG
    pick = (local < CAP) & (come == group * CAP + local)
    pick |= (local >= CAP) & (local < 2 * CAP) & (come == SLOTS + group * CAP + local - CAP)
    pick |= (local == 18) & (come == 288 + group)
    pick |= (local == 19) & (come == 304 + group)
    pick = jnp.where(pick, 1.0, 0.0).astype(BF16)
    for y in range(4):
        value = in_ref[0, y].astype(F32)
        for x in range(1, 4):
            value = value + in_ref[x, y].astype(F32)
        high, low = split_two(value[288:304] + value[304:320])
        rows = jnp.concatenate([value[0:288].astype(BF16), high, low], axis=0)
        message = dot_nn(pick, rows).astype(BF16)
        for e in range(BLOCKS):
            out_ref[e, y] = message[e * MSG : (e + 1) * MSG]


def combine(in_ref, place_ref, gate_ref, out_ref):
    value = in_ref[:, 0].astype(F32)
    for y in range(1, 4):
        value = value + in_ref[:, y].astype(F32)
    stats = value[:, 18:19] + value[:, 19:20]
    stats = jnp.broadcast_to(stats, (BLOCKS, MSG, 128)).reshape(ROWS, 128)
    value = value.reshape(ROWS, 128).astype(BF16)
    row = iota((ROWS, 128), 0)
    lane = iota((ROWS, 128), 1)
    local = row - div(row, MSG) * MSG
    forward = local < CAP
    place = place_ref[...].astype(F32)
    ahead = jnp.where(forward, place, 0.0)
    behind = jnp.where(forward, 0.0, place).astype(BF16)
    gate = jnp.where(forward, gate_ref[...], 0.0)
    mixture = dot_tn(value.astype(F32), gate, precision=HIGHEST)
    grad = dot_tn(value, behind)
    out_ref[0, 0:64] = mixture[0:64]
    out_ref[1, 0:64] = mixture[64:128]
    out_ref[0, 64:128] = grad[0:64]
    out_ref[1, 64:128] = grad[64:128]
    for q in range(4):
        column = jnp.sum(jnp.where(lane == local + 16 * q, stats, 0.0), axis=1, keepdims=True)
        token = jnp.sum(ahead * column, axis=0, keepdims=True)
        out_ref[0, 128 + q : 129 + q] = token
        out_ref[1, 128 + q : 129 + q] = token
    out_ref[0, 132:136] = jnp.zeros((4, 128), F32)
    out_ref[1, 132:136] = jnp.zeros((4, 128), F32)


def finish(in_ref, own_ref, gain_ref, weight_ref, heads_ref, result_ref, grad_ref, gh_ref, gw_ref):
    got = in_ref[0] + in_ref[1]
    stream = own_ref[0:64]
    cot = own_ref[64:128]
    mixture = got[0:64]
    scaled = got[64:128] * gain_ref[...]
    first = got[128:129] / WIDTH
    second = got[129:130] / WIDTH
    center = got[130:131] * 0.5
    inv_scale = got[131:132] * 0.5
    normal = (stream - center) * inv_scale
    grad = (cot + inv_scale * (scaled - first - normal * second)).astype(BF16)
    result = (stream + mixture).astype(BF16)
    turn = eye(128)
    result_ref[...] = dot_nt(turn, result).astype(BF16)
    grad_ref[...] = dot_nt(turn, grad).astype(BF16)
    heads_grad = dot_nn(weight_ref[...], grad).astype(BF16)
    for chip in range(16):
        for core in range(2):
            at = (chip * 2 + core) * 64
            gh_ref[core, chip] = heads_grad[at : at + 64]
            heads = jnp.concatenate([heads_ref[0, chip], heads_ref[1, chip]], axis=0)
        gw_ref[chip] = dot_nt(grad, heads).astype(BF16)


def a2a(value, axes):
    return lax.all_to_all(value, axes, split_axis=0, concat_axis=0, tiled=True)


def total(value):
    return jnp.sum(value.astype(F32), axis=0)


def local(
    residual, heads_out, out_weight, norm_gain, up_weight, down_weight, routes, gates, cotangent
):
    core = lax.axis_index("c").astype(jnp.int32).reshape(1)
    swap = [(0, 1), (1, 0)]
    heads_t, place, gate = call(
        prepare,
        (shape((16, 64, 128), BF16), shape((ROWS, 128), BF16), shape((ROWS, 128), F32)),
        "prepare",
        1,
        3,
    )(core, heads_out, routes.T, gates.T)
    heads_t = a2a(heads_t, ("yl", "x"))
    heads_t = lax.all_gather(heads_t, "c", axis=0)
    gain_row = jnp.concatenate([norm_gain, norm_gain]).reshape(1, 128)
    own = call(project, shape((136, 128), F32), "project", 1, 5)(
        core, heads_t, out_weight, residual, cotangent, gain_row
    )
    both = lax.all_gather(own, "c", axis=0)
    message = call(dispatch, shape((BLOCKS, 4, MSG, 128), BF16), "dispatch", 0, 3)(
        both, place, gate
    )
    message = a2a(message.reshape(64, MSG, 128), ("yh", "z", "yl"))
    packed = call(repack, shape((4, 4, PACK, 128), BF16), "repack", 0, 1)(
        message.reshape(BLOCKS, 4, MSG, 128)
    )
    mine = a2a(packed, "x")
    other = lax.ppermute(mine, "c", swap)
    other_part = run_experts(1 - core, other, up_weight, down_weight)
    mine_part = run_experts(core, mine, up_weight, down_weight)
    came = lax.ppermute(other_part, "c", swap)
    part = call(add_pair, shape((4, 4, PACK, 128), BF16), "add_pair", 0, 2)(mine_part, came)
    part = a2a(part, "x")
    message = call(add_four, shape((BLOCKS, 4, MSG, 128), BF16), "add_four", 0, 1)(part)
    message = a2a(message.reshape(64, MSG, 128), ("yh", "z", "yl"))
    halves = call(combine, shape((2, 136, 128), F32), "combine", 0, 3)(
        message.reshape(BLOCKS, 4, MSG, 128), place, gate
    )
    halves = a2a(halves, "c")
    result, grad_residual, grad_heads, grad_weight = call(
        finish,
        (
            shape((128, 64), BF16),
            shape((128, 64), BF16),
            shape((2, 16, 64, 128), BF16),
            shape((16, 64, 128), BF16),
        ),
        "finish",
        0,
        5,
    )(halves, own, norm_gain.reshape(64, 1), out_weight, heads_t)
    grad_weight = total(a2a(grad_weight, EXPERT)).astype(BF16)
    grad_weight = a2a(jnp.broadcast_to(grad_weight, (16, 64, 128)), EXPERT)
    grad_weight = grad_weight.transpose(0, 2, 1).reshape(WIDTH, 64)
    grad_heads = total(a2a(grad_heads, "c")).astype(BF16)
    grad_heads = total(a2a(grad_heads, ("yl", "x"))).astype(BF16).T
    return (result, grad_residual, grad_heads, grad_weight)


def solution(mesh):
    view = Mesh(mesh.devices.reshape(SPLIT), AXES)
    return jax.shard_map(
        local,
        mesh=view,
        in_specs=(
            P(EXPERT, TENSOR),
            P(EXPERT, TENSOR),
            P(None, TENSOR),
            P(TENSOR),
            P(EXPERT, None, TENSOR),
            P(EXPERT, TENSOR, None),
            P(EXPERT, None),
            P(EXPERT, None),
            P(EXPERT, TENSOR),
        ),
        out_specs=(
            P(EXPERT, TENSOR),
            P(EXPERT, TENSOR),
            P(EXPERT, TENSOR),
            P(None, TENSOR),
        ),
        check_vma=False,
    )
```

time: 788 us -> 201 us (0.26)
  the two profiles are of different devices: /device:TPU:63 before, /device:TPU:16 now
where the time goes in v1:
time: 201 us; the launch traced here: 200 us
  blocking collectives  84.3 us (42%)
  waiting for transfers between devices  60.2 us (30%)
  starting transfers between devices  33.8 us (17%)
  Pallas kernels  12.8 us (6%)
  local copies, waits for them, and re-layouts  6.64 us (3%)
    all_to_all x5, blocking collectives, a2a(): return lax.all_to_all(value, axes, split_axis=0, concat_axis=0, tiled=True)  80.3 us
    all_to_all x5, waiting for transfers between devices, a2a(): return lax.all_to_all(value, axes, split_axis=0, concat_axis=0, tiled=True)  57.2 us
    all_to_all x5, starting transfers between devices, a2a(): return lax.all_to_all(value, axes, split_axis=0, concat_axis=0, tiled=True)  29.8 us
    pallas_call x2, Pallas kernels, run_experts(): pl.pallas_call(experts, out_shape=shape((4, 4, PACK, 128), BF16), grid_sp...  6.56 us
    unnamed x18, local copies, waits for them, and re-layouts  5.06 us
  transfers between devices with their start and end apart: 7, of which 6 were waited for; matrix products, arithmetic and copies ran while one was open for 2% of the time, Pallas kernels for 2%

profile of v1, /device:TPU:16, one launch (start us, length us, event | category | flops | bytes accessed | tf_op | source)
XLA Modules:
  0.0 200.2 jit_solution(1910889540743992419)
XLA Ops:
  0.6 0.0 copy-start.3
  0.6 0.0 copy-start.4
  0.7 0.0 copy-start.5
  0.7 0.8 copy.38.heads_ref
  1.5 0.0 copy-start.1
  1.5 0.7 copy-done.1
  2.2 0.0 copy-start.2
  2.2 0.7 copy-done.2
  2.9 0.9 prepare.1
  3.8 9.1 %all-to-all-start = ((bf16[16,64,128]{2,1,0:T(8,128)(2,1)}), bf16[16,64,128]{2,1,0:T(8,128)(2,1)S(1)}, u32[]{:S(2)}, u32[]{:S(2)}) async-start(bf16[16,64,128]{2,1,0:T(8,128)(2,1)} %get-tuple-element.11), calls=%async_computation | async-start | bytes 524288 | tf_op jit(solution)/shard_map/all_to_all | solution.py:337
  12.8 1.2 copy.39.weight_ref
  14.1 0.0 copy-done.3
  14.1 0.1 copy.40.residual_ref
  14.2 0.0 copy-done.4
  14.2 0.1 copy.41.cotangent_ref
  14.3 0.0 copy-done.5
  14.3 0.1 maximum_bitcast_fusion.gain_ref
  14.4 6.1 %all-to-all-done = bf16[16,64,128]{2,1,0:T(8,128)(2,1)S(1)} async-done(((bf16[16,64,128]{2,1,0:T(8,128)(2,1)}), bf16[16,64,128]{2,1,0:T(8,128)(2,1)S(1)}, u32[]{:S(2)}, u32[]{:S(2)}) %all-to-all-start) | async-done | bytes 262176 | tf_op jit(solution)/shard_map/all_to_all | solution.py:337
  20.5 2.2 %all-gather = bf16[32,64,128]{2,1,0:T(8,128)(2,1)S(1)} all-gather(bf16[16,64,128]{2,1,0:T(8,128)(2,1)S(1)} %all-to-all-done), channel_id=2, replica_groups=mesh['yh'=2,'z'=8,'yl'=4,'x'=4,'c'=2] {'c'}, dimensions={0}, use_global_device_ids=true | all-gather | bytes 786432 | tf_op jit(solution)/shard_map/all_gather | solution.py:357
  22.6 0.3 project.1.own_ref
  23.0 1.9 all-gather.1
  24.9 0.4 dispatch.1
  25.3 32.0 %all_to_all.50 = bf16[64,24,128]{2,1,0:T(8,128)(2,1)S(1)} all-to-all(bf16[64,24,128]{2,1,0:T(8,128)(2,1)S(1)} %bitcast.22), channel_id=1, replica_groups=mesh['yh'=2,'z'=8,'yl'=4,'x'=4,'c'=2] {'yh','z','yl'}, dimensions={0} | all-to-all | bytes 786432 | tf_op jit(solution)/shard_map/all_to_all | solution.py:337
  57.3 0.8 repack.1
  58.1 0.0 copy-start
  58.1 19.2 %all_to_all.51.in_ref = bf16[4,4,320,128]{3,2,1,0:T(8,128)(2,1)S(1)} all-to-all(bf16[4,4,320,128]{3,2,1,0:T(8,128)(2,1)S(1)} %repack.1), channel_id=1, replica_groups=mesh['yh'=2,'z'=8,'yl'=4,'x'=4,'c'=2] {'x'}, dimensions={0} | all-to-all | bytes 2621440 | tf_op jit(solution)/shard_map/all_to_all | solution.py:337
  77.3 1.9 collective-permute-start
  79.2 3.0 %collective-permute-done.in_ref = bf16[4,4,320,128]{3,2,1,0:T(8,128)(2,1)S(1)} collective-permute-done((bf16[4,4,320,128]{3,2,1,0:T(8,128)(2,1)S(1)}, bf16[4,4,320,128]{3,2,1,0:T(8,128)(2,1)S(1)}, u32[]{:S(2)}, u32[]{:S(2)}) %collective-permute-start) | collective-permute-done | bytes 1310752 | tf_op jit(solution)/shard_map/ppermute | solution.py:371
  82.2 0.0 copy-done
  82.2 3.3 %experts.3 = bf16[4,4,320,128]{3,2,1,0:T(8,128)(2,1)S(1)} custom-call(s32[1]{0:T(128)S(6)} %sub.3.which_ref, bf16[4,4,320,128]{3,2,1,0:T(8,128)(2,1)S(1)} %collective-permute-done.in_ref, bf16[2,2048,256]{2,1,0:T(8,128)(2,1)S(1)} %copy-done, bf16[2,256,2048]{2,1,0:T(8,128)(2,1)} %down_ref.3), custom_call_target="tpu_custom_call" | custom-call | tf_op jit(solution)/shard_map/experts/pallas_call | solution.py:232
  85.5 2.0 %collective-permute-start.1 = (bf16[4,4,320,128]{3,2,1,0:T(8,128)(2,1)S(1)}, bf16[4,4,320,128]{3,2,1,0:T(8,128)(2,1)S(1)}, u32[]{:S(2)}, u32[]{:S(2)}) collective-permute-start(bf16[4,4,320,128]{3,2,1,0:T(8,128)(2,1)S(1)} %experts.3), channel_id=1, source_target_pairs={{0,1},{1,0},{2,3},{3,2},{4,5},{5,4},{6,7},{7,6},{8,9},{9,8},{10,11... | collective-permute-start | bytes 3932168 | tf_op jit(solution)/shard_map/ppermute | solution.py:374
  87.5 3.3 %experts.2.a_ref = bf16[4,4,320,128]{3,2,1,0:T(8,128)(2,1)S(1)} custom-call(s32[1]{0:T(128)} %bitcast.core_ref.which_ref, bf16[4,4,320,128]{3,2,1,0:T(8,128)(2,1)S(1)} %all_to_all.51.in_ref, bf16[2,2048,256]{2,1,0:T(8,128)(2,1)S(1)} %copy-done, bf16[2,256,2048]{2,1,0:T(8,128)(2,1)} %down_ref.3), custom_call_target="tpu_custom_call" | custom-call | tf_op jit(solution)/shard_map/experts/pallas_call | solution.py:232
  90.9 0.0 collective-permute-done.1.b_ref
  90.9 0.3 add_pair.1
  91.2 21.1 %all_to_all.52.in_ref = bf16[4,4,320,128]{3,2,1,0:T(8,128)(2,1)S(1)} all-to-all(bf16[4,4,320,128]{3,2,1,0:T(8,128)(2,1)S(1)} %add_pair.1), channel_id=1, replica_groups=mesh['yh'=2,'z'=8,'yl'=4,'x'=4,'c'=2] {'x'}, dimensions={0} | all-to-all | bytes 2621440 | tf_op jit(solution)/shard_map/all_to_all | solution.py:337
  112.3 1.7 add_four.1
  114.0 6.5 %all-to-all-start.4 = ((bf16[64,24,128]{2,1,0:T(8,128)(2,1)}), bf16[64,24,128]{2,1,0:T(8,128)(2,1)S(1)}, u32[]{:S(2)}, u32[]{:S(2)}) async-start(bf16[64,24,128]{2,1,0:T(8,128)(2,1)} %bitcast.8), calls=%async_computation.4 | async-start | bytes 786432 | tf_op jit(solution)/shard_map/all_to_all | solution.py:337
  120.5 0.1 copy.42.gain_ref
  120.6 15.9 %all-to-all-done.4 = bf16[64,24,128]{2,1,0:T(8,128)(2,1)S(1)} async-done(((bf16[64,24,128]{2,1,0:T(8,128)(2,1)}), bf16[64,24,128]{2,1,0:T(8,128)(2,1)S(1)}, u32[]{:S(2)}, u32[]{:S(2)}) %all-to-all-start.4) | async-done | bytes 393248 | tf_op jit(solution)/shard_map/all_to_all | solution.py:337
  136.5 0.5 combine.1
  137.0 3.8 %all_to_all.53.in_ref = f32[2,136,128]{2,1,0:T(8,128)S(1)} all-to-all(f32[2,136,128]{2,1,0:T(8,128)S(1)} %combine.1), channel_id=1, replica_groups=mesh['yh'=2,'z'=8,'yl'=4,'x'=4,'c'=2] {'c'}, dimensions={0} | all-to-all | bytes 278528 | tf_op jit(solution)/shard_map/all_to_all | solution.py:337
  140.8 1.3 finish.1
  142.1 4.1 %all_to_all.54 = bf16[2,16,64,128]{3,2,1,0:T(8,128)(2,1)S(1)} all-to-all(bf16[2,16,64,128]{3,2,1,0:T(8,128)(2,1)S(1)} %get-tuple-element.16), channel_id=1, replica_groups=mesh['yh'=2,'z'=8,'yl'=4,'x'=4,'c'=2] {'c'}, dimensions={0} | all-to-all | bytes 1048576 | tf_op jit(solution)/shard_map/all_to_all | solution.py:337
  146.3 4.0 %all-to-all-start.8 = ((bf16[16,64,128]{2,1,0:T(8,128)(2,1)}), bf16[16,64,128]{2,1,0:T(8,128)(2,1)S(1)}, u32[]{:S(2)}, u32[]{:S(2)}) async-start(bf16[16,64,128]{2,1,0:T(8,128)(2,1)} %get-tuple-element.17), calls=%async_computation.8 | async-start | bytes 524288 | tf_op jit(solution)/shard_map/all_to_all | solution.py:337
  150.3 0.8 reduce_sum.36
  151.2 14.8 %all-to-all-done.8 = bf16[16,64,128]{2,1,0:T(8,128)(2,1)S(1)} async-done(((bf16[16,64,128]{2,1,0:T(8,128)(2,1)}), bf16[16,64,128]{2,1,0:T(8,128)(2,1)S(1)}, u32[]{:S(2)}, u32[]{:S(2)}) %all-to-all-start.8) | async-done | bytes 262176 | tf_op jit(solution)/shard_map/all_to_all | solution.py:337
  165.9 4.8 %all-to-all-start.7 = ((bf16[16,64,128]{2,1,0:T(8,128)(2,1)}), bf16[16,64,128]{2,1,0:T(8,128)(2,1)S(1)}, u32[]{:S(2)}, u32[]{:S(2)}) async-start(bf16[16,64,128]{2,1,0:T(8,128)(2,1)} %reduce_sum.36), calls=%async_computation.7 | async-start | bytes 524288 | tf_op jit(solution)/shard_map/all_to_all | solution.py:337
  170.8 7.7 %all-to-all-done.7 = bf16[16,64,128]{2,1,0:T(8,128)(2,1)S(1)} async-done(((bf16[16,64,128]{2,1,0:T(8,128)(2,1)}), bf16[16,64,128]{2,1,0:T(8,128)(2,1)S(1)}, u32[]{:S(2)}, u32[]{:S(2)}) %all-to-all-start.7) | async-done | bytes 262176 | tf_op jit(solution)/shard_map/all_to_all | solution.py:337
  178.5 0.8 broadcast_in_dim.3
  179.2 5.4 %all-to-all-start.9 = ((bf16[16,64,128]{2,1,0:T(8,128)(2,1)}), bf16[16,64,128]{2,1,0:T(8,128)(2,1)S(1)}, u32[]{:S(2)}, u32[]{:S(2)}) async-start(bf16[16,64,128]{2,1,0:T(8,128)(2,1)} %broadcast_in_dim.3), calls=%async_computation.9 | async-start | bytes 524288 | tf_op jit(solution)/shard_map/all_to_all | solution.py:337
  184.7 0.7 copy.45
  185.4 0.7 copy.46
  186.1 0.6 reduce_sum.37
  186.7 12.7 %all-to-all-done.9 = bf16[16,64,128]{2,1,0:T(8,128)(2,1)S(1)} async-done(((bf16[16,64,128]{2,1,0:T(8,128)(2,1)}), bf16[16,64,128]{2,1,0:T(8,128)(2,1)S(1)}, u32[]{:S(2)}, u32[]{:S(2)}) %all-to-all-start.9) | async-done | bytes 262176 | tf_op jit(solution)/shard_map/all_to_all | solution.py:337
  199.5 0.7 copy_bitcast_fusion
  (1 shorter events, 0.0 us)
Async XLA Ops:
  0.6 13.4 %copy-start.3 = (bf16[128,64]{0,1:T(8,128)(2,1)S(1)}, bf16[128,64]{0,1:T(8,128)(2,1)}, u32[]{:S(2)}) copy-start(bf16[128,64]{0,1:T(8,128)(2,1)} %param.9) | copy-start | bytes 49156
  0.6 13.6 %copy-start.4 = (bf16[128,64]{0,1:T(8,128)(2,1)S(1)}, bf16[128,64]{0,1:T(8,128)(2,1)}, u32[]{:S(2)}) copy-start(bf16[128,64]{0,1:T(8,128)(2,1)} %param.17) | copy-start | bytes 49156
  0.7 13.7 %copy-start.5 = (f32[64]{0:T(128)S(1)}, f32[64]{0:T(128)}, u32[]{:S(2)}) copy-start(f32[64]{0:T(128)} %param.12) | copy-start | bytes 772
  1.5 0.7 copy-start.1
  2.2 0.7 copy-start.2
  3.8 16.7 %all-to-all-start = ((bf16[16,64,128]{2,1,0:T(8,128)(2,1)}), bf16[16,64,128]{2,1,0:T(8,128)(2,1)S(1)}, u32[]{:S(2)}, u32[]{:S(2)}) async-start(bf16[16,64,128]{2,1,0:T(8,128)(2,1)} %get-tuple-element.11), calls=%async_computation | async-start | bytes 524288 | tf_op jit(solution)/shard_map/all_to_all | solution.py:337
  58.1 24.1 %copy-start = (bf16[2,2048,256]{2,1,0:T(8,128)(2,1)S(1)}, bf16[2,2048,256]{2,1,0:T(8,128)(2,1)}, u32[]{:S(2)}) copy-start(bf16[2,2048,256]{2,1,0:T(8,128)(2,1)} %up_ref.3) | copy-start | bytes 6291460
  77.3 4.9 %collective-permute-start = (bf16[4,4,320,128]{3,2,1,0:T(8,128)(2,1)S(1)}, bf16[4,4,320,128]{3,2,1,0:T(8,128)(2,1)S(1)}, u32[]{:S(2)}, u32[]{:S(2)}) collective-permute-start(bf16[4,4,320,128]{3,2,1,0:T(8,128)(2,1)S(1)} %all_to_all.51.in_ref), channel_id=1, source_target_pairs={{0,1},{1,0},{2,3},{3,2},{4,5},{5,4},{6,7},{7,6},{8,9},{9,8},{10,11... | collective-permute-start | bytes 3932168 | tf_op jit(solution)/shard_map/ppermute | solution.py:371
  85.5 5.4 %collective-permute-start.1 = (bf16[4,4,320,128]{3,2,1,0:T(8,128)(2,1)S(1)}, bf16[4,4,320,128]{3,2,1,0:T(8,128)(2,1)S(1)}, u32[]{:S(2)}, u32[]{:S(2)}) collective-permute-start(bf16[4,4,320,128]{3,2,1,0:T(8,128)(2,1)S(1)} %experts.3), channel_id=1, source_target_pairs={{0,1},{1,0},{2,3},{3,2},{4,5},{5,4},{6,7},{7,6},{8,9},{9,8},{10,11... | collective-permute-start | bytes 3932168 | tf_op jit(solution)/shard_map/ppermute | solution.py:374
  114.0 22.5 %all-to-all-start.4 = ((bf16[64,24,128]{2,1,0:T(8,128)(2,1)}), bf16[64,24,128]{2,1,0:T(8,128)(2,1)S(1)}, u32[]{:S(2)}, u32[]{:S(2)}) async-start(bf16[64,24,128]{2,1,0:T(8,128)(2,1)} %bitcast.8), calls=%async_computation.4 | async-start | bytes 786432 | tf_op jit(solution)/shard_map/all_to_all | solution.py:337
  146.3 19.6 %all-to-all-start.8 = ((bf16[16,64,128]{2,1,0:T(8,128)(2,1)}), bf16[16,64,128]{2,1,0:T(8,128)(2,1)S(1)}, u32[]{:S(2)}, u32[]{:S(2)}) async-start(bf16[16,64,128]{2,1,0:T(8,128)(2,1)} %get-tuple-element.17), calls=%async_computation.8 | async-start | bytes 524288 | tf_op jit(solution)/shard_map/all_to_all | solution.py:337
  165.9 12.5 %all-to-all-start.7 = ((bf16[16,64,128]{2,1,0:T(8,128)(2,1)}), bf16[16,64,128]{2,1,0:T(8,128)(2,1)S(1)}, u32[]{:S(2)}, u32[]{:S(2)}) async-start(bf16[16,64,128]{2,1,0:T(8,128)(2,1)} %reduce_sum.36), calls=%async_computation.7 | async-start | bytes 524288 | tf_op jit(solution)/shard_map/all_to_all | solution.py:337
  179.2 20.2 %all-to-all-start.9 = ((bf16[16,64,128]{2,1,0:T(8,128)(2,1)}), bf16[16,64,128]{2,1,0:T(8,128)(2,1)S(1)}, u32[]{:S(2)}, u32[]{:S(2)}) async-start(bf16[16,64,128]{2,1,0:T(8,128)(2,1)} %broadcast_in_dim.3), calls=%async_computation.9 | async-start | bytes 524288 | tf_op jit(solution)/shard_map/all_to_all | solution.py:337

commit v2 on v1

v2 whole, which is shorter than its diff:
```python
import jax
import jax.numpy as jnp
from jax import lax
from jax.experimental import pallas as pl
from jax.experimental.pallas import tpu as pltpu
from jax.sharding import Mesh, PartitionSpec as P

AXES = ("yh", "z", "yl", "x", "c")
EXPERT = ("yh", "z")
TENSOR = ("yl", "x", "c")
SPLIT = (2, 8, 4, 4, 2)
BLOCKS = 16
CAP = 9
MSG = 24
PACK = 304
SLOTS = BLOCKS * CAP
SIDE = 2432
ROWS = BLOCKS * MSG
WIDTH = 2048
HID = 256
F32 = jnp.float32
BF16 = jnp.bfloat16
HIGHEST = lax.Precision.HIGHEST
ROOT = 0.7978845608028654
CUBIC = 0.044715


def iota(shape, axis):
    return lax.broadcasted_iota(jnp.int32, shape, axis)


def div(value, by):
    scale = -(-(1 << 14) // by)
    return lax.shift_right_logical(value * scale, 14)


def dot_nn(a, b, **kw):
    return lax.dot_general(a, b, (((1,), (0,)), ((), ())), preferred_element_type=F32, **kw)


def dot_nt(a, b, **kw):
    return lax.dot_general(a, b, (((1,), (1,)), ((), ())), preferred_element_type=F32, **kw)


def dot_tn(a, b, **kw):
    return lax.dot_general(a, b, (((0,), (0,)), ((), ())), preferred_element_type=F32, **kw)


def eye(n):
    return (iota((n, n), 0) == iota((n, n), 1)).astype(F32).astype(BF16)


def call(kernel, outs, name, n_smem, n_in):
    return pl.pallas_call(
        kernel,
        out_shape=outs,
        in_specs=[pl.BlockSpec(memory_space=pltpu.SMEM)] * n_smem
        + [pl.BlockSpec(memory_space=pltpu.VMEM)] * n_in,
        name=name,
        compiler_params=pltpu.CompilerParams(vmem_limit_bytes=48 * 1024 * 1024),
    )


def shape(dims, dtype):
    return jax.ShapeDtypeStruct(dims, dtype)


def split_three(value):
    high = value.astype(BF16)
    rest = value - high.astype(F32)
    middle = rest.astype(BF16)
    return high, middle, (rest - middle.astype(F32)).astype(BF16)


def split_two(value):
    high = value.astype(BF16)
    low = (value - high.astype(F32)).astype(BF16)
    return high, low


def join(block):
    return block + jnp.concatenate([block[:, 64:], block[:, :64]], axis=1)


def part(value):
    high, low = split_two(value)
    lane = iota(value.shape, 1)
    return jnp.where(lane < 64, high.astype(F32), low.astype(F32)).astype(BF16)


def pack(weight_ref, residual_ref, cotangent_ref, gain_ref, out_ref):
    out_ref[:, 0:2048] = weight_ref[...]
    out_ref[:, 2048:2176] = residual_ref[...]
    out_ref[:, 2176:2304] = cotangent_ref[...]
    high, middle, low = split_three(jnp.broadcast_to(gain_ref[...], (64, 128)))
    lane = iota((64, 128), 1)
    value = jnp.where(lane == 0, high.astype(F32), middle.astype(F32))
    out_ref[:, 2304:2432] = jnp.where(lane == 2, low.astype(F32), value).astype(BF16)


def prepare(core_ref, routes_ref, gates_ref, place_ref, gate_ref):
    core = core_ref[0]
    row = iota((ROWS, 128), 0)
    group = div(row, MSG)
    local = row - group * MSG
    slot = jnp.where(local < CAP, local, local - CAP)
    used = local < 2 * CAP
    expert = 2 * group + core
    first = (routes_ref[0:1, :] == expert) & used
    second = (routes_ref[1:2, :] == expert) & used
    named = jnp.where(first | second, 1.0, 0.0)
    before = (iota((128, 128), 0) < iota((128, 128), 1)).astype(F32).astype(BF16)
    earlier = dot_nn(named.astype(BF16), before)
    taken = (earlier == slot.astype(F32)) & (named > 0.5)
    place_ref[...] = jnp.where(taken, 1.0, 0.0).astype(BF16)
    gate = jnp.where(first, gates_ref[0:1, :], gates_ref[1:2, :])
    gate_ref[...] = jnp.where(taken, gate, 0.0)


def turn_weight(core_ref, side_ref, out_ref):
    mirror = eye(128)
    for chip in range(16):
        turned = dot_nt(mirror, side_ref[:, chip * 128 : chip * 128 + 128])
        out_ref[chip] = jnp.where(core_ref[0] == 0, turned[0:64], turned[64:128]).astype(BF16)


def dispatch(block_ref, heads_ref, side_ref, place_ref, gate_ref, stream_ref, out_ref):
    pieces = []
    for chip in range(16):
        pieces.append(heads_ref[0, chip])
        pieces.append(heads_ref[1, chip])
    mixed = dot_nn(side_ref[:, 0:2048], jnp.concatenate(pieces, axis=0))
    stream = side_ref[:, 2048:2176].astype(F32) + mixed
    stream_ref[...] = stream
    shift = jnp.mean(stream, axis=0, keepdims=True)
    centered = (stream - shift).astype(BF16)
    place = place_ref[...]
    placed = place.astype(F32)
    rows_x = dot_nt(place, centered)
    rows_c = dot_nt(place, side_ref[:, 2176:2304])
    gate_col = jnp.sum(gate_ref[...], axis=1, keepdims=True)
    shift_col = jnp.sum(placed * shift, axis=1, keepdims=True)
    row = iota((ROWS, 128), 0)
    lane = iota((ROWS, 128), 1)
    local = row - div(row, MSG) * MSG
    high, low = split_two(shift_col)
    spread = jnp.where(lane == local, high.astype(F32), 0.0)
    spread = spread + jnp.where(lane == local + 16, low.astype(F32), 0.0)
    spread = jnp.where(local < CAP, spread, 0.0).astype(BF16)
    to = iota((ROWS, ROWS), 0)
    come = iota((ROWS, ROWS), 1)
    to_group = div(to, MSG)
    gather = (to - to_group * MSG == 18) & (to_group == div(come, MSG))
    stats = dot_nn(jnp.where(gather, 1.0, 0.0).astype(BF16), spread)
    feature = iota((128, 128), 0)
    at = iota((128, 128), 1) - 32
    which = lax.shift_right_logical(jnp.maximum(at, 0), 3)
    mine = (at >= 0) & (at < 24) & (feature == 8 * block_ref[0] + (at & 7))
    gains = side_ref[:, 2304:2432].astype(F32)
    gain = jnp.where(which == 0, gains[:, 0:1], jnp.where(which == 1, gains[:, 1:2], gains[:, 2:3]))
    gain = jnp.sum(jnp.where(mine, gain, 0.0), axis=0, keepdims=True)
    value = jnp.where(local < CAP, rows_x, jnp.where(local < 2 * CAP, rows_c * gate_col, stats))
    value = jnp.where(local == 18, value + gain, value).astype(BF16)
    for e in range(BLOCKS):
        piece = value[e * MSG : (e + 1) * MSG]
        for y in range(4):
            out_ref[e, y] = piece


def selection(to, come):
    group = div(come, MSG)
    local = come - group * MSG
    pick = (local < CAP) & (to == group * CAP + local)
    pick |= (local >= CAP) & (local < 2 * CAP) & (to == SLOTS + group * CAP + local - CAP)
    pick |= (local == 18) & (to == 2 * SLOTS + group)
    return jnp.where(pick, 1.0, 0.0).astype(BF16)


def repack(in_ref, out_ref):
    pick = selection(iota((PACK, ROWS), 0), iota((PACK, ROWS), 1))
    for y in range(4):
        rows = in_ref[:, y].astype(F32).reshape(ROWS, 128).astype(BF16)
        packed = dot_nn(pick, rows).astype(BF16)
        for x in range(4):
            out_ref[x, y] = packed


def slot_tables():
    slot = iota((SLOTS, 128), 0)
    return slot - div(slot, CAP) * CAP, iota((SLOTS, 128), 1)


def read_rows(in_ref):
    local, lane = slot_tables()
    expand = (div(iota((SLOTS, 16), 0), CAP) == iota((SLOTS, 16), 1)).astype(F32).astype(BF16)
    shift_lane = (lane == local) | (lane == local + 16)
    at = iota((128, 128), 0) - 32
    collect = (at >= 0) & (at < 24) & ((at & 7) == (iota((128, 128), 1) & 7))
    collect = jnp.where(collect, 1.0, 0.0).astype(BF16)
    own = lax.shift_right_logical(iota((16, 128), 1), 3) == iota((16, 128), 0)
    chunks = [None] * 16
    gains = [None] * 16
    total = jnp.zeros((SLOTS, 128), F32)
    for x in range(4):
        for y in range(4):
            block = in_ref[x, y, 288:304]
            shift = dot_nn(expand, block)
            shift = jnp.sum(jnp.where(shift_lane, shift, 0.0), axis=1, keepdims=True)
            chunk = in_ref[x, y, 0:144].astype(F32) + shift
            total = total + chunk
            chunks[y * 4 + x] = chunk
            gain = jnp.where(own, dot_nn(block, collect), 0.0)
            gains[y * 4 + x] = jnp.sum(gain, axis=0, keepdims=True)
    center = jnp.sum(total, axis=1, keepdims=True) / WIDTH
    squares = jnp.zeros((SLOTS, 128), F32)
    for i in range(16):
        chunks[i] = chunks[i] - center
        squares = squares + chunks[i] * chunks[i]
    inv_scale = lax.rsqrt(jnp.sum(squares, axis=1, keepdims=True) / WIDTH + 1e-05)
    rows = []
    for i in range(16):
        rows.append((chunks[i] * inv_scale * gains[i]).astype(BF16))
    return jnp.concatenate(rows, axis=1), jnp.concatenate(gains, axis=1), center, inv_scale


def ahead(in_ref, up, down):
    rows, gain, center, inv_scale = read_rows(in_ref)
    high, middle, low = split_three(jnp.broadcast_to(gain, (16, WIDTH)))
    row = iota((16, WIDTH), 0)
    gain = jnp.where(row == 0, high.astype(F32), middle.astype(F32))
    gain = jnp.where(row == 2, low.astype(F32), gain).astype(BF16)
    product = dot_nn(jnp.concatenate([rows, gain], axis=0), up)
    pre = product[0:SLOTS]
    weigh = product[SLOTS : SLOTS + 1] + product[SLOTS + 1 : SLOTS + 2]
    weigh = weigh + product[SLOTS + 2 : SLOTS + 3]
    bend = jnp.tanh(ROOT * (pre + CUBIC * pre * pre * pre))
    hidden = (0.5 * pre * (1.0 + bend)).astype(BF16)
    return pre, weigh, center, inv_scale, dot_nn(hidden, down).astype(BF16)


def behind(in_ref, up, down, pre, weigh, center, inv_scale):
    cots = [None] * 16
    for x in range(4):
        for y in range(4):
            cots[y * 4 + x] = in_ref[x, y, 144:288]
    grad_hidden = dot_nt(jnp.concatenate(cots, axis=1), down)
    bend = jnp.tanh(ROOT * (pre + CUBIC * pre * pre * pre))
    slope = 0.5 * (1.0 + bend) + 0.5 * pre * (1.0 - bend * bend) * (
        ROOT * (1.0 + 3.0 * CUBIC * pre * pre)
    )
    grad_act = (grad_hidden * slope).astype(BF16)
    wide = grad_act.astype(F32)
    sum_first = jnp.sum(wide * weigh, axis=1, keepdims=True)
    sum_second = jnp.sum(wide * pre, axis=1, keepdims=True)
    local, lane = slot_tables()
    spread = jnp.where(lane == local, sum_first, 0.0)
    spread = spread + jnp.where(lane == local + 16, sum_second, 0.0)
    spread = spread + jnp.where(lane == local + 32, center * (1.0 / 32), 0.0)
    spread = spread + jnp.where(lane == local + 48, inv_scale * (1.0 / 32), 0.0)
    high, low = split_two(spread)
    collect = (iota((16, SLOTS), 0) == div(iota((16, SLOTS), 1), CAP)).astype(F32).astype(BF16)
    high = dot_nn(collect, high)
    low = dot_nn(collect, low)
    stats = high + jnp.concatenate([low[:, 64:], low[:, :64]], axis=1)
    return dot_nt(grad_act, up).astype(BF16), stats.astype(BF16)


def both_ways(which_ref, in_ref, up_ref, down_ref, out_ref):
    up, down = up_ref[which_ref[0]], down_ref[which_ref[0]]
    pre, weigh, center, inv_scale, value = ahead(in_ref, up, down)
    grad_in, stats = behind(in_ref, up, down, pre, weigh, center, inv_scale)
    for x in range(4):
        for y in range(4):
            at = (y * 4 + x) * 128
            out_ref[x, y, 0:144] = value[:, at : at + 128]
            out_ref[x, y, 144:288] = grad_in[:, at : at + 128]
            out_ref[x, y, 288:304] = stats


def only_ahead(which_ref, in_ref, up_ref, down_ref, out_ref, pre_ref, weigh_ref, scalar_ref):
    up, down = up_ref[which_ref[0]], down_ref[which_ref[0]]
    pre, weigh, center, inv_scale, value = ahead(in_ref, up, down)
    pre_ref[...] = pre
    weigh_ref[...] = jnp.broadcast_to(weigh, (8, HID))
    lane = iota((SLOTS, 128), 1)
    scalar_ref[...] = jnp.where(lane == 0, center, inv_scale)
    for x in range(4):
        for y in range(4):
            at = (y * 4 + x) * 128
            out_ref[x, y] = value[:, at : at + 128]


def only_behind(
    which_ref, in_ref, up_ref, down_ref, pre_ref, weigh_ref, scalar_ref, out_ref
):
    up, down = up_ref[which_ref[0]], down_ref[which_ref[0]]
    center, inv_scale = scalar_ref[:, 0:1], scalar_ref[:, 1:2]
    grad_in, stats = behind(
        in_ref, up, down, pre_ref[...], weigh_ref[0:1], center, inv_scale
    )
    for x in range(4):
        for y in range(4):
            at = (y * 4 + x) * 128
            out_ref[x, y, 0:144] = grad_in[:, at : at + 128]
            out_ref[x, y, 144:160] = stats


def add_pair(value_ref, grad_ref, came_ref, out_ref):
    for x in range(4):
        for y in range(4):
            came = came_ref[x, y].astype(F32)
            out_ref[x, y, 0:144] = (value_ref[x, y].astype(F32) + came[0:144]).astype(BF16)
            grad = grad_ref[x, y].astype(F32)
            out_ref[x, y, 144:288] = (grad[0:144] + came[144:288]).astype(BF16)
            out_ref[x, y, 288:304] = part(join(grad[144:160] + came[288:304]))


def add_four(in_ref, out_ref):
    pick = selection(iota((ROWS, PACK), 1), iota((ROWS, PACK), 0))
    for y in range(4):
        value = in_ref[0, y].astype(F32)
        for x in range(1, 4):
            value = value + in_ref[x, y].astype(F32)
        rows = jnp.concatenate([value[0:288].astype(BF16), part(join(value[288:304]))], axis=0)
        message = dot_nn(pick, rows).astype(BF16)
        for e in range(BLOCKS):
            out_ref[e, y] = message[e * MSG : (e + 1) * MSG]


def combine(in_ref, place_ref, gate_ref, out_ref):
    value = in_ref[:, 0].astype(F32)
    for y in range(1, 4):
        value = value + in_ref[:, y].astype(F32)
    stats = value[:, 18]
    stats = join(stats).reshape(BLOCKS, 1, 128)
    stats = jnp.broadcast_to(stats, (BLOCKS, MSG, 128)).reshape(ROWS, 128)
    value = value.reshape(ROWS, 128).astype(BF16)
    row = iota((ROWS, 128), 0)
    lane = iota((ROWS, 128), 1)
    local = row - div(row, MSG) * MSG
    forward = local < CAP
    place = place_ref[...].astype(F32)
    ahead_place = jnp.where(forward, place, 0.0)
    behind_place = jnp.where(forward, 0.0, place).astype(BF16)
    gate = jnp.where(forward, gate_ref[...], 0.0)
    out_ref[0:128] = dot_tn(value.astype(F32), gate, precision=HIGHEST)
    out_ref[128:256] = dot_tn(value, behind_place)
    for q in range(4):
        column = jnp.sum(jnp.where(lane == local + 16 * q, stats, 0.0), axis=1, keepdims=True)
        out_ref[256 + q : 257 + q] = jnp.sum(ahead_place * column, axis=0, keepdims=True)
    out_ref[260:264] = jnp.zeros((4, 128), F32)


def finish(
    core_ref, in_ref, stream_ref, side_ref, weight_ref, heads_ref, result_ref, grad_ref, gh_ref, gw_ref
):
    got = in_ref[0] + in_ref[1]
    stream = stream_ref[...]
    cot = side_ref[:, 2176:2304].astype(F32)
    gains = side_ref[:, 2304:2432].astype(F32)
    scaled = got[128:256] * (gains[:, 0:1] + gains[:, 1:2] + gains[:, 2:3])
    first = got[256:257] / WIDTH
    second = got[257:258] / WIDTH
    center = got[258:259] * 0.5
    inv_scale = got[259:260] * 0.5
    normal = (stream - center) * inv_scale
    grad = cot + inv_scale * (scaled - first - normal * second)
    result = stream + got[0:128]
    low = core_ref[0] == 0
    result_ref[...] = jnp.where(low, result[0:64], result[64:128]).astype(BF16)
    own = jnp.where(low, grad[0:64], grad[64:128]).astype(BF16)
    grad_ref[...] = own
    grad = grad.astype(BF16)
    for chip in range(16):
        gh_ref[chip] = dot_nn(weight_ref[chip], grad).astype(BF16)
        heads = jnp.concatenate([heads_ref[0, chip], heads_ref[1, chip]], axis=0)
        gw_ref[chip] = dot_nt(own, heads).astype(BF16)


def a2a(value, axes):
    return lax.all_to_all(value, axes, split_axis=0, concat_axis=0, tiled=True)


def total(value):
    return jnp.sum(value.astype(F32), axis=0)


def local(
    residual, heads_out, out_weight, norm_gain, up_weight, down_weight, routes, gates, cotangent
):
    core = lax.axis_index("c").astype(jnp.int32).reshape(1)
    block = lax.axis_index(EXPERT).astype(jnp.int32).reshape(1)
    swap = [(0, 1), (1, 0)]
    heads_t = a2a(jnp.broadcast_to(heads_out.T, (16, 64, 128)), ("yl", "x"))
    side = call(pack, shape((64, SIDE), BF16), "pack", 0, 4)(
        out_weight.T, residual.T, cotangent.T, norm_gain.reshape(64, 1)
    )
    side = lax.all_gather(side, "c", axis=0, tiled=True)
    place, gate = call(
        prepare, (shape((ROWS, 128), BF16), shape((ROWS, 128), F32)), "prepare", 1, 2
    )(core, routes.T, gates.T)
    turned = call(turn_weight, shape((16, 64, 128), BF16), "turn_weight", 1, 1)(core, side)
    heads_t = lax.all_gather(heads_t, "c", axis=0)
    stream, message = call(
        dispatch, (shape((128, 128), F32), shape((BLOCKS, 4, MSG, 128), BF16)), "dispatch", 1, 4
    )(block, heads_t, side, place, gate)
    message = a2a(message.reshape(64, MSG, 128), ("yh", "z", "yl"))
    packed = call(repack, shape((4, 4, PACK, 128), BF16), "repack", 0, 1)(
        message.reshape(BLOCKS, 4, MSG, 128)
    )
    mine = a2a(packed, "x")
    other = lax.ppermute(mine, "c", swap)
    value, pre, weigh, scalars = call(
        only_ahead,
        (
            shape((4, 4, SLOTS, 128), BF16),
            shape((SLOTS, HID), F32),
            shape((8, HID), F32),
            shape((SLOTS, 128), F32),
        ),
        "only_ahead",
        1,
        3,
    )(core, mine, up_weight, down_weight)
    sent = call(both_ways, shape((4, 4, PACK, 128), BF16), "both_ways", 1, 3)(
        1 - core, other, up_weight, down_weight
    )
    sent, pre = lax.optimization_barrier((sent, pre))
    came = lax.ppermute(sent, "c", swap)
    grad = call(only_behind, shape((4, 4, SLOTS + 16, 128), BF16), "only_behind", 1, 6)(
        core, mine, up_weight, down_weight, pre, weigh, scalars
    )
    summed = call(add_pair, shape((4, 4, PACK, 128), BF16), "add_pair", 0, 3)(value, grad, came)
    summed = a2a(summed, "x")
    message = call(add_four, shape((BLOCKS, 4, MSG, 128), BF16), "add_four", 0, 1)(summed)
    message = a2a(message.reshape(64, MSG, 128), ("yh", "z", "yl"))
    both = call(combine, shape((264, 128), F32), "combine", 0, 3)(
        message.reshape(BLOCKS, 4, MSG, 128), place, gate
    )
    both = lax.all_gather(both, "c", axis=0)
    result, grad_residual, grad_heads, grad_weight = call(
        finish,
        (
            shape((64, 128), BF16),
            shape((64, 128), BF16),
            shape((16, 64, 128), BF16),
            shape((16, 64, 128), BF16),
        ),
        "finish",
        1,
        5,
    )(core, both, stream, side, turned, heads_t)
    grad_weight = total(a2a(grad_weight.reshape(8, 2, 64, 128), "z"))
    grad_weight, grad_heads = lax.optimization_barrier((grad_weight, grad_heads))
    grad_weight = grad_weight + lax.ppermute(grad_weight, "yh", swap)
    grad_heads = total(a2a(grad_heads, ("yl", "x"))).astype(BF16).T
    grad_weight = jnp.broadcast_to(grad_weight.astype(BF16), (8, 2, 64, 128))
    grad_weight = a2a(grad_weight, "z")
    grad_weight = grad_weight.transpose(2, 0, 1, 3).reshape(64, WIDTH).T
    return (result.T, grad_residual.T, grad_heads, grad_weight)


def solution(mesh):
    view = Mesh(mesh.devices.reshape(SPLIT), AXES)
    return jax.shard_map(
        local,
        mesh=view,
        in_specs=(
            P(EXPERT, TENSOR),
            P(EXPERT, TENSOR),
            P(None, TENSOR),
            P(TENSOR),
            P(EXPERT, None, TENSOR),
            P(EXPERT, TENSOR, None),
            P(EXPERT, None),
            P(EXPERT, None),
            P(EXPERT, TENSOR),
        ),
        out_specs=(
            P(EXPERT, TENSOR),
            P(EXPERT, TENSOR),
            P(EXPERT, TENSOR),
            P(None, TENSOR),
        ),
        check_vma=False,
    )
```

time: 201 us -> 185 us (0.920)
  the two profiles are of different devices: /device:TPU:16 before, /device:TPU:8 now
where the time goes in v2:
time: 185 us; the launch traced here: 184 us
  blocking collectives  90.9 us (49%)
  waiting for transfers between devices  34.2 us (18%)
  starting transfers between devices  32.7 us (18%)
  Pallas kernels  17 us (9%)
  local copies, waits for them, and re-layouts  7.9 us (4%)
    all_to_all x4, blocking collectives, a2a(): return lax.all_to_all(value, axes, split_axis=0, concat_axis=0, tiled=True)  84.5 us
    all_to_all x4, waiting for transfers between devices, a2a(): return lax.all_to_all(value, axes, split_axis=0, concat_axis=0, tiled=True)  28.2 us
    all_to_all x4, starting transfers between devices, a2a(): return lax.all_to_all(value, axes, split_axis=0, concat_axis=0, tiled=True)  24.3 us
    ppermute x1, waiting for transfers between devices, local(): grad_weight = grad_weight + lax.ppermute(grad_weight, 'yh', swap)  6 us
    pallas_call x1, Pallas kernels, local(): call(both_ways, shape((4, 4, PACK, 128), BF16), 'both_ways', 1, 3)  4.6 us
    ppermute x1, starting transfers between devices, local(): grad_weight = grad_weight + lax.ppermute(grad_weight, 'yh', swap)  4.09 us
    unnamed x12, local copies, waits for them, and re-layouts  3.74 us
  transfers between devices with their start and end apart: 7, of which 5 were waited for; matrix products, arithmetic and copies ran while one was open for 1% of the time, Pallas kernels for 4%

profile of v2, /device:TPU:8, one launch (start us, length us, event | category | flops | bytes accessed | tf_op | source)
XLA Modules:
  0.0 184.2 jit_solution(5470619475989244750)
XLA Ops:
  0.6 1.5 broadcast_in_dim.6
  2.1 9.2 %all-to-all-start = ((bf16[16,64,128]{2,1,0:T(8,128)(2,1)}), bf16[16,64,128]{2,1,0:T(8,128)(2,1)S(1)}, u32[]{:S(2)}, u32[]{:S(2)}) async-start(bf16[16,64,128]{2,1,0:T(8,128)(2,1)} %broadcast_in_dim.6), calls=%async_computation | async-start | bytes 524288 | tf_op jit(solution)/shard_map/all_to_all | solution.py:381
  11.3 0.7 copy.16.gain_ref
  12.0 0.0 copy-start.4
  12.0 0.7 copy-done.4
  12.7 0.0 copy-start.5
  12.7 0.7 copy-done.5
  13.4 0.2 prepare.1
  13.6 0.0 copy-start.1
  13.6 0.9 copy-done.1
  14.6 0.0 copy-start.2
  14.6 0.7 copy-done.2
  15.3 0.0 copy-start.3
  15.3 0.7 copy-done.3
  16.0 0.1 pack.1
  16.1 2.3 %all_gather.17.side_ref = bf16[128,2432]{1,0:T(8,128)(2,1)S(1)} all-gather(bf16[64,2432]{1,0:T(8,128)(2,1)S(1)} %pack.1), channel_id=1, replica_groups=mesh['yh'=2,'z'=8,'yl'=4,'x'=4,'c'=2] {'c'}, dimensions={0}, use_global_device_ids=true | all-gather | bytes 933888 | tf_op jit(solution)/shard_map/all_gather | solution.py:398
  18.3 0.9 all-to-all-done
  19.3 2.2 %all-gather = bf16[32,64,128]{2,1,0:T(8,128)(2,1)S(1)} all-gather(bf16[16,64,128]{2,1,0:T(8,128)(2,1)S(1)} %all-to-all-done), channel_id=2, replica_groups=mesh['yh'=2,'z'=8,'yl'=4,'x'=4,'c'=2] {'c'}, dimensions={0}, use_global_device_ids=true | all-gather | bytes 786432 | tf_op jit(solution)/shard_map/all_gather | solution.py:403
  21.4 0.7 dispatch.1
  22.1 31.8 %all_to_all.40 = bf16[64,24,128]{2,1,0:T(8,128)(2,1)S(1)} all-to-all(bf16[64,24,128]{2,1,0:T(8,128)(2,1)S(1)} %bitcast.26), channel_id=1, replica_groups=mesh['yh'=2,'z'=8,'yl'=4,'x'=4,'c'=2] {'yh','z','yl'}, dimensions={0} | all-to-all | bytes 786432 | tf_op jit(solution)/shard_map/all_to_all | solution.py:381
  53.9 0.6 repack.1
  54.6 0.0 copy-start
  54.6 17.7 %all_to_all.41.in_ref = bf16[4,4,304,128]{3,2,1,0:T(8,128)(2,1)S(1)} all-to-all(bf16[4,4,304,128]{3,2,1,0:T(8,128)(2,1)S(1)} %repack.1), channel_id=1, replica_groups=mesh['yh'=2,'z'=8,'yl'=4,'x'=4,'c'=2] {'x'}, dimensions={0} | all-to-all | bytes 2490368 | tf_op jit(solution)/shard_map/all_to_all | solution.py:381
  72.3 1.9 %collective-permute-start = (bf16[4,4,304,128]{3,2,1,0:T(8,128)(2,1)S(1)}, bf16[4,4,304,128]{3,2,1,0:T(8,128)(2,1)S(1)}, u32[]{:S(2)}, u32[]{:S(2)}) collective-permute-start(bf16[4,4,304,128]{3,2,1,0:T(8,128)(2,1)S(1)} %all_to_all.41.in_ref), channel_id=1, source_target_pairs={{0,1},{1,0},{2,3},{3,2},{4,5},{5,4},{6,7},{7,6},{8,9},{9,8},{10,11... | collective-permute-start | bytes 3735560 | tf_op jit(solution)/shard_map/ppermute | solution.py:412
  74.3 0.0 copy-done
  74.3 3.3 %only_ahead.1 = (bf16[4,4,144,128]{3,2,1,0:T(8,128)(2,1)S(1)}, f32[144,256]{1,0:T(8,128)S(1)}, f32[8,256]{1,0:T(8,128)S(1)}, f32[144,128]{1,0:T(8,128)S(1)}) custom-call(s32[1]{0:T(128)} %bitcast.core_ref.which_ref, bf16[4,4,304,128]{3,2,1,0:T(8,128)(2,1)S(1)} %all_to_all.41.in_ref, bf16[2,2048,256]{2,1,0:T(8,128)(2,1)S(1)} %copy-done, ...), custom_call_target="tpu_custom_call" | custom-call | tf_op jit(solution)/shard_map/only_ahead/pallas_call | solution.py:413
  77.6 0.0 collective-permute-done.in_ref
  77.6 4.6 %both_ways.1 = bf16[4,4,304,128]{3,2,1,0:T(8,128)(2,1)S(1)} custom-call(s32[1]{0:T(128)S(6)} %sub.3.which_ref, bf16[4,4,304,128]{3,2,1,0:T(8,128)(2,1)S(1)} %collective-permute-done.in_ref, bf16[2,2048,256]{2,1,0:T(8,128)(2,1)S(1)} %copy-done, bf16[2,256,2048]{2,1,0:T(8,128)(2,1)} %down_ref.5), custom_call_target="tpu_custom_call" | custom-call | tf_op jit(solution)/shard_map/both_ways/pallas_call | solution.py:425
  82.2 2.4 %collective-permute-start.1 = (bf16[4,4,304,128]{3,2,1,0:T(8,128)(2,1)S(1)}, bf16[4,4,304,128]{3,2,1,0:T(8,128)(2,1)S(1)}, u32[]{:S(2)}, u32[]{:S(2)}) collective-permute-start(bf16[4,4,304,128]{3,2,1,0:T(8,128)(2,1)S(1)} %both_ways.1), channel_id=1, source_target_pairs={{0,1},{1,0},{2,3},{3,2},{4,5},{5,4},{6,7},{7,6},{8,9},{9,8},{10,11... | collective-permute-start | bytes 3735560 | tf_op jit(solution)/shard_map/ppermute | solution.py:429
  84.6 3.1 %only_behind.1.grad_ref = bf16[4,4,160,128]{3,2,1,0:T(8,128)(2,1)S(1)} custom-call(s32[1]{0:T(128)} %bitcast.core_ref.which_ref, bf16[4,4,304,128]{3,2,1,0:T(8,128)(2,1)S(1)} %all_to_all.41.in_ref, bf16[2,2048,256]{2,1,0:T(8,128)(2,1)S(1)} %copy-done, bf16[2,256,2048]{2,1,0:T(8,128)(2,1)} %down_ref.5, f32[144,256]{1,0:T(8,128)S(1)} %get-tuple-element.25.pre_ref, ...), custom_call_target="tpu_custom_call" | custom-call | tf_op jit(solution)/shard_map/only_behind/pallas_call | solution.py:430
  87.7 0.0 collective-permute-done.1.came_ref
  87.7 0.3 add_pair.1
  88.1 20.1 %all_to_all.42.in_ref = bf16[4,4,304,128]{3,2,1,0:T(8,128)(2,1)S(1)} all-to-all(bf16[4,4,304,128]{3,2,1,0:T(8,128)(2,1)S(1)} %add_pair.1), channel_id=1, replica_groups=mesh['yh'=2,'z'=8,'yl'=4,'x'=4,'c'=2] {'x'}, dimensions={0} | all-to-all | bytes 2490368 | tf_op jit(solution)/shard_map/all_to_all | solution.py:381
  108.2 1.6 add_four.1
  109.7 7.0 %all-to-all-start.4 = ((bf16[64,24,128]{2,1,0:T(8,128)(2,1)}), bf16[64,24,128]{2,1,0:T(8,128)(2,1)S(1)}, u32[]{:S(2)}, u32[]{:S(2)}) async-start(bf16[64,24,128]{2,1,0:T(8,128)(2,1)} %bitcast.12), calls=%async_computation.4 | async-start | bytes 786432 | tf_op jit(solution)/shard_map/all_to_all | solution.py:381
  116.7 0.5 turn_weight.1.weight_ref
  117.2 15.5 %all-to-all-done.4 = bf16[64,24,128]{2,1,0:T(8,128)(2,1)S(1)} async-done(((bf16[64,24,128]{2,1,0:T(8,128)(2,1)}), bf16[64,24,128]{2,1,0:T(8,128)(2,1)S(1)}, u32[]{:S(2)}, u32[]{:S(2)}) %all-to-all-start.4) | async-done | bytes 393248 | tf_op jit(solution)/shard_map/all_to_all | solution.py:381
  132.7 0.5 combine.1
  133.2 2.0 %all-gather.1 = f32[528,128]{1,0:T(8,128)S(1)} all-gather(f32[264,128]{1,0:T(8,128)S(1)} %combine.1), channel_id=3, replica_groups=mesh['yh'=2,'z'=8,'yl'=4,'x'=4,'c'=2] {'c'}, dimensions={0}, use_global_device_ids=true | all-gather | bytes 405504 | tf_op jit(solution)/shard_map/all_gather | solution.py:440
  135.2 1.5 finish.1
  136.7 14.9 %all_to_all.43 = bf16[8,2,64,128]{3,2,1,0:T(8,128)(2,1)S(1)} all-to-all(bf16[8,2,64,128]{3,2,1,0:T(8,128)(2,1)S(1)} %bitcast.28), channel_id=1, replica_groups=mesh['yh'=2,'z'=8,'yl'=4,'x'=4,'c'=2] {'z'}, dimensions={0} | all-to-all | bytes 524288 | tf_op jit(solution)/shard_map/all_to_all | solution.py:381
  151.6 4.8 %all-to-all-start.6 = ((bf16[16,64,128]{2,1,0:T(8,128)(2,1)}), bf16[16,64,128]{2,1,0:T(8,128)(2,1)S(1)}, u32[]{:S(2)}, u32[]{:S(2)}) async-start(bf16[16,64,128]{2,1,0:T(8,128)(2,1)} %get-tuple-element.34), calls=%async_computation.6 | async-start | bytes 524288 | tf_op jit(solution)/shard_map/all_to_all | solution.py:381
  156.4 4.1 %collective-permute-start.2 = (f32[2,64,128]{2,1,0:T(8,128)S(1)}, f32[2,64,128]{2,1,0:T(8,128)S(1)}, u32[]{:S(2)}, u32[]{:S(2)}) collective-permute-start(f32[2,64,128]{2,1,0:T(8,128)S(1)} %convert_reduce_fusion), channel_id=1, source_target_pairs={{0,256},{256,0},{1,257},{257,1},{2,258},{258,2},{3,259},{259,3},{4... | collective-permute-start | bytes 196616 | tf_op jit(solution)/shard_map/ppermute | solution.py:455
  160.5 6.0 %collective-permute-done.2 = f32[2,64,128]{2,1,0:T(8,128)S(1)} collective-permute-done((f32[2,64,128]{2,1,0:T(8,128)S(1)}, f32[2,64,128]{2,1,0:T(8,128)S(1)}, u32[]{:S(2)}, u32[]{:S(2)}) %collective-permute-start.2) | collective-permute-done | bytes 65568 | tf_op jit(solution)/shard_map/ppermute | solution.py:455
  166.5 2.0 %all-to-all-done.6 = bf16[16,64,128]{2,1,0:T(8,128)(2,1)S(1)} async-done(((bf16[16,64,128]{2,1,0:T(8,128)(2,1)}), bf16[16,64,128]{2,1,0:T(8,128)(2,1)S(1)}, u32[]{:S(2)}, u32[]{:S(2)}) %all-to-all-start.6) | async-done | bytes 262176 | tf_op jit(solution)/shard_map/all_to_all | solution.py:381
  168.5 0.8 broadcast_in_dim.7
  169.3 3.4 %all-to-all-start.7 = ((bf16[8,2,64,128]{3,1,2,0:T(2,128)(2,1)}), bf16[8,2,64,128]{3,1,2,0:T(2,128)(2,1)S(1)}, u32[]{:S(2)}, u32[]{:S(2)}) async-start(bf16[8,2,64,128]{3,1,2,0:T(2,128)(2,1)} %broadcast_in_dim.7), calls=%async_computation.7 | async-start | bytes 524288 | tf_op jit(solution)/shard_map/all_to_all | solution.py:381
  172.8 0.7 reduce_sum.22
  173.4 9.7 %all-to-all-done.7 = bf16[8,2,64,128]{3,1,2,0:T(2,128)(2,1)S(1)} async-done(((bf16[8,2,64,128]{3,1,2,0:T(2,128)(2,1)}), bf16[8,2,64,128]{3,1,2,0:T(2,128)(2,1)S(1)}, u32[]{:S(2)}, u32[]{:S(2)}) %all-to-all-start.7) | async-done | bytes 262176 | tf_op jit(solution)/shard_map/all_to_all | solution.py:381
  183.2 0.2 copy.18
  183.3 0.9 reshape.43
  (3 shorter events, 0.1 us)
Async XLA Ops:
  2.1 17.2 %all-to-all-start = ((bf16[16,64,128]{2,1,0:T(8,128)(2,1)}), bf16[16,64,128]{2,1,0:T(8,128)(2,1)S(1)}, u32[]{:S(2)}, u32[]{:S(2)}) async-start(bf16[16,64,128]{2,1,0:T(8,128)(2,1)} %broadcast_in_dim.6), calls=%async_computation | async-start | bytes 524288 | tf_op jit(solution)/shard_map/all_to_all | solution.py:381
  12.0 0.7 copy-start.4
  12.7 0.7 copy-start.5
  13.6 1.0 copy-start.1
  14.6 0.7 copy-start.2
  15.3 0.7 copy-start.3
  54.6 19.7 %copy-start = (bf16[2,2048,256]{2,1,0:T(8,128)(2,1)S(1)}, bf16[2,2048,256]{2,1,0:T(8,128)(2,1)}, u32[]{:S(2)}) copy-start(bf16[2,2048,256]{2,1,0:T(8,128)(2,1)} %up_ref.5) | copy-start | bytes 6291460
  72.3 5.2 %collective-permute-start = (bf16[4,4,304,128]{3,2,1,0:T(8,128)(2,1)S(1)}, bf16[4,4,304,128]{3,2,1,0:T(8,128)(2,1)S(1)}, u32[]{:S(2)}, u32[]{:S(2)}) collective-permute-start(bf16[4,4,304,128]{3,2,1,0:T(8,128)(2,1)S(1)} %all_to_all.41.in_ref), channel_id=1, source_target_pairs={{0,1},{1,0},{2,3},{3,2},{4,5},{5,4},{6,7},{7,6},{8,9},{9,8},{10,11... | collective-permute-start | bytes 3735560 | tf_op jit(solution)/shard_map/ppermute | solution.py:412
  82.2 5.5 %collective-permute-start.1 = (bf16[4,4,304,128]{3,2,1,0:T(8,128)(2,1)S(1)}, bf16[4,4,304,128]{3,2,1,0:T(8,128)(2,1)S(1)}, u32[]{:S(2)}, u32[]{:S(2)}) collective-permute-start(bf16[4,4,304,128]{3,2,1,0:T(8,128)(2,1)S(1)} %both_ways.1), channel_id=1, source_target_pairs={{0,1},{1,0},{2,3},{3,2},{4,5},{5,4},{6,7},{7,6},{8,9},{9,8},{10,11... | collective-permute-start | bytes 3735560 | tf_op jit(solution)/shard_map/ppermute | solution.py:429
  109.7 23.0 %all-to-all-start.4 = ((bf16[64,24,128]{2,1,0:T(8,128)(2,1)}), bf16[64,24,128]{2,1,0:T(8,128)(2,1)S(1)}, u32[]{:S(2)}, u32[]{:S(2)}) async-start(bf16[64,24,128]{2,1,0:T(8,128)(2,1)} %bitcast.12), calls=%async_computation.4 | async-start | bytes 786432 | tf_op jit(solution)/shard_map/all_to_all | solution.py:381
  151.6 16.9 %all-to-all-start.6 = ((bf16[16,64,128]{2,1,0:T(8,128)(2,1)}), bf16[16,64,128]{2,1,0:T(8,128)(2,1)S(1)}, u32[]{:S(2)}, u32[]{:S(2)}) async-start(bf16[16,64,128]{2,1,0:T(8,128)(2,1)} %get-tuple-element.34), calls=%async_computation.6 | async-start | bytes 524288 | tf_op jit(solution)/shard_map/all_to_all | solution.py:381
  156.4 10.1 %collective-permute-start.2 = (f32[2,64,128]{2,1,0:T(8,128)S(1)}, f32[2,64,128]{2,1,0:T(8,128)S(1)}, u32[]{:S(2)}, u32[]{:S(2)}) collective-permute-start(f32[2,64,128]{2,1,0:T(8,128)S(1)} %convert_reduce_fusion), channel_id=1, source_target_pairs={{0,256},{256,0},{1,257},{257,1},{2,258},{258,2},{3,259},{259,3},{4... | collective-permute-start | bytes 196616 | tf_op jit(solution)/shard_map/ppermute | solution.py:455
  169.3 13.8 %all-to-all-start.7 = ((bf16[8,2,64,128]{3,1,2,0:T(2,128)(2,1)}), bf16[8,2,64,128]{3,1,2,0:T(2,128)(2,1)S(1)}, u32[]{:S(2)}, u32[]{:S(2)}) async-start(bf16[8,2,64,128]{3,1,2,0:T(2,128)(2,1)} %broadcast_in_dim.7), calls=%async_computation.7 | async-start | bytes 524288 | tf_op jit(solution)/shard_map/all_to_all | solution.py:381

commit v3 on v2

--- a/solution.py
+++ b/solution.py
@@ -12,6 +12,7 @@
 BLOCKS = 16
 CAP = 9
 MSG = 24
+ORDER = (0, 2, 1, 3)
 PACK = 304
 SLOTS = BLOCKS * CAP
 SIDE = 2432
@@ -56,8 +57,9 @@
         out_shape=outs,
         in_specs=[pl.BlockSpec(memory_space=pltpu.SMEM)] * n_smem
         + [pl.BlockSpec(memory_space=pltpu.VMEM)] * n_in,
+        out_specs=jax.tree.map(lambda _: pl.BlockSpec(memory_space=pltpu.VMEM), outs),
         name=name,
-        compiler_params=pltpu.CompilerParams(vmem_limit_bytes=48 * 1024 * 1024),
+        compiler_params=pltpu.CompilerParams(vmem_limit_bytes=16 * 1024 * 1024),
     )
 
 
@@ -98,7 +100,7 @@
     out_ref[:, 2304:2432] = jnp.where(lane == 2, low.astype(F32), value).astype(BF16)
 
 
-def prepare(core_ref, routes_ref, gates_ref, place_ref, gate_ref):
+def prepare(core_ref, routes_ref, gates_ref, place_ref, gate_ref, pick_ref, drop_ref):
     core = core_ref[0]
     row = iota((ROWS, 128), 0)
     group = div(row, MSG)
@@ -115,6 +117,8 @@
     place_ref[...] = jnp.where(taken, 1.0, 0.0).astype(BF16)
     gate = jnp.where(first, gates_ref[0:1, :], gates_ref[1:2, :])
     gate_ref[...] = jnp.where(taken, gate, 0.0)
+    pick_ref[...] = selection(iota((PACK, ROWS), 0), iota((PACK, ROWS), 1))
+    drop_ref[...] = selection(iota((ROWS, PACK), 1), iota((ROWS, PACK), 0))
 
 
 def turn_weight(core_ref, side_ref, out_ref):
@@ -160,9 +164,9 @@
     gain = jnp.where(which == 0, gains[:, 0:1], jnp.where(which == 1, gains[:, 1:2], gains[:, 2:3]))
     gain = jnp.sum(jnp.where(mine, gain, 0.0), axis=0, keepdims=True)
     value = jnp.where(local < CAP, rows_x, jnp.where(local < 2 * CAP, rows_c * gate_col, stats))
-    value = jnp.where(local == 18, value + gain, value).astype(BF16)
+    value = jnp.where(local == 18, value + gain, value)
     for e in range(BLOCKS):
-        piece = value[e * MSG : (e + 1) * MSG]
+        piece = value[e * MSG : (e + 1) * MSG].astype(BF16)
         for y in range(4):
             out_ref[e, y] = piece
 
@@ -176,8 +180,8 @@
     return jnp.where(pick, 1.0, 0.0).astype(BF16)
 
 
-def repack(in_ref, out_ref):
-    pick = selection(iota((PACK, ROWS), 0), iota((PACK, ROWS), 1))
+def repack(in_ref, pick_ref, out_ref):
+    pick = pick_ref[...]
     for y in range(4):
         rows = in_ref[:, y].astype(F32).reshape(ROWS, 128).astype(BF16)
         packed = dot_nn(pick, rows).astype(BF16)
@@ -197,20 +201,21 @@
     at = iota((128, 128), 0) - 32
     collect = (at >= 0) & (at < 24) & ((at & 7) == (iota((128, 128), 1) & 7))
     collect = jnp.where(collect, 1.0, 0.0).astype(BF16)
+    ones = jnp.ones((128, 128), BF16)
     own = lax.shift_right_logical(iota((16, 128), 1), 3) == iota((16, 128), 0)
-    chunks = [None] * 16
-    gains = [None] * 16
+    blocks = [in_ref[i % 4, i // 4, 288:304] for i in range(16)]
+    shifts = dot_nn(expand, jnp.concatenate(blocks, axis=1))
+    gain_rows = dot_nn(jnp.concatenate(blocks, axis=0), collect)
+    chunks = []
+    gains = []
     total = jnp.zeros((SLOTS, 128), F32)
-    for x in range(4):
-        for y in range(4):
-            block = in_ref[x, y, 288:304]
-            shift = dot_nn(expand, block)
-            shift = jnp.sum(jnp.where(shift_lane, shift, 0.0), axis=1, keepdims=True)
-            chunk = in_ref[x, y, 0:144].astype(F32) + shift
-            total = total + chunk
-            chunks[y * 4 + x] = chunk
-            gain = jnp.where(own, dot_nn(block, collect), 0.0)
-            gains[y * 4 + x] = jnp.sum(gain, axis=0, keepdims=True)
+    for i in range(16):
+        shift = jnp.where(shift_lane, shifts[:, i * 128 : i * 128 + 128], 0.0).astype(BF16)
+        chunk = in_ref[i % 4, i // 4, 0:144].astype(F32) + dot_nn(shift, ones)
+        total = total + chunk
+        chunks.append(chunk)
+        gain = jnp.where(own, gain_rows[i * 16 : i * 16 + 16], 0.0)
+        gains.append(jnp.sum(gain, axis=0, keepdims=True))
     center = jnp.sum(total, axis=1, keepdims=True) / WIDTH
     squares = jnp.zeros((SLOTS, 128), F32)
     for i in range(16):
@@ -315,16 +320,16 @@
             out_ref[x, y, 288:304] = part(join(grad[144:160] + came[288:304]))
 
 
-def add_four(in_ref, out_ref):
-    pick = selection(iota((ROWS, PACK), 1), iota((ROWS, PACK), 0))
+def add_four(in_ref, drop_ref, out_ref):
+    drop = drop_ref[...]
     for y in range(4):
         value = in_ref[0, y].astype(F32)
         for x in range(1, 4):
             value = value + in_ref[x, y].astype(F32)
         rows = jnp.concatenate([value[0:288].astype(BF16), part(join(value[288:304]))], axis=0)
-        message = dot_nn(pick, rows).astype(BF16)
+        message = dot_nn(drop, rows)
         for e in range(BLOCKS):
-            out_ref[e, y] = message[e * MSG : (e + 1) * MSG]
+            out_ref[e, y] = message[e * MSG : (e + 1) * MSG].astype(BF16)
 
 
 def combine(in_ref, place_ref, gate_ref, out_ref):
@@ -352,7 +357,7 @@
 
 
 def finish(
-    core_ref, in_ref, stream_ref, side_ref, weight_ref, heads_ref, result_ref, grad_ref, gh_ref, gw_ref
+    core_ref, in_ref, stream_ref, side_ref, heads_ref, result_ref, grad_ref, pair_ref, gw_ref
 ):
     got = in_ref[0] + in_ref[1]
     stream = stream_ref[...]
@@ -370,15 +375,34 @@
     result_ref[...] = jnp.where(low, result[0:64], result[64:128]).astype(BF16)
     own = jnp.where(low, grad[0:64], grad[64:128]).astype(BF16)
     grad_ref[...] = own
-    grad = grad.astype(BF16)
+    pair_ref[...] = grad.astype(BF16)
     for chip in range(16):
-        gh_ref[chip] = dot_nn(weight_ref[chip], grad).astype(BF16)
         heads = jnp.concatenate([heads_ref[0, chip], heads_ref[1, chip]], axis=0)
         gw_ref[chip] = dot_nt(own, heads).astype(BF16)
 
 
+def heads_back(at_ref, pair_ref, weight_ref, keep_ref, send_ref):
+    for k in range(4):
+        for j in range(4):
+            chip = (at_ref[1] ^ ORDER[j]) * 4 + (at_ref[0] ^ ORDER[k])
+            out_ref = keep_ref if k < 2 else send_ref
+            out_ref[k % 2, j] = dot_nn(weight_ref[chip], pair_ref[...]).astype(BF16)
+
+
+def lay(in_ref, out_ref):
+    for chip in range(16):
+        out_ref[:, chip * 128 : chip * 128 + 128] = in_ref[chip]
+
+
 def a2a(value, axes):
     return lax.all_to_all(value, axes, split_axis=0, concat_axis=0, tiled=True)
+
+
+def halve(keep, send, axis):
+    came = lax.ppermute(send, axis, [(i, i ^ 1) for i in range(4)])
+    half = keep.astype(F32) + came.astype(F32)
+    came = lax.ppermute(half[1].astype(BF16), axis, [(i, i ^ 2) for i in range(4)])
+    return half[0], came
 
 
 def total(value):
@@ -396,17 +420,27 @@
         out_weight.T, residual.T, cotangent.T, norm_gain.reshape(64, 1)
     )
     side = lax.all_gather(side, "c", axis=0, tiled=True)
-    place, gate = call(
-        prepare, (shape((ROWS, 128), BF16), shape((ROWS, 128), F32)), "prepare", 1, 2
+    place, gate, pick, drop = call(
+        prepare,
+        (
+            shape((ROWS, 128), BF16),
+            shape((ROWS, 128), F32),
+            shape((PACK, ROWS), BF16),
+            shape((ROWS, PACK), BF16),
+        ),
+        "prepare",
+        1,
+        2,
     )(core, routes.T, gates.T)
     turned = call(turn_weight, shape((16, 64, 128), BF16), "turn_weight", 1, 1)(core, side)
+    heads_t, turned = lax.optimization_barrier((heads_t, turned))
     heads_t = lax.all_gather(heads_t, "c", axis=0)
     stream, message = call(
         dispatch, (shape((128, 128), F32), shape((BLOCKS, 4, MSG, 128), BF16)), "dispatch", 1, 4
     )(block, heads_t, side, place, gate)
     message = a2a(message.reshape(64, MSG, 128), ("yh", "z", "yl"))
-    packed = call(repack, shape((4, 4, PACK, 128), BF16), "repack", 0, 1)(
-        message.reshape(BLOCKS, 4, MSG, 128)
+    packed = call(repack, shape((4, 4, PACK, 128), BF16), "repack", 0, 2)(
+        message.reshape(BLOCKS, 4, MSG, 128), pick
     )
     mine = a2a(packed, "x")
     other = lax.ppermute(mine, "c", swap)
@@ -432,32 +466,40 @@
     )
     summed = call(add_pair, shape((4, 4, PACK, 128), BF16), "add_pair", 0, 3)(value, grad, came)
     summed = a2a(summed, "x")
-    message = call(add_four, shape((BLOCKS, 4, MSG, 128), BF16), "add_four", 0, 1)(summed)
+    message = call(add_four, shape((BLOCKS, 4, MSG, 128), BF16), "add_four", 0, 2)(
+        summed, drop
+    )
     message = a2a(message.reshape(64, MSG, 128), ("yh", "z", "yl"))
     both = call(combine, shape((264, 128), F32), "combine", 0, 3)(
         message.reshape(BLOCKS, 4, MSG, 128), place, gate
     )
     both = lax.all_gather(both, "c", axis=0)
-    result, grad_residual, grad_heads, grad_weight = call(
+    result, grad_residual, grad_pair, grad_weight = call(
         finish,
         (
             shape((64, 128), BF16),
             shape((64, 128), BF16),
-            shape((16, 64, 128), BF16),
+            shape((128, 128), BF16),
             shape((16, 64, 128), BF16),
         ),
         "finish",
         1,
-        5,
-    )(core, both, stream, side, turned, heads_t)
-    grad_weight = total(a2a(grad_weight.reshape(8, 2, 64, 128), "z"))
-    grad_weight, grad_heads = lax.optimization_barrier((grad_weight, grad_heads))
-    grad_weight = grad_weight + lax.ppermute(grad_weight, "yh", swap)
-    grad_heads = total(a2a(grad_heads, ("yl", "x"))).astype(BF16).T
-    grad_weight = jnp.broadcast_to(grad_weight.astype(BF16), (8, 2, 64, 128))
-    grad_weight = a2a(grad_weight, "z")
-    grad_weight = grad_weight.transpose(2, 0, 1, 3).reshape(64, WIDTH).T
-    return (result.T, grad_residual.T, grad_heads, grad_weight)
+        4,
+    )(core, both, stream, side, heads_t)
+    grad_weight = total(a2a(grad_weight, EXPERT)).astype(BF16)
+    at = jnp.stack([lax.axis_index("x"), lax.axis_index("yl")]).astype(jnp.int32)
+    keep, send = call(heads_back, (shape((2, 4, 64, 128), BF16),) * 2, "heads_back", 1, 2)(
+        at, grad_pair, turned
+    )
+    pieces = halve(keep, send, "x")
+    grad_weight = jnp.broadcast_to(grad_weight, (16, 64, 128))
+    grad_weight, pieces = lax.optimization_barrier((grad_weight, pieces))
+    grad_weight = a2a(grad_weight, EXPERT)
+    grad_weight = call(lay, shape((64, WIDTH), BF16), "lay", 0, 1)(grad_weight)
+    heads_sum = (pieces[0] + pieces[1].astype(F32)).astype(BF16)
+    pieces = halve(heads_sum[0:2], heads_sum[2:4], "yl")
+    grad_heads = (pieces[0] + pieces[1].astype(F32)).astype(BF16).T
+    return (result.T, grad_residual.T, grad_heads, grad_weight.T)
 
 
 def solution(mesh):

time: 185 us -> 180 us (0.973)
  the two profiles are of different devices: /device:TPU:8 before, /device:TPU:16 now
where the time goes in v3:
time: 180 us; the launch traced here: 179 us
  blocking collectives  76.8 us (43%)
  waiting for transfers between devices  41.5 us (23%)
  starting transfers between devices  39.5 us (22%)
  Pallas kernels  13.8 us (8%)
  local copies, waits for them, and re-layouts  5.42 us (3%)
    all_to_all x3, blocking collectives, a2a(): return lax.all_to_all(value, axes, split_axis=0, concat_axis=0, tiled=True)  70.4 us
    all_to_all x4, waiting for transfers between devices, a2a(): return lax.all_to_all(value, axes, split_axis=0, concat_axis=0, tiled=True)  33.4 us
    all_to_all x4, starting transfers between devices, a2a(): return lax.all_to_all(value, axes, split_axis=0, concat_axis=0, tiled=True)  25.5 us
    ppermute x2, starting transfers between devices, halve(): lax.ppermute(half[1].astype(BF16), axis, [(i, i ^ 2) for i in range(4)])  5.66 us
    ppermute x2, waiting for transfers between devices, halve(): lax.ppermute(half[1].astype(BF16), axis, [(i, i ^ 2) for i in range(4)])  4.81 us
    ppermute x2, starting transfers between devices, halve(): came = lax.ppermute(send, axis, [(i, i ^ 1) for i in range(4)])  4.4 us
  transfers between devices with their start and end apart: 10, of which 8 were waited for; matrix products, arithmetic and copies ran while one was open for 1% of the time, Pallas kernels for 3%

profile of v3, /device:TPU:16, one launch (start us, length us, event | category | flops | bytes accessed | tf_op | source)
XLA Modules:
  0.0 178.7 jit_solution(14071460267951371682)
XLA Ops:
  0.6 1.5 broadcast_in_dim.6
  2.1 9.1 %all-to-all-start = ((bf16[16,64,128]{2,1,0:T(8,128)(2,1)}), bf16[16,64,128]{2,1,0:T(8,128)(2,1)S(1)}, u32[]{:S(2)}, u32[]{:S(2)}) async-start(bf16[16,64,128]{2,1,0:T(8,128)(2,1)} %broadcast_in_dim.6), calls=%async_computation | async-start | bytes 524288 | tf_op jit(solution)/shard_map/all_to_all | solution.py:398
  11.2 0.0 copy-start.5
  11.2 0.0 copy-start.6
  11.2 0.8 copy.14.gain_ref
  12.0 0.0 copy-start.2
  12.0 0.9 copy-done.2
  12.9 0.0 copy-start.3
  12.9 0.7 copy-done.3
  13.6 0.0 copy-start.4
  13.6 0.7 copy-done.4
  14.3 0.1 pack.1
  14.4 2.3 %all_gather.15.side_ref = bf16[128,2432]{1,0:T(8,128)(2,1)S(1)} all-gather(bf16[64,2432]{1,0:T(8,128)(2,1)S(1)} %pack.1), channel_id=1, replica_groups=mesh['yh'=2,'z'=8,'yl'=4,'x'=4,'c'=2] {'c'}, dimensions={0}, use_global_device_ids=true | all-gather | bytes 933888 | tf_op jit(solution)/shard_map/all_gather | solution.py:422
  16.7 0.5 turn_weight.1.weight_ref
  17.2 0.0 copy-done.5
  17.2 0.0 copy-done.6
  17.2 1.0 prepare.1
  18.2 0.6 all-to-all-done
  18.8 2.2 %all-gather = bf16[32,64,128]{2,1,0:T(8,128)(2,1)S(1)} all-gather(bf16[16,64,128]{2,1,0:T(8,128)(2,1)S(1)} %all-to-all-done), channel_id=2, replica_groups=mesh['yh'=2,'z'=8,'yl'=4,'x'=4,'c'=2] {'c'}, dimensions={0}, use_global_device_ids=true | all-gather | bytes 786432 | tf_op jit(solution)/shard_map/all_gather | solution.py:437
  21.0 0.7 dispatch.1
  21.7 31.9 %all_to_all.35 = bf16[64,24,128]{2,1,0:T(8,128)(2,1)S(1)} all-to-all(bf16[64,24,128]{2,1,0:T(8,128)(2,1)S(1)} %bitcast.41), channel_id=1, replica_groups=mesh['yh'=2,'z'=8,'yl'=4,'x'=4,'c'=2] {'yh','z','yl'}, dimensions={0} | all-to-all | bytes 786432 | tf_op jit(solution)/shard_map/all_to_all | solution.py:398
  53.6 0.0 copy-start.1
  53.6 0.5 repack.1
  54.1 0.0 copy-start
  54.1 18.3 %all_to_all.36.in_ref = bf16[4,4,304,128]{3,2,1,0:T(8,128)(2,1)S(1)} all-to-all(bf16[4,4,304,128]{3,2,1,0:T(8,128)(2,1)S(1)} %repack.1), channel_id=1, replica_groups=mesh['yh'=2,'z'=8,'yl'=4,'x'=4,'c'=2] {'x'}, dimensions={0} | all-to-all | bytes 2490368 | tf_op jit(solution)/shard_map/all_to_all | solution.py:398
  72.4 1.9 %collective-permute-start = (bf16[4,4,304,128]{3,2,1,0:T(8,128)(2,1)S(1)}, bf16[4,4,304,128]{3,2,1,0:T(8,128)(2,1)S(1)}, u32[]{:S(2)}, u32[]{:S(2)}) collective-permute-start(bf16[4,4,304,128]{3,2,1,0:T(8,128)(2,1)S(1)} %all_to_all.36.in_ref), channel_id=1, source_target_pairs={{0,1},{1,0},{2,3},{3,2},{4,5},{5,4},{6,7},{7,6},{8,9},{9,8},{10,11... | collective-permute-start | bytes 3735560 | tf_op jit(solution)/shard_map/ppermute | solution.py:446
  74.3 0.0 copy-done.1
  74.3 0.0 copy-done
  74.3 1.8 only_ahead.1
  76.1 1.1 collective-permute-done.in_ref
  77.2 2.8 %both_ways.1 = bf16[4,4,304,128]{3,2,1,0:T(8,128)(2,1)S(1)} custom-call(s32[1]{0:T(128)S(6)} %sub.3.which_ref, bf16[4,4,304,128]{3,2,1,0:T(8,128)(2,1)S(1)} %collective-permute-done.in_ref, bf16[2,2048,256]{2,1,0:T(8,128)(2,1)S(1)} %copy-done, bf16[2,256,2048]{2,1,0:T(8,128)(2,1)S(1)} %copy-done.1), custom_call_target="tpu_custom_call" | custom-call | tf_op jit(solution)/shard_map/both_ways/pallas_call | solution.py:459
  80.0 2.0 %collective-permute-start.1 = (bf16[4,4,304,128]{3,2,1,0:T(8,128)(2,1)S(1)}, bf16[4,4,304,128]{3,2,1,0:T(8,128)(2,1)S(1)}, u32[]{:S(2)}, u32[]{:S(2)}) collective-permute-start(bf16[4,4,304,128]{3,2,1,0:T(8,128)(2,1)S(1)} %both_ways.1), channel_id=1, source_target_pairs={{0,1},{1,0},{2,3},{3,2},{4,5},{5,4},{6,7},{7,6},{8,9},{9,8},{10,11... | collective-permute-start | bytes 3735560 | tf_op jit(solution)/shard_map/ppermute | solution.py:463
  82.0 1.5 only_behind.1.grad_ref
  83.6 1.2 collective-permute-done.1.came_ref
  84.8 0.3 add_pair.1
  85.2 20.2 %all_to_all.37.in_ref = bf16[4,4,304,128]{3,2,1,0:T(8,128)(2,1)S(1)} all-to-all(bf16[4,4,304,128]{3,2,1,0:T(8,128)(2,1)S(1)} %add_pair.1), channel_id=1, replica_groups=mesh['yh'=2,'z'=8,'yl'=4,'x'=4,'c'=2] {'x'}, dimensions={0} | all-to-all | bytes 2490368 | tf_op jit(solution)/shard_map/all_to_all | solution.py:398
  105.4 1.3 add_four.1
  106.6 6.7 %all-to-all-start.4 = ((bf16[64,24,128]{2,1,0:T(8,128)(2,1)}), bf16[64,24,128]{2,1,0:T(8,128)(2,1)S(1)}, u32[]{:S(2)}, u32[]{:S(2)}) async-start(bf16[64,24,128]{2,1,0:T(8,128)(2,1)} %bitcast.12), calls=%async_computation.4 | async-start | bytes 786432 | tf_op jit(solution)/shard_map/all_to_all | solution.py:398
  113.3 0.1 pad_add_fusion.at_ref
  113.4 15.7 %all-to-all-done.4 = bf16[64,24,128]{2,1,0:T(8,128)(2,1)S(1)} async-done(((bf16[64,24,128]{2,1,0:T(8,128)(2,1)}), bf16[64,24,128]{2,1,0:T(8,128)(2,1)S(1)}, u32[]{:S(2)}, u32[]{:S(2)}) %all-to-all-start.4) | async-done | bytes 393248 | tf_op jit(solution)/shard_map/all_to_all | solution.py:398
  129.1 0.5 combine.1
  129.6 2.0 %all-gather.1 = f32[528,128]{1,0:T(8,128)S(1)} all-gather(f32[264,128]{1,0:T(8,128)S(1)} %combine.1), channel_id=3, replica_groups=mesh['yh'=2,'z'=8,'yl'=4,'x'=4,'c'=2] {'c'}, dimensions={0}, use_global_device_ids=true | all-gather | bytes 405504 | tf_op jit(solution)/shard_map/all_gather | solution.py:476
  131.6 1.3 finish.1
  132.9 0.8 heads_back.1
  133.7 2.5 %collective-permute-start.2 = (bf16[2,4,64,128]{3,2,1,0:T(8,128)(2,1)S(1)}, bf16[2,4,64,128]{3,2,1,0:T(8,128)(2,1)S(1)}, u32[]{:S(2)}, u32[]{:S(2)}) collective-permute-start(bf16[2,4,64,128]{3,2,1,0:T(8,128)(2,1)S(1)} %get-tuple-element.46), channel_id=1, source_target_pairs={{0,2},{2,0},{4,6},{6,4},{1,3},{3,1},{5,7},{7,5},{8,10},{10,8},{12,... | collective-permute-start | bytes 393224 | tf_op jit(solution)/shard_map/ppermute | solution.py:402
  136.1 4.0 %all-to-all-start.5 = ((bf16[16,64,128]{2,1,0:T(8,128)(2,1)}), bf16[16,64,128]{2,1,0:T(8,128)(2,1)S(1)}, u32[]{:S(2)}, u32[]{:S(2)}) async-start(bf16[16,64,128]{2,1,0:T(8,128)(2,1)} %get-tuple-element.42), calls=%async_computation.5 | async-start | bytes 524288 | tf_op jit(solution)/shard_map/all_to_all | solution.py:398
  140.2 0.9 collective-permute-done.2
  141.2 3.1 %collective-permute-start.3 = (bf16[4,64,128]{2,1,0:T(8,128)(2,1)S(1)}, bf16[4,64,128]{2,1,0:T(8,128)(2,1)S(1)}, u32[]{:S(2)}, u32[]{:S(2)}) collective-permute-start(bf16[4,64,128]{2,1,0:T(8,128)(2,1)S(1)} %fusion), channel_id=1, source_target_pairs={{0,4},{2,6},{4,0},{6,2},{1,5},{3,7},{5,1},{7,3},{8,12},{10,14},{12... | collective-permute-start | bytes 196616 | tf_op jit(solution)/shard_map/ppermute | solution.py:404
  144.2 11.3 %all-to-all-done.5 = bf16[16,64,128]{2,1,0:T(8,128)(2,1)S(1)} async-done(((bf16[16,64,128]{2,1,0:T(8,128)(2,1)}), bf16[16,64,128]{2,1,0:T(8,128)(2,1)S(1)}, u32[]{:S(2)}, u32[]{:S(2)}) %all-to-all-start.5) | async-done | bytes 262176 | tf_op jit(solution)/shard_map/all_to_all | solution.py:398
  155.6 0.0 collective-permute-done.3
  155.6 0.8 broadcast_in_dim.7
  156.4 1.9 %collective-permute-start.4 = (bf16[2,64,128]{2,1,0:T(8,128)(2,1)S(1)}, bf16[2,64,128]{2,1,0:T(8,128)(2,1)S(1)}, u32[]{:S(2)}, u32[]{:S(2)}) collective-permute-start(bf16[2,64,128]{2,1,0:T(8,128)(2,1)S(1)} %slice.29), channel_id=1, source_target_pairs={{0,8},{8,0},{16,24},{24,16},{1,9},{9,1},{17,25},{25,17},{2,10},{10... | collective-permute-start | bytes 98312 | tf_op jit(solution)/shard_map/ppermute | solution.py:402
  158.3 5.8 %all-to-all-start.6 = ((bf16[16,64,128]{2,1,0:T(8,128)(2,1)}), bf16[16,64,128]{2,1,0:T(8,128)(2,1)S(1)}, u32[]{:S(2)}, u32[]{:S(2)}) async-start(bf16[16,64,128]{2,1,0:T(8,128)(2,1)} %broadcast_in_dim.7), calls=%async_computation.6 | async-start | bytes 524288 | tf_op jit(solution)/shard_map/all_to_all | solution.py:398
  164.1 0.0 collective-permute-done.4
  164.1 2.6 %collective-permute-start.5 = (bf16[64,128]{1,0:T(8,128)(2,1)S(1)}, bf16[64,128]{1,0:T(8,128)(2,1)S(1)}, u32[]{:S(2)}, u32[]{:S(2)}) collective-permute-start(bf16[64,128]{1,0:T(8,128)(2,1)S(1)} %fusion.4), channel_id=1, source_target_pairs={{0,16},{8,24},{16,0},{24,8},{1,17},{9,25},{17,1},{25,9},{2,18},{10... | collective-permute-start | bytes 49160 | tf_op jit(solution)/shard_map/ppermute | solution.py:404
  166.7 4.8 %collective-permute-done.5 = bf16[64,128]{1,0:T(8,128)(2,1)S(1)} collective-permute-done((bf16[64,128]{1,0:T(8,128)(2,1)S(1)}, bf16[64,128]{1,0:T(8,128)(2,1)S(1)}, u32[]{:S(2)}, u32[]{:S(2)}) %collective-permute-start.5) | collective-permute-done | bytes 16416 | tf_op jit(solution)/shard_map/ppermute | solution.py:404
  171.5 0.6 fusion.3
  172.1 5.8 %all-to-all-done.6.in_ref = bf16[16,64,128]{2,1,0:T(8,128)(2,1)S(1)} async-done(((bf16[16,64,128]{2,1,0:T(8,128)(2,1)}), bf16[16,64,128]{2,1,0:T(8,128)(2,1)S(1)}, u32[]{:S(2)}, u32[]{:S(2)}) %all-to-all-start.6) | async-done | bytes 262176 | tf_op jit(solution)/shard_map/all_to_all | solution.py:398
  178.0 0.8 lay.1
  (8 shorter events, 0.1 us)
Async XLA Ops:
  2.1 16.7 %all-to-all-start = ((bf16[16,64,128]{2,1,0:T(8,128)(2,1)}), bf16[16,64,128]{2,1,0:T(8,128)(2,1)S(1)}, u32[]{:S(2)}, u32[]{:S(2)}) async-start(bf16[16,64,128]{2,1,0:T(8,128)(2,1)} %broadcast_in_dim.6), calls=%async_computation | async-start | bytes 524288 | tf_op jit(solution)/shard_map/all_to_all | solution.py:398
  11.2 6.0 %copy-start.5 = (s32[128,2]{0,1:T(2,128)S(1)}, s32[128,2]{0,1:T(2,128)}, u32[]{:S(2)}) copy-start(s32[128,2]{0,1:T(2,128)} %param.15) | copy-start | bytes 3076
  11.2 6.0 %copy-start.6 = (f32[128,2]{0,1:T(2,128)S(1)}, f32[128,2]{0,1:T(2,128)}, u32[]{:S(2)}) copy-start(f32[128,2]{0,1:T(2,128)} %param.16) | copy-start | bytes 3076
  12.0 0.9 copy-start.2
  12.9 0.7 copy-start.3
  13.6 0.7 copy-start.4
  53.6 20.7 %copy-start.1 = (bf16[2,256,2048]{2,1,0:T(8,128)(2,1)S(1)}, bf16[2,256,2048]{2,1,0:T(8,128)(2,1)}, u32[]{:S(2)}) copy-start(bf16[2,256,2048]{2,1,0:T(8,128)(2,1)} %down_ref.5) | copy-start | bytes 6291460
  54.1 20.2 %copy-start = (bf16[2,2048,256]{2,1,0:T(8,128)(2,1)S(1)}, bf16[2,2048,256]{2,1,0:T(8,128)(2,1)}, u32[]{:S(2)}) copy-start(bf16[2,2048,256]{2,1,0:T(8,128)(2,1)} %up_ref.5) | copy-start | bytes 6291460
  72.4 4.8 %collective-permute-start = (bf16[4,4,304,128]{3,2,1,0:T(8,128)(2,1)S(1)}, bf16[4,4,304,128]{3,2,1,0:T(8,128)(2,1)S(1)}, u32[]{:S(2)}, u32[]{:S(2)}) collective-permute-start(bf16[4,4,304,128]{3,2,1,0:T(8,128)(2,1)S(1)} %all_to_all.36.in_ref), channel_id=1, source_target_pairs={{0,1},{1,0},{2,3},{3,2},{4,5},{5,4},{6,7},{7,6},{8,9},{9,8},{10,11... | collective-permute-start | bytes 3735560 | tf_op jit(solution)/shard_map/ppermute | solution.py:446
  80.0 4.8 %collective-permute-start.1 = (bf16[4,4,304,128]{3,2,1,0:T(8,128)(2,1)S(1)}, bf16[4,4,304,128]{3,2,1,0:T(8,128)(2,1)S(1)}, u32[]{:S(2)}, u32[]{:S(2)}) collective-permute-start(bf16[4,4,304,128]{3,2,1,0:T(8,128)(2,1)S(1)} %both_ways.1), channel_id=1, source_target_pairs={{0,1},{1,0},{2,3},{3,2},{4,5},{5,4},{6,7},{7,6},{8,9},{9,8},{10,11... | collective-permute-start | bytes 3735560 | tf_op jit(solution)/shard_map/ppermute | solution.py:463
  106.6 22.4 %all-to-all-start.4 = ((bf16[64,24,128]{2,1,0:T(8,128)(2,1)}), bf16[64,24,128]{2,1,0:T(8,128)(2,1)S(1)}, u32[]{:S(2)}, u32[]{:S(2)}) async-start(bf16[64,24,128]{2,1,0:T(8,128)(2,1)} %bitcast.12), calls=%async_computation.4 | async-start | bytes 786432 | tf_op jit(solution)/shard_map/all_to_all | solution.py:398
  133.7 7.4 %collective-permute-start.2 = (bf16[2,4,64,128]{3,2,1,0:T(8,128)(2,1)S(1)}, bf16[2,4,64,128]{3,2,1,0:T(8,128)(2,1)S(1)}, u32[]{:S(2)}, u32[]{:S(2)}) collective-permute-start(bf16[2,4,64,128]{3,2,1,0:T(8,128)(2,1)S(1)} %get-tuple-element.46), channel_id=1, source_target_pairs={{0,2},{2,0},{4,6},{6,4},{1,3},{3,1},{5,7},{7,5},{8,10},{10,8},{12,... | collective-permute-start | bytes 393224 | tf_op jit(solution)/shard_map/ppermute | solution.py:402
  136.1 19.4 %all-to-all-start.5 = ((bf16[16,64,128]{2,1,0:T(8,128)(2,1)}), bf16[16,64,128]{2,1,0:T(8,128)(2,1)S(1)}, u32[]{:S(2)}, u32[]{:S(2)}) async-start(bf16[16,64,128]{2,1,0:T(8,128)(2,1)} %get-tuple-element.42), calls=%async_computation.5 | async-start | bytes 524288 | tf_op jit(solution)/shard_map/all_to_all | solution.py:398
  141.2 14.4 %collective-permute-start.3 = (bf16[4,64,128]{2,1,0:T(8,128)(2,1)S(1)}, bf16[4,64,128]{2,1,0:T(8,128)(2,1)S(1)}, u32[]{:S(2)}, u32[]{:S(2)}) collective-permute-start(bf16[4,64,128]{2,1,0:T(8,128)(2,1)S(1)} %fusion), channel_id=1, source_target_pairs={{0,4},{2,6},{4,0},{6,2},{1,5},{3,7},{5,1},{7,3},{8,12},{10,14},{12... | collective-permute-start | bytes 196616 | tf_op jit(solution)/shard_map/ppermute | solution.py:404
  156.4 7.7 %collective-permute-start.4 = (bf16[2,64,128]{2,1,0:T(8,128)(2,1)S(1)}, bf16[2,64,128]{2,1,0:T(8,128)(2,1)S(1)}, u32[]{:S(2)}, u32[]{:S(2)}) collective-permute-start(bf16[2,64,128]{2,1,0:T(8,128)(2,1)S(1)} %slice.29), channel_id=1, source_target_pairs={{0,8},{8,0},{16,24},{24,16},{1,9},{9,1},{17,25},{25,17},{2,10},{10... | collective-permute-start | bytes 98312 | tf_op jit(solution)/shard_map/ppermute | solution.py:402
  158.3 19.7 %all-to-all-start.6 = ((bf16[16,64,128]{2,1,0:T(8,128)(2,1)}), bf16[16,64,128]{2,1,0:T(8,128)(2,1)S(1)}, u32[]{:S(2)}, u32[]{:S(2)}) async-start(bf16[16,64,128]{2,1,0:T(8,128)(2,1)} %broadcast_in_dim.7), calls=%async_computation.6 | async-start | bytes 524288 | tf_op jit(solution)/shard_map/all_to_all | solution.py:398
  164.1 7.4 %collective-permute-start.5 = (bf16[64,128]{1,0:T(8,128)(2,1)S(1)}, bf16[64,128]{1,0:T(8,128)(2,1)S(1)}, u32[]{:S(2)}, u32[]{:S(2)}) collective-permute-start(bf16[64,128]{1,0:T(8,128)(2,1)S(1)} %fusion.4), channel_id=1, source_target_pairs={{0,16},{8,24},{16,0},{24,8},{1,17},{9,25},{17,1},{25,9},{2,18},{10... | collective-permute-start | bytes 49160 | tf_op jit(solution)/shard_map/ppermute | solution.py:404

commit v4 on v3

--- a/solution.py
+++ b/solution.py
@@ -90,17 +90,16 @@
     return jnp.where(lane < 64, high.astype(F32), low.astype(F32)).astype(BF16)
 
 
-def pack(weight_ref, residual_ref, cotangent_ref, gain_ref, out_ref):
-    out_ref[:, 0:2048] = weight_ref[...]
-    out_ref[:, 2048:2176] = residual_ref[...]
-    out_ref[:, 2176:2304] = cotangent_ref[...]
-    high, middle, low = split_three(jnp.broadcast_to(gain_ref[...], (64, 128)))
-    lane = iota((64, 128), 1)
-    value = jnp.where(lane == 0, high.astype(F32), middle.astype(F32))
-    out_ref[:, 2304:2432] = jnp.where(lane == 2, low.astype(F32), value).astype(BF16)
-
-
-def prepare(core_ref, routes_ref, gates_ref, place_ref, gate_ref, pick_ref, drop_ref):
+def prepare(
+    core_ref, wide_ref, small_ref, side_ref, place_ref, gate_ref, pick_ref, drop_ref
+):
+    side_ref[:, 0:2304] = wide_ref[...]
+    pick = iota((PACK, ROWS), 0) == packed_row(iota((8, ROWS), 1))[0:1]
+    pick_ref[...] = jnp.where(pick, 1.0, 0.0).astype(BF16)
+    drop = iota((ROWS, PACK), 1) == packed_row(iota((ROWS, 128), 0))[:, 0:1]
+    drop_ref[...] = jnp.where(drop, 1.0, 0.0).astype(BF16)
+    routes = small_ref[0:2].astype(jnp.int32)
+    gates = small_ref[2:4]
     core = core_ref[0]
     row = iota((ROWS, 128), 0)
     group = div(row, MSG)
@@ -108,17 +107,21 @@
     slot = jnp.where(local < CAP, local, local - CAP)
     used = local < 2 * CAP
     expert = 2 * group + core
-    first = (routes_ref[0:1, :] == expert) & used
-    second = (routes_ref[1:2, :] == expert) & used
+    first = (routes[0:1, :] == expert) & used
+    second = (routes[1:2, :] == expert) & used
     named = jnp.where(first | second, 1.0, 0.0)
     before = (iota((128, 128), 0) < iota((128, 128), 1)).astype(F32).astype(BF16)
     earlier = dot_nn(named.astype(BF16), before)
     taken = (earlier == slot.astype(F32)) & (named > 0.5)
     place_ref[...] = jnp.where(taken, 1.0, 0.0).astype(BF16)
-    gate = jnp.where(first, gates_ref[0:1, :], gates_ref[1:2, :])
+    gate = jnp.where(first, gates[0:1, :], gates[1:2, :])
     gate_ref[...] = jnp.where(taken, gate, 0.0)
-    pick_ref[...] = selection(iota((PACK, ROWS), 0), iota((PACK, ROWS), 1))
-    drop_ref[...] = selection(iota((ROWS, PACK), 1), iota((ROWS, PACK), 0))
+    own = iota((64, 64), 0) == iota((64, 64), 1)
+    gain = jnp.sum(jnp.where(own, small_ref[4:5, 0:64], 0.0), axis=1, keepdims=True)
+    high, middle, low = split_three(jnp.broadcast_to(gain, (64, 128)))
+    lane = iota((64, 128), 1)
+    value = jnp.where(lane == 0, high.astype(F32), middle.astype(F32))
+    side_ref[:, 2304:2432] = jnp.where(lane == 2, low.astype(F32), value).astype(BF16)
 
 
 def turn_weight(core_ref, side_ref, out_ref):
@@ -171,13 +174,11 @@
             out_ref[e, y] = piece
 
 
-def selection(to, come):
+def packed_row(come):
     group = div(come, MSG)
     local = come - group * MSG
-    pick = (local < CAP) & (to == group * CAP + local)
-    pick |= (local >= CAP) & (local < 2 * CAP) & (to == SLOTS + group * CAP + local - CAP)
-    pick |= (local == 18) & (to == 2 * SLOTS + group)
-    return jnp.where(pick, 1.0, 0.0).astype(BF16)
+    to = jnp.where(local < CAP, group * CAP + local, SLOTS + group * CAP + local - CAP)
+    return jnp.where(local < 2 * CAP, to, jnp.where(local == 18, 2 * SLOTS + group, -1))
 
 
 def repack(in_ref, pick_ref, out_ref):
@@ -209,22 +210,21 @@
     chunks = []
     gains = []
     total = jnp.zeros((SLOTS, 128), F32)
+    squares = jnp.zeros((SLOTS, 128), F32)
     for i in range(16):
         shift = jnp.where(shift_lane, shifts[:, i * 128 : i * 128 + 128], 0.0).astype(BF16)
         chunk = in_ref[i % 4, i // 4, 0:144].astype(F32) + dot_nn(shift, ones)
         total = total + chunk
+        squares = squares + chunk * chunk
         chunks.append(chunk)
         gain = jnp.where(own, gain_rows[i * 16 : i * 16 + 16], 0.0)
         gains.append(jnp.sum(gain, axis=0, keepdims=True))
     center = jnp.sum(total, axis=1, keepdims=True) / WIDTH
-    squares = jnp.zeros((SLOTS, 128), F32)
-    for i in range(16):
-        chunks[i] = chunks[i] - center
-        squares = squares + chunks[i] * chunks[i]
-    inv_scale = lax.rsqrt(jnp.sum(squares, axis=1, keepdims=True) / WIDTH + 1e-05)
+    variance = jnp.sum(squares, axis=1, keepdims=True) / WIDTH - center * center
+    inv_scale = lax.rsqrt(variance + 1e-05)
     rows = []
     for i in range(16):
-        rows.append((chunks[i] * inv_scale * gains[i]).astype(BF16))
+        rows.append(((chunks[i] - center) * inv_scale * gains[i]).astype(BF16))
     return jnp.concatenate(rows, axis=1), jnp.concatenate(gains, axis=1), center, inv_scale
 
 
@@ -416,13 +416,14 @@
     block = lax.axis_index(EXPERT).astype(jnp.int32).reshape(1)
     swap = [(0, 1), (1, 0)]
     heads_t = a2a(jnp.broadcast_to(heads_out.T, (16, 64, 128)), ("yl", "x"))
-    side = call(pack, shape((64, SIDE), BF16), "pack", 0, 4)(
-        out_weight.T, residual.T, cotangent.T, norm_gain.reshape(64, 1)
-    )
-    side = lax.all_gather(side, "c", axis=0, tiled=True)
-    place, gate, pick, drop = call(
+    wide = jnp.concatenate([out_weight.T, residual.T, cotangent.T], axis=1)
+    small = jnp.concatenate(
+        [routes.T.astype(F32), gates.T, jnp.pad(norm_gain, (0, 64)).reshape(1, 128)], axis=0
+    )
+    side, place, gate, pick, drop = call(
         prepare,
         (
+            shape((64, SIDE), BF16),
             shape((ROWS, 128), BF16),
             shape((ROWS, 128), F32),
             shape((PACK, ROWS), BF16),
@@ -431,9 +432,11 @@
         "prepare",
         1,
         2,
-    )(core, routes.T, gates.T)
+    )(core, wide, small)
+    side = lax.all_gather(side, "c", axis=0, tiled=True)
     turned = call(turn_weight, shape((16, 64, 128), BF16), "turn_weight", 1, 1)(core, side)
-    heads_t, turned = lax.optimization_barrier((heads_t, turned))
+    at = jnp.stack([lax.axis_index("x"), lax.axis_index("yl")]).astype(jnp.int32)
+    heads_t, turned, at = lax.optimization_barrier((heads_t, turned, at))
     heads_t = lax.all_gather(heads_t, "c", axis=0)
     stream, message = call(
         dispatch, (shape((128, 128), F32), shape((BLOCKS, 4, MSG, 128), BF16)), "dispatch", 1, 4
@@ -487,13 +490,11 @@
         4,
     )(core, both, stream, side, heads_t)
     grad_weight = total(a2a(grad_weight, EXPERT)).astype(BF16)
-    at = jnp.stack([lax.axis_index("x"), lax.axis_index("yl")]).astype(jnp.int32)
     keep, send = call(heads_back, (shape((2, 4, 64, 128), BF16),) * 2, "heads_back", 1, 2)(
         at, grad_pair, turned
     )
     pieces = halve(keep, send, "x")
     grad_weight = jnp.broadcast_to(grad_weight, (16, 64, 128))
-    grad_weight, pieces = lax.optimization_barrier((grad_weight, pieces))
     grad_weight = a2a(grad_weight, EXPERT)
     grad_weight = call(lay, shape((64, WIDTH), BF16), "lay", 0, 1)(grad_weight)
     heads_sum = (pieces[0] + pieces[1].astype(F32)).astype(BF16)

time: 180 us -> 179 us (level)
  the two profiles are of different devices: /device:TPU:16 before, /device:TPU:2 now
where the time goes in v4:
time: 179 us; the launch traced here: 178 us
  blocking collectives  98 us (55%)
  starting transfers between devices  40.3 us (23%)
  waiting for transfers between devices  21.7 us (12%)
  Pallas kernels  12 us (7%)
  other arithmetic  2.49 us (1%)
  local copies, waits for them, and re-layouts  2.28 us (1%)
    all_to_all x4, blocking collectives, a2a(): return lax.all_to_all(value, axes, split_axis=0, concat_axis=0, tiled=True)  91.6 us
    all_to_all x3, starting transfers between devices, a2a(): return lax.all_to_all(value, axes, split_axis=0, concat_axis=0, tiled=True)  22.7 us
    all_to_all x3, waiting for transfers between devices, a2a(): return lax.all_to_all(value, axes, split_axis=0, concat_axis=0, tiled=True)  11.5 us
    ppermute x2, starting transfers between devices, halve(): lax.ppermute(half[1].astype(BF16), axis, [(i, i ^ 2) for i in range(4)])  7.53 us
    ppermute x2, waiting for transfers between devices, halve(): lax.ppermute(half[1].astype(BF16), axis, [(i, i ^ 2) for i in range(4)])  7.15 us
    ppermute x2, starting transfers between devices, halve(): came = lax.ppermute(send, axis, [(i, i ^ 1) for i in range(4)])  6.16 us
  transfers between devices with their start and end apart: 9, of which 8 were waited for; matrix products, arithmetic and copies ran while one was open for 2% of the time, Pallas kernels for 2%

profile of v4, /device:TPU:2, one launch (start us, length us, event | category | flops | bytes accessed | tf_op | source)
XLA Modules:
  0.0 177.6 jit_solution(11673385708632149196)
XLA Ops:
  0.6 0.0 copy-start.3
  0.6 0.0 copy-start.2
  0.7 1.5 broadcast_in_dim.6
  2.1 9.2 %all-to-all-start = ((bf16[16,64,128]{2,1,0:T(8,128)(2,1)}), bf16[16,64,128]{2,1,0:T(8,128)(2,1)S(1)}, u32[]{:S(2)}, u32[]{:S(2)}) async-start(bf16[16,64,128]{2,1,0:T(8,128)(2,1)} %broadcast_in_dim.6), calls=%async_computation | async-start | bytes 524288 | tf_op jit(solution)/shard_map/all_to_all | solution.py:398
  11.4 0.7 convert_bitcast_fusion
  12.0 1.0 pad_maximum_fusion.wide_ref
  13.1 0.0 copy-done.3
  13.1 0.0 copy-done.2
  13.1 0.4 prepare.1
  13.5 2.3 %all_gather.15.side_ref = bf16[128,2432]{1,0:T(8,128)(2,1)S(1)} all-gather(bf16[64,2432]{1,0:T(8,128)(2,1)S(1)} %get-tuple-element.26), channel_id=1, replica_groups=mesh['yh'=2,'z'=8,'yl'=4,'x'=4,'c'=2] {'c'}, dimensions={0}, use_global_device_ids=true | all-gather | bytes 933888 | tf_op jit(solution)/shard_map/all_gather | solution.py:436
  15.8 0.5 turn_weight.1.weight_ref
  16.2 0.1 pad_add_fusion.at_ref
  16.3 3.8 %all-to-all-done = bf16[16,64,128]{2,1,0:T(8,128)(2,1)S(1)} async-done(((bf16[16,64,128]{2,1,0:T(8,128)(2,1)}), bf16[16,64,128]{2,1,0:T(8,128)(2,1)S(1)}, u32[]{:S(2)}, u32[]{:S(2)}) %all-to-all-start) | async-done | bytes 262176 | tf_op jit(solution)/shard_map/all_to_all | solution.py:398
  20.1 2.2 %all-gather = bf16[32,64,128]{2,1,0:T(8,128)(2,1)S(1)} all-gather(bf16[16,64,128]{2,1,0:T(8,128)(2,1)S(1)} %all-to-all-done), channel_id=2, replica_groups=mesh['yh'=2,'z'=8,'yl'=4,'x'=4,'c'=2] {'c'}, dimensions={0}, use_global_device_ids=true | all-gather | bytes 786432 | tf_op jit(solution)/shard_map/all_gather | solution.py:440
  22.2 0.7 dispatch.1
  22.9 30.9 %all_to_all.35 = bf16[64,24,128]{2,1,0:T(8,128)(2,1)S(1)} all-to-all(bf16[64,24,128]{2,1,0:T(8,128)(2,1)S(1)} %bitcast.48), channel_id=1, replica_groups=mesh['yh'=2,'z'=8,'yl'=4,'x'=4,'c'=2] {'yh','z','yl'}, dimensions={0} | all-to-all | bytes 786432 | tf_op jit(solution)/shard_map/all_to_all | solution.py:398
  53.8 0.0 copy-start.1
  53.8 0.5 repack.1
  54.3 0.0 copy-start
  54.3 18.1 %all_to_all.36.in_ref = bf16[4,4,304,128]{3,2,1,0:T(8,128)(2,1)S(1)} all-to-all(bf16[4,4,304,128]{3,2,1,0:T(8,128)(2,1)S(1)} %repack.1), channel_id=1, replica_groups=mesh['yh'=2,'z'=8,'yl'=4,'x'=4,'c'=2] {'x'}, dimensions={0} | all-to-all | bytes 2490368 | tf_op jit(solution)/shard_map/all_to_all | solution.py:398
  72.4 1.9 %collective-permute-start = (bf16[4,4,304,128]{3,2,1,0:T(8,128)(2,1)S(1)}, bf16[4,4,304,128]{3,2,1,0:T(8,128)(2,1)S(1)}, u32[]{:S(2)}, u32[]{:S(2)}) collective-permute-start(bf16[4,4,304,128]{3,2,1,0:T(8,128)(2,1)S(1)} %all_to_all.36.in_ref), channel_id=1, source_target_pairs={{0,1},{1,0},{2,3},{3,2},{4,5},{5,4},{6,7},{7,6},{8,9},{9,8},{10,11... | collective-permute-start | bytes 3735560 | tf_op jit(solution)/shard_map/ppermute | solution.py:449
  74.3 0.0 copy-done.1
  74.3 0.0 copy-done
  74.3 1.6 only_ahead.1
  75.9 1.3 collective-permute-done.in_ref
  77.2 2.6 %both_ways.1 = bf16[4,4,304,128]{3,2,1,0:T(8,128)(2,1)S(1)} custom-call(s32[1]{0:T(128)S(6)} %sub.3.which_ref, bf16[4,4,304,128]{3,2,1,0:T(8,128)(2,1)S(1)} %collective-permute-done.in_ref, bf16[2,2048,256]{2,1,0:T(8,128)(2,1)S(1)} %copy-done, bf16[2,256,2048]{2,1,0:T(8,128)(2,1)S(1)} %copy-done.1), custom_call_target="tpu_custom_call" | custom-call | tf_op jit(solution)/shard_map/both_ways/pallas_call | solution.py:462
  79.8 2.0 %collective-permute-start.1 = (bf16[4,4,304,128]{3,2,1,0:T(8,128)(2,1)S(1)}, bf16[4,4,304,128]{3,2,1,0:T(8,128)(2,1)S(1)}, u32[]{:S(2)}, u32[]{:S(2)}) collective-permute-start(bf16[4,4,304,128]{3,2,1,0:T(8,128)(2,1)S(1)} %both_ways.1), channel_id=1, source_target_pairs={{0,1},{1,0},{2,3},{3,2},{4,5},{5,4},{6,7},{7,6},{8,9},{9,8},{10,11... | collective-permute-start | bytes 3735560 | tf_op jit(solution)/shard_map/ppermute | solution.py:466
  81.9 1.5 only_behind.1.grad_ref
  83.4 1.2 collective-permute-done.1.came_ref
  84.7 0.3 add_pair.1
  85.0 20.2 %all_to_all.37.in_ref = bf16[4,4,304,128]{3,2,1,0:T(8,128)(2,1)S(1)} all-to-all(bf16[4,4,304,128]{3,2,1,0:T(8,128)(2,1)S(1)} %add_pair.1), channel_id=1, replica_groups=mesh['yh'=2,'z'=8,'yl'=4,'x'=4,'c'=2] {'x'}, dimensions={0} | all-to-all | bytes 2490368 | tf_op jit(solution)/shard_map/all_to_all | solution.py:398
  105.2 0.5 add_four.1
  105.7 22.4 %all_to_all.38 = bf16[64,24,128]{2,1,0:T(8,128)(2,1)S(1)} all-to-all(bf16[64,24,128]{2,1,0:T(8,128)(2,1)S(1)} %bitcast.46), channel_id=1, replica_groups=mesh['yh'=2,'z'=8,'yl'=4,'x'=4,'c'=2] {'yh','z','yl'}, dimensions={0} | all-to-all | bytes 786432 | tf_op jit(solution)/shard_map/all_to_all | solution.py:398
  128.2 0.5 combine.1
  128.7 2.0 %all-gather.1 = f32[528,128]{1,0:T(8,128)S(1)} all-gather(f32[264,128]{1,0:T(8,128)S(1)} %combine.1), channel_id=3, replica_groups=mesh['yh'=2,'z'=8,'yl'=4,'x'=4,'c'=2] {'c'}, dimensions={0}, use_global_device_ids=true | all-gather | bytes 405504 | tf_op jit(solution)/shard_map/all_gather | solution.py:479
  130.7 1.3 finish.1
  132.0 0.8 heads_back.1
  132.8 3.4 %collective-permute-start.2 = (bf16[2,4,64,128]{3,2,1,0:T(8,128)(2,1)S(1)}, bf16[2,4,64,128]{3,2,1,0:T(8,128)(2,1)S(1)}, u32[]{:S(2)}, u32[]{:S(2)}) collective-permute-start(bf16[2,4,64,128]{3,2,1,0:T(8,128)(2,1)S(1)} %get-tuple-element.46), channel_id=1, source_target_pairs={{0,2},{2,0},{4,6},{6,4},{1,3},{3,1},{5,7},{7,5},{8,10},{10,8},{12,... | collective-permute-start | bytes 393224 | tf_op jit(solution)/shard_map/ppermute | solution.py:402
  136.2 3.5 %all-to-all-start.5 = ((bf16[16,64,128]{2,1,0:T(8,128)(2,1)}), bf16[16,64,128]{2,1,0:T(8,128)(2,1)S(1)}, u32[]{:S(2)}, u32[]{:S(2)}) async-start(bf16[16,64,128]{2,1,0:T(8,128)(2,1)} %get-tuple-element.47), calls=%async_computation.5 | async-start | bytes 524288 | tf_op jit(solution)/shard_map/all_to_all | solution.py:398
  139.7 0.5 collective-permute-done.2
  140.3 3.4 %collective-permute-start.3 = (bf16[4,64,128]{2,1,0:T(8,128)(2,1)S(1)}, bf16[4,64,128]{2,1,0:T(8,128)(2,1)S(1)}, u32[]{:S(2)}, u32[]{:S(2)}) collective-permute-start(bf16[4,64,128]{2,1,0:T(8,128)(2,1)S(1)} %fusion.2), channel_id=1, source_target_pairs={{0,4},{2,6},{4,0},{6,2},{1,5},{3,7},{5,1},{7,3},{8,12},{10,14},{12... | collective-permute-start | bytes 196616 | tf_op jit(solution)/shard_map/ppermute | solution.py:404
  143.7 4.3 %collective-permute-done.3 = bf16[4,64,128]{2,1,0:T(8,128)(2,1)S(1)} collective-permute-done((bf16[4,64,128]{2,1,0:T(8,128)(2,1)S(1)}, bf16[4,64,128]{2,1,0:T(8,128)(2,1)S(1)}, u32[]{:S(2)}, u32[]{:S(2)}) %collective-permute-start.3) | collective-permute-done | bytes 65568 | tf_op jit(solution)/shard_map/ppermute | solution.py:404
  148.0 2.8 %collective-permute-start.4 = (bf16[2,64,128]{2,1,0:T(8,128)(2,1)S(1)}, bf16[2,64,128]{2,1,0:T(8,128)(2,1)S(1)}, u32[]{:S(2)}, u32[]{:S(2)}) collective-permute-start(bf16[2,64,128]{2,1,0:T(8,128)(2,1)S(1)} %slice.29), channel_id=1, source_target_pairs={{0,8},{8,0},{16,24},{24,16},{1,9},{9,1},{17,25},{25,17},{2,10},{10... | collective-permute-start | bytes 98312 | tf_op jit(solution)/shard_map/ppermute | solution.py:402
  150.8 1.9 %all-to-all-done.5 = bf16[16,64,128]{2,1,0:T(8,128)(2,1)S(1)} async-done(((bf16[16,64,128]{2,1,0:T(8,128)(2,1)}), bf16[16,64,128]{2,1,0:T(8,128)(2,1)S(1)}, u32[]{:S(2)}, u32[]{:S(2)}) %all-to-all-start.5) | async-done | bytes 262176 | tf_op jit(solution)/shard_map/all_to_all | solution.py:398
  152.7 0.8 broadcast_in_dim.7
  153.5 9.9 %all-to-all-start.6 = ((bf16[16,64,128]{2,1,0:T(8,128)(2,1)}), bf16[16,64,128]{2,1,0:T(8,128)(2,1)S(1)}, u32[]{:S(2)}, u32[]{:S(2)}) async-start(bf16[16,64,128]{2,1,0:T(8,128)(2,1)} %broadcast_in_dim.7), calls=%async_computation.6 | async-start | bytes 524288 | tf_op jit(solution)/shard_map/all_to_all | solution.py:398
  163.4 0.0 collective-permute-done.4
  163.4 4.2 %collective-permute-start.5 = (bf16[64,128]{1,0:T(8,128)(2,1)S(1)}, bf16[64,128]{1,0:T(8,128)(2,1)S(1)}, u32[]{:S(2)}, u32[]{:S(2)}) collective-permute-start(bf16[64,128]{1,0:T(8,128)(2,1)S(1)} %fusion.6), channel_id=1, source_target_pairs={{0,16},{8,24},{16,0},{24,8},{1,17},{9,25},{17,1},{25,9},{2,18},{10... | collective-permute-start | bytes 49160 | tf_op jit(solution)/shard_map/ppermute | solution.py:404
  167.6 2.9 %collective-permute-done.5 = bf16[64,128]{1,0:T(8,128)(2,1)S(1)} collective-permute-done((bf16[64,128]{1,0:T(8,128)(2,1)S(1)}, bf16[64,128]{1,0:T(8,128)(2,1)S(1)}, u32[]{:S(2)}, u32[]{:S(2)}) %collective-permute-start.5) | collective-permute-done | bytes 16416 | tf_op jit(solution)/shard_map/ppermute | solution.py:404
  170.5 0.6 fusion.5
  171.1 5.8 %all-to-all-done.6.in_ref = bf16[16,64,128]{2,1,0:T(8,128)(2,1)S(1)} async-done(((bf16[16,64,128]{2,1,0:T(8,128)(2,1)}), bf16[16,64,128]{2,1,0:T(8,128)(2,1)S(1)}, u32[]{:S(2)}, u32[]{:S(2)}) %all-to-all-start.6) | async-done | bytes 262176 | tf_op jit(solution)/shard_map/all_to_all | solution.py:398
  176.9 0.8 lay.1
  (9 shorter events, 0.1 us)
Async XLA Ops:
  0.6 12.4 %copy-start.3 = (f32[64]{0:T(128)S(1)}, f32[64]{0:T(128)}, u32[]{:S(2)}) copy-start(f32[64]{0:T(128)} %param.12) | copy-start | bytes 772
  0.6 12.4 %copy-start.2 = (f32[128,2]{0,1:T(2,128)S(1)}, f32[128,2]{0,1:T(2,128)}, u32[]{:S(2)}) copy-start(f32[128,2]{0,1:T(2,128)} %param.16) | copy-start | bytes 3076
  2.1 17.9 %all-to-all-start = ((bf16[16,64,128]{2,1,0:T(8,128)(2,1)}), bf16[16,64,128]{2,1,0:T(8,128)(2,1)S(1)}, u32[]{:S(2)}, u32[]{:S(2)}) async-start(bf16[16,64,128]{2,1,0:T(8,128)(2,1)} %broadcast_in_dim.6), calls=%async_computation | async-start | bytes 524288 | tf_op jit(solution)/shard_map/all_to_all | solution.py:398
  53.8 20.5 %copy-start.1 = (bf16[2,256,2048]{2,1,0:T(8,128)(2,1)S(1)}, bf16[2,256,2048]{2,1,0:T(8,128)(2,1)}, u32[]{:S(2)}) copy-start(bf16[2,256,2048]{2,1,0:T(8,128)(2,1)} %down_ref.5) | copy-start | bytes 6291460
  54.3 20.0 %copy-start = (bf16[2,2048,256]{2,1,0:T(8,128)(2,1)S(1)}, bf16[2,2048,256]{2,1,0:T(8,128)(2,1)}, u32[]{:S(2)}) copy-start(bf16[2,2048,256]{2,1,0:T(8,128)(2,1)} %up_ref.5) | copy-start | bytes 6291460
  72.4 4.8 %collective-permute-start = (bf16[4,4,304,128]{3,2,1,0:T(8,128)(2,1)S(1)}, bf16[4,4,304,128]{3,2,1,0:T(8,128)(2,1)S(1)}, u32[]{:S(2)}, u32[]{:S(2)}) collective-permute-start(bf16[4,4,304,128]{3,2,1,0:T(8,128)(2,1)S(1)} %all_to_all.36.in_ref), channel_id=1, source_target_pairs={{0,1},{1,0},{2,3},{3,2},{4,5},{5,4},{6,7},{7,6},{8,9},{9,8},{10,11... | collective-permute-start | bytes 3735560 | tf_op jit(solution)/shard_map/ppermute | solution.py:449
  79.8 4.8 %collective-permute-start.1 = (bf16[4,4,304,128]{3,2,1,0:T(8,128)(2,1)S(1)}, bf16[4,4,304,128]{3,2,1,0:T(8,128)(2,1)S(1)}, u32[]{:S(2)}, u32[]{:S(2)}) collective-permute-start(bf16[4,4,304,128]{3,2,1,0:T(8,128)(2,1)S(1)} %both_ways.1), channel_id=1, source_target_pairs={{0,1},{1,0},{2,3},{3,2},{4,5},{5,4},{6,7},{7,6},{8,9},{9,8},{10,11... | collective-permute-start | bytes 3735560 | tf_op jit(solution)/shard_map/ppermute | solution.py:466
  132.8 7.4 %collective-permute-start.2 = (bf16[2,4,64,128]{3,2,1,0:T(8,128)(2,1)S(1)}, bf16[2,4,64,128]{3,2,1,0:T(8,128)(2,1)S(1)}, u32[]{:S(2)}, u32[]{:S(2)}) collective-permute-start(bf16[2,4,64,128]{3,2,1,0:T(8,128)(2,1)S(1)} %get-tuple-element.46), channel_id=1, source_target_pairs={{0,2},{2,0},{4,6},{6,4},{1,3},{3,1},{5,7},{7,5},{8,10},{10,8},{12,... | collective-permute-start | bytes 393224 | tf_op jit(solution)/shard_map/ppermute | solution.py:402
  136.2 16.5 %all-to-all-start.5 = ((bf16[16,64,128]{2,1,0:T(8,128)(2,1)}), bf16[16,64,128]{2,1,0:T(8,128)(2,1)S(1)}, u32[]{:S(2)}, u32[]{:S(2)}) async-start(bf16[16,64,128]{2,1,0:T(8,128)(2,1)} %get-tuple-element.47), calls=%async_computation.5 | async-start | bytes 524288 | tf_op jit(solution)/shard_map/all_to_all | solution.py:398
  140.3 7.7 %collective-permute-start.3 = (bf16[4,64,128]{2,1,0:T(8,128)(2,1)S(1)}, bf16[4,64,128]{2,1,0:T(8,128)(2,1)S(1)}, u32[]{:S(2)}, u32[]{:S(2)}) collective-permute-start(bf16[4,64,128]{2,1,0:T(8,128)(2,1)S(1)} %fusion.2), channel_id=1, source_target_pairs={{0,4},{2,6},{4,0},{6,2},{1,5},{3,7},{5,1},{7,3},{8,12},{10,14},{12... | collective-permute-start | bytes 196616 | tf_op jit(solution)/shard_map/ppermute | solution.py:404
  148.0 15.4 %collective-permute-start.4 = (bf16[2,64,128]{2,1,0:T(8,128)(2,1)S(1)}, bf16[2,64,128]{2,1,0:T(8,128)(2,1)S(1)}, u32[]{:S(2)}, u32[]{:S(2)}) collective-permute-start(bf16[2,64,128]{2,1,0:T(8,128)(2,1)S(1)} %slice.29), channel_id=1, source_target_pairs={{0,8},{8,0},{16,24},{24,16},{1,9},{9,1},{17,25},{25,17},{2,10},{10... | collective-permute-start | bytes 98312 | tf_op jit(solution)/shard_map/ppermute | solution.py:402
  153.5 23.4 %all-to-all-start.6 = ((bf16[16,64,128]{2,1,0:T(8,128)(2,1)}), bf16[16,64,128]{2,1,0:T(8,128)(2,1)S(1)}, u32[]{:S(2)}, u32[]{:S(2)}) async-start(bf16[16,64,128]{2,1,0:T(8,128)(2,1)} %broadcast_in_dim.7), calls=%async_computation.6 | async-start | bytes 524288 | tf_op jit(solution)/shard_map/all_to_all | solution.py:398
  163.4 7.0 %collective-permute-start.5 = (bf16[64,128]{1,0:T(8,128)(2,1)S(1)}, bf16[64,128]{1,0:T(8,128)(2,1)S(1)}, u32[]{:S(2)}, u32[]{:S(2)}) collective-permute-start(bf16[64,128]{1,0:T(8,128)(2,1)S(1)} %fusion.6), channel_id=1, source_target_pairs={{0,16},{8,24},{16,0},{24,8},{1,17},{9,25},{17,1},{25,9},{2,18},{10... | collective-permute-start | bytes 49160 | tf_op jit(solution)/shard_map/ppermute | solution.py:404

commit v5 on v4

--- a/solution.py
+++ b/solution.py
@@ -11,7 +11,7 @@
 SPLIT = (2, 8, 4, 4, 2)
 BLOCKS = 16
 CAP = 9
-MSG = 24
+MSG = 20
 ORDER = (0, 2, 1, 3)
 PACK = 304
 SLOTS = BLOCKS * CAP
@@ -90,6 +90,29 @@
     return jnp.where(lane < 64, high.astype(F32), low.astype(F32)).astype(BF16)
 
 
+def row_place(row):
+    return row & 15, lax.shift_right_logical(row, 4)
+
+
+def write_messages(out_ref, value, ways):
+    for i in range(MSG // 2):
+        at = i * 32
+        pair = jnp.stack([value[at : at + 16], value[at + 16 : at + 32]], axis=1).astype(BF16)
+        for y in ways:
+            out_ref[:, y, :, i * 128 : i * 128 + 128] = pair
+
+
+def read_messages(in_ref, ways):
+    rows = []
+    for i in range(MSG // 2):
+        pair = None
+        for y in ways:
+            came = in_ref[:, y, :, i * 128 : i * 128 + 128].astype(F32)
+            pair = came if pair is None else pair + came
+        rows.extend([pair[:, 0], pair[:, 1]])
+    return jnp.concatenate(rows, axis=0)
+
+
 def prepare(
     core_ref, wide_ref, small_ref, side_ref, place_ref, gate_ref, pick_ref, drop_ref
 ):
@@ -102,8 +125,7 @@
     gates = small_ref[2:4]
     core = core_ref[0]
     row = iota((ROWS, 128), 0)
-    group = div(row, MSG)
-    local = row - group * MSG
+    group, local = row_place(row)
     slot = jnp.where(local < CAP, local, local - CAP)
     used = local < 2 * CAP
     expert = 2 * group + core
@@ -149,15 +171,13 @@
     shift_col = jnp.sum(placed * shift, axis=1, keepdims=True)
     row = iota((ROWS, 128), 0)
     lane = iota((ROWS, 128), 1)
-    local = row - div(row, MSG) * MSG
+    local = row_place(row)[1]
     high, low = split_two(shift_col)
     spread = jnp.where(lane == local, high.astype(F32), 0.0)
     spread = spread + jnp.where(lane == local + 16, low.astype(F32), 0.0)
     spread = jnp.where(local < CAP, spread, 0.0).astype(BF16)
-    to = iota((ROWS, ROWS), 0)
-    come = iota((ROWS, ROWS), 1)
-    to_group = div(to, MSG)
-    gather = (to - to_group * MSG == 18) & (to_group == div(come, MSG))
+    to_group, to_local = row_place(iota((ROWS, ROWS), 0))
+    gather = (to_local == 18) & (to_group == row_place(iota((ROWS, ROWS), 1))[0])
     stats = dot_nn(jnp.where(gather, 1.0, 0.0).astype(BF16), spread)
     feature = iota((128, 128), 0)
     at = iota((128, 128), 1) - 32
@@ -168,15 +188,11 @@
     gain = jnp.sum(jnp.where(mine, gain, 0.0), axis=0, keepdims=True)
     value = jnp.where(local < CAP, rows_x, jnp.where(local < 2 * CAP, rows_c * gate_col, stats))
     value = jnp.where(local == 18, value + gain, value)
-    for e in range(BLOCKS):
-        piece = value[e * MSG : (e + 1) * MSG].astype(BF16)
-        for y in range(4):
-            out_ref[e, y] = piece
+    write_messages(out_ref, value, range(4))
 
 
 def packed_row(come):
-    group = div(come, MSG)
-    local = come - group * MSG
+    group, local = row_place(come)
     to = jnp.where(local < CAP, group * CAP + local, SLOTS + group * CAP + local - CAP)
     return jnp.where(local < 2 * CAP, to, jnp.where(local == 18, 2 * SLOTS + group, -1))
 
@@ -184,7 +200,7 @@
 def repack(in_ref, pick_ref, out_ref):
     pick = pick_ref[...]
     for y in range(4):
-        rows = in_ref[:, y].astype(F32).reshape(ROWS, 128).astype(BF16)
+        rows = read_messages(in_ref, (y,)).astype(BF16)
         packed = dot_nn(pick, rows).astype(BF16)
         for x in range(4):
             out_ref[x, y] = packed
@@ -213,7 +229,9 @@
     squares = jnp.zeros((SLOTS, 128), F32)
     for i in range(16):
         shift = jnp.where(shift_lane, shifts[:, i * 128 : i * 128 + 128], 0.0).astype(BF16)
-        chunk = in_ref[i % 4, i // 4, 0:144].astype(F32) + dot_nn(shift, ones)
+        shift = dot_nn(shift, ones)
+        base = shift if i == 0 else base
+        chunk = in_ref[i % 4, i // 4, 0:144].astype(F32) + (shift - base)
         total = total + chunk
         squares = squares + chunk * chunk
         chunks.append(chunk)
@@ -225,6 +243,7 @@
     rows = []
     for i in range(16):
         rows.append(((chunks[i] - center) * inv_scale * gains[i]).astype(BF16))
+    center = center + base[:, 0:1]
     return jnp.concatenate(rows, axis=1), jnp.concatenate(gains, axis=1), center, inv_scale
 
 
@@ -327,22 +346,16 @@
         for x in range(1, 4):
             value = value + in_ref[x, y].astype(F32)
         rows = jnp.concatenate([value[0:288].astype(BF16), part(join(value[288:304]))], axis=0)
-        message = dot_nn(drop, rows)
-        for e in range(BLOCKS):
-            out_ref[e, y] = message[e * MSG : (e + 1) * MSG].astype(BF16)
+        write_messages(out_ref, dot_nn(drop, rows), (y,))
 
 
 def combine(in_ref, place_ref, gate_ref, out_ref):
-    value = in_ref[:, 0].astype(F32)
-    for y in range(1, 4):
-        value = value + in_ref[:, y].astype(F32)
-    stats = value[:, 18]
-    stats = join(stats).reshape(BLOCKS, 1, 128)
-    stats = jnp.broadcast_to(stats, (BLOCKS, MSG, 128)).reshape(ROWS, 128)
-    value = value.reshape(ROWS, 128).astype(BF16)
+    value = read_messages(in_ref, range(4))
+    stats = jnp.concatenate([join(value[288:304])] * MSG, axis=0)
+    value = value.astype(BF16)
     row = iota((ROWS, 128), 0)
     lane = iota((ROWS, 128), 1)
-    local = row - div(row, MSG) * MSG
+    local = row_place(row)[1]
     forward = local < CAP
     place = place_ref[...].astype(F32)
     ahead_place = jnp.where(forward, place, 0.0)
@@ -439,11 +452,11 @@
     heads_t, turned, at = lax.optimization_barrier((heads_t, turned, at))
     heads_t = lax.all_gather(heads_t, "c", axis=0)
     stream, message = call(
-        dispatch, (shape((128, 128), F32), shape((BLOCKS, 4, MSG, 128), BF16)), "dispatch", 1, 4
+        dispatch, (shape((128, 128), F32), shape((BLOCKS, 4, 2, MSG * 64), BF16)), "dispatch", 1, 4
     )(block, heads_t, side, place, gate)
-    message = a2a(message.reshape(64, MSG, 128), ("yh", "z", "yl"))
+    message = a2a(message.reshape(64, 2, MSG * 64), ("yh", "z", "yl"))
     packed = call(repack, shape((4, 4, PACK, 128), BF16), "repack", 0, 2)(
-        message.reshape(BLOCKS, 4, MSG, 128), pick
+        message.reshape(BLOCKS, 4, 2, MSG * 64), pick
     )
     mine = a2a(packed, "x")
     other = lax.ppermute(mine, "c", swap)
@@ -469,12 +482,12 @@
     )
     summed = call(add_pair, shape((4, 4, PACK, 128), BF16), "add_pair", 0, 3)(value, grad, came)
     summed = a2a(summed, "x")
-    message = call(add_four, shape((BLOCKS, 4, MSG, 128), BF16), "add_four", 0, 2)(
+    message = call(add_four, shape((BLOCKS, 4, 2, MSG * 64), BF16), "add_four", 0, 2)(
         summed, drop
     )
-    message = a2a(message.reshape(64, MSG, 128), ("yh", "z", "yl"))
+    message = a2a(message.reshape(64, 2, MSG * 64), ("yh", "z", "yl"))
     both = call(combine, shape((264, 128), F32), "combine", 0, 3)(
-        message.reshape(BLOCKS, 4, MSG, 128), place, gate
+        message.reshape(BLOCKS, 4, 2, MSG * 64), place, gate
     )
     both = lax.all_gather(both, "c", axis=0)
     result, grad_residual, grad_pair, grad_weight = call(

time: 179 us -> 177 us (0.989)
  blocking collectives: 98 us -> 95.3 us
    all_to_all x4, blocking collectives: 91.6 us -> 88.9 us  [a2a(): return lax.all_to_all(value, axes, split_axis=0, concat_axis=0, tiled=True)]
where the time goes in v5:
time: 177 us; the launch traced here: 176 us
  blocking collectives  95.3 us (54%)
  starting transfers between devices  40.6 us (23%)
  waiting for transfers between devices  21.4 us (12%)
  Pallas kernels  12.9 us (7%)
  other arithmetic  2.49 us (1%)
  local copies, waits for them, and re-layouts  2.28 us (1%)
    all_to_all x4, blocking collectives, a2a(): return lax.all_to_all(value, axes, split_axis=0, concat_axis=0, tiled=True)  88.9 us
    all_to_all x3, starting transfers between devices, a2a(): return lax.all_to_all(value, axes, split_axis=0, concat_axis=0, tiled=True)  22.7 us
    all_to_all x3, waiting for transfers between devices, a2a(): return lax.all_to_all(value, axes, split_axis=0, concat_axis=0, tiled=True)  11.3 us
    ppermute x2, starting transfers between devices, halve(): lax.ppermute(half[1].astype(BF16), axis, [(i, i ^ 2) for i in range(4)])  7.36 us
    ppermute x2, waiting for transfers between devices, halve(): lax.ppermute(half[1].astype(BF16), axis, [(i, i ^ 2) for i in range(4)])  7.11 us
    ppermute x2, starting transfers between devices, halve(): came = lax.ppermute(send, axis, [(i, i ^ 1) for i in range(4)])  6.54 us
  transfers between devices with their start and end apart: 9, of which 8 were waited for; matrix products, arithmetic and copies ran while one was open for 2% of the time, Pallas kernels for 2%

profile of v5, /device:TPU:2, one launch (start us, length us, event | category | flops | bytes accessed | tf_op | source)
XLA Modules:
  0.0 175.9 jit_solution(805614926750410853)
XLA Ops:
  0.6 0.0 copy-start.3
  0.6 0.0 copy-start.2
  0.7 1.5 broadcast_in_dim.6
  2.1 9.2 %all-to-all-start = ((bf16[16,64,128]{2,1,0:T(8,128)(2,1)}), bf16[16,64,128]{2,1,0:T(8,128)(2,1)S(1)}, u32[]{:S(2)}, u32[]{:S(2)}) async-start(bf16[16,64,128]{2,1,0:T(8,128)(2,1)} %broadcast_in_dim.6), calls=%async_computation | async-start | bytes 524288 | tf_op jit(solution)/shard_map/all_to_all | solution.py:411
  11.4 0.7 convert_bitcast_fusion
  12.0 1.0 pad_maximum_fusion.wide_ref
  13.1 0.0 copy-done.3
  13.1 0.0 copy-done.2
  13.1 0.2 prepare.1
  13.4 2.3 %all_gather.15.side_ref = bf16[128,2432]{1,0:T(8,128)(2,1)S(1)} all-gather(bf16[64,2432]{1,0:T(8,128)(2,1)S(1)} %get-tuple-element.26), channel_id=1, replica_groups=mesh['yh'=2,'z'=8,'yl'=4,'x'=4,'c'=2] {'c'}, dimensions={0}, use_global_device_ids=true | all-gather | bytes 933888 | tf_op jit(solution)/shard_map/all_gather | solution.py:449
  15.6 0.5 turn_weight.1.weight_ref
  16.1 0.1 pad_add_fusion.at_ref
  16.2 3.9 %all-to-all-done = bf16[16,64,128]{2,1,0:T(8,128)(2,1)S(1)} async-done(((bf16[16,64,128]{2,1,0:T(8,128)(2,1)}), bf16[16,64,128]{2,1,0:T(8,128)(2,1)S(1)}, u32[]{:S(2)}, u32[]{:S(2)}) %all-to-all-start) | async-done | bytes 262176 | tf_op jit(solution)/shard_map/all_to_all | solution.py:411
  20.1 2.2 %all-gather = bf16[32,64,128]{2,1,0:T(8,128)(2,1)S(1)} all-gather(bf16[16,64,128]{2,1,0:T(8,128)(2,1)S(1)} %all-to-all-done), channel_id=2, replica_groups=mesh['yh'=2,'z'=8,'yl'=4,'x'=4,'c'=2] {'c'}, dimensions={0}, use_global_device_ids=true | all-gather | bytes 786432 | tf_op jit(solution)/shard_map/all_gather | solution.py:453
  22.2 0.7 dispatch.1
  23.0 29.5 %all_to_all.35 = bf16[64,2,1280]{2,1,0:T(2,128)(2,1)S(1)} all-to-all(bf16[64,2,1280]{2,1,0:T(2,128)(2,1)S(1)} %bitcast.48), channel_id=1, replica_groups=mesh['yh'=2,'z'=8,'yl'=4,'x'=4,'c'=2] {'yh','z','yl'}, dimensions={0} | all-to-all | bytes 655360 | tf_op jit(solution)/shard_map/all_to_all | solution.py:411
  52.5 0.0 copy-start.1
  52.5 0.9 repack.1
  53.4 0.0 copy-start
  53.5 18.0 %all_to_all.36.in_ref = bf16[4,4,304,128]{3,2,1,0:T(8,128)(2,1)S(1)} all-to-all(bf16[4,4,304,128]{3,2,1,0:T(8,128)(2,1)S(1)} %repack.1), channel_id=1, replica_groups=mesh['yh'=2,'z'=8,'yl'=4,'x'=4,'c'=2] {'x'}, dimensions={0} | all-to-all | bytes 2490368 | tf_op jit(solution)/shard_map/all_to_all | solution.py:411
  71.5 1.9 %collective-permute-start = (bf16[4,4,304,128]{3,2,1,0:T(8,128)(2,1)S(1)}, bf16[4,4,304,128]{3,2,1,0:T(8,128)(2,1)S(1)}, u32[]{:S(2)}, u32[]{:S(2)}) collective-permute-start(bf16[4,4,304,128]{3,2,1,0:T(8,128)(2,1)S(1)} %all_to_all.36.in_ref), channel_id=1, source_target_pairs={{0,1},{1,0},{2,3},{3,2},{4,5},{5,4},{6,7},{7,6},{8,9},{9,8},{10,11... | collective-permute-start | bytes 3735560 | tf_op jit(solution)/shard_map/ppermute | solution.py:462
  73.4 0.0 copy-done.1
  73.4 0.0 copy-done
  73.4 1.6 only_ahead.1
  75.1 1.3 collective-permute-done.in_ref
  76.3 2.7 %both_ways.1 = bf16[4,4,304,128]{3,2,1,0:T(8,128)(2,1)S(1)} custom-call(s32[1]{0:T(128)S(6)} %sub.3.which_ref, bf16[4,4,304,128]{3,2,1,0:T(8,128)(2,1)S(1)} %collective-permute-done.in_ref, bf16[2,2048,256]{2,1,0:T(8,128)(2,1)S(1)} %copy-done, bf16[2,256,2048]{2,1,0:T(8,128)(2,1)S(1)} %copy-done.1), custom_call_target="tpu_custom_call" | custom-call | tf_op jit(solution)/shard_map/both_ways/pallas_call | solution.py:475
  79.0 2.0 %collective-permute-start.1 = (bf16[4,4,304,128]{3,2,1,0:T(8,128)(2,1)S(1)}, bf16[4,4,304,128]{3,2,1,0:T(8,128)(2,1)S(1)}, u32[]{:S(2)}, u32[]{:S(2)}) collective-permute-start(bf16[4,4,304,128]{3,2,1,0:T(8,128)(2,1)S(1)} %both_ways.1), channel_id=1, source_target_pairs={{0,1},{1,0},{2,3},{3,2},{4,5},{5,4},{6,7},{7,6},{8,9},{9,8},{10,11... | collective-permute-start | bytes 3735560 | tf_op jit(solution)/shard_map/ppermute | solution.py:479
  81.0 1.5 only_behind.1.grad_ref
  82.6 1.2 collective-permute-done.1.came_ref
  83.8 0.3 add_pair.1
  84.2 20.2 %all_to_all.37.in_ref = bf16[4,4,304,128]{3,2,1,0:T(8,128)(2,1)S(1)} all-to-all(bf16[4,4,304,128]{3,2,1,0:T(8,128)(2,1)S(1)} %add_pair.1), channel_id=1, replica_groups=mesh['yh'=2,'z'=8,'yl'=4,'x'=4,'c'=2] {'x'}, dimensions={0} | all-to-all | bytes 2490368 | tf_op jit(solution)/shard_map/all_to_all | solution.py:411
  104.4 0.8 add_four.1
  105.2 21.2 %all_to_all.38 = bf16[64,2,1280]{2,1,0:T(2,128)(2,1)S(1)} all-to-all(bf16[64,2,1280]{2,1,0:T(2,128)(2,1)S(1)} %bitcast.45), channel_id=1, replica_groups=mesh['yh'=2,'z'=8,'yl'=4,'x'=4,'c'=2] {'yh','z','yl'}, dimensions={0} | all-to-all | bytes 655360 | tf_op jit(solution)/shard_map/all_to_all | solution.py:411
  126.4 0.7 combine.1
  127.0 2.0 %all-gather.1 = f32[528,128]{1,0:T(8,128)S(1)} all-gather(f32[264,128]{1,0:T(8,128)S(1)} %combine.1), channel_id=3, replica_groups=mesh['yh'=2,'z'=8,'yl'=4,'x'=4,'c'=2] {'c'}, dimensions={0}, use_global_device_ids=true | all-gather | bytes 405504 | tf_op jit(solution)/shard_map/all_gather | solution.py:492
  129.0 1.3 finish.1
  130.3 0.8 heads_back.1
  131.1 3.4 %collective-permute-start.2 = (bf16[2,4,64,128]{3,2,1,0:T(8,128)(2,1)S(1)}, bf16[2,4,64,128]{3,2,1,0:T(8,128)(2,1)S(1)}, u32[]{:S(2)}, u32[]{:S(2)}) collective-permute-start(bf16[2,4,64,128]{3,2,1,0:T(8,128)(2,1)S(1)} %get-tuple-element.46), channel_id=1, source_target_pairs={{0,2},{2,0},{4,6},{6,4},{1,3},{3,1},{5,7},{7,5},{8,10},{10,8},{12,... | collective-permute-start | bytes 393224 | tf_op jit(solution)/shard_map/ppermute | solution.py:415
  134.5 3.5 %all-to-all-start.5 = ((bf16[16,64,128]{2,1,0:T(8,128)(2,1)}), bf16[16,64,128]{2,1,0:T(8,128)(2,1)S(1)}, u32[]{:S(2)}, u32[]{:S(2)}) async-start(bf16[16,64,128]{2,1,0:T(8,128)(2,1)} %get-tuple-element.47), calls=%async_computation.5 | async-start | bytes 524288 | tf_op jit(solution)/shard_map/all_to_all | solution.py:411
  138.1 0.5 collective-permute-done.2
  138.6 3.4 %collective-permute-start.3 = (bf16[4,64,128]{2,1,0:T(8,128)(2,1)S(1)}, bf16[4,64,128]{2,1,0:T(8,128)(2,1)S(1)}, u32[]{:S(2)}, u32[]{:S(2)}) collective-permute-start(bf16[4,64,128]{2,1,0:T(8,128)(2,1)S(1)} %fusion.2), channel_id=1, source_target_pairs={{0,4},{2,6},{4,0},{6,2},{1,5},{3,7},{5,1},{7,3},{8,12},{10,14},{12... | collective-permute-start | bytes 196616 | tf_op jit(solution)/shard_map/ppermute | solution.py:417
  142.0 4.3 %collective-permute-done.3 = bf16[4,64,128]{2,1,0:T(8,128)(2,1)S(1)} collective-permute-done((bf16[4,64,128]{2,1,0:T(8,128)(2,1)S(1)}, bf16[4,64,128]{2,1,0:T(8,128)(2,1)S(1)}, u32[]{:S(2)}, u32[]{:S(2)}) %collective-permute-start.3) | collective-permute-done | bytes 65568 | tf_op jit(solution)/shard_map/ppermute | solution.py:417
  146.3 3.2 %collective-permute-start.4 = (bf16[2,64,128]{2,1,0:T(8,128)(2,1)S(1)}, bf16[2,64,128]{2,1,0:T(8,128)(2,1)S(1)}, u32[]{:S(2)}, u32[]{:S(2)}) collective-permute-start(bf16[2,64,128]{2,1,0:T(8,128)(2,1)S(1)} %slice.29), channel_id=1, source_target_pairs={{0,8},{8,0},{16,24},{24,16},{1,9},{9,1},{17,25},{25,17},{2,10},{10... | collective-permute-start | bytes 98312 | tf_op jit(solution)/shard_map/ppermute | solution.py:415
  149.5 1.5 all-to-all-done.5
  151.1 0.8 broadcast_in_dim.7
  151.8 9.9 %all-to-all-start.6 = ((bf16[16,64,128]{2,1,0:T(8,128)(2,1)}), bf16[16,64,128]{2,1,0:T(8,128)(2,1)S(1)}, u32[]{:S(2)}, u32[]{:S(2)}) async-start(bf16[16,64,128]{2,1,0:T(8,128)(2,1)} %broadcast_in_dim.7), calls=%async_computation.6 | async-start | bytes 524288 | tf_op jit(solution)/shard_map/all_to_all | solution.py:411
  161.8 0.0 collective-permute-done.4
  161.8 4.0 %collective-permute-start.5 = (bf16[64,128]{1,0:T(8,128)(2,1)S(1)}, bf16[64,128]{1,0:T(8,128)(2,1)S(1)}, u32[]{:S(2)}, u32[]{:S(2)}) collective-permute-start(bf16[64,128]{1,0:T(8,128)(2,1)S(1)} %fusion.6), channel_id=1, source_target_pairs={{0,16},{8,24},{16,0},{24,8},{1,17},{9,25},{17,1},{25,9},{2,18},{10... | collective-permute-start | bytes 49160 | tf_op jit(solution)/shard_map/ppermute | solution.py:417
  165.8 2.8 %collective-permute-done.5 = bf16[64,128]{1,0:T(8,128)(2,1)S(1)} collective-permute-done((bf16[64,128]{1,0:T(8,128)(2,1)S(1)}, bf16[64,128]{1,0:T(8,128)(2,1)S(1)}, u32[]{:S(2)}, u32[]{:S(2)}) %collective-permute-start.5) | collective-permute-done | bytes 16416 | tf_op jit(solution)/shard_map/ppermute | solution.py:417
  168.7 0.6 fusion.5
  169.3 5.9 %all-to-all-done.6.in_ref = bf16[16,64,128]{2,1,0:T(8,128)(2,1)S(1)} async-done(((bf16[16,64,128]{2,1,0:T(8,128)(2,1)}), bf16[16,64,128]{2,1,0:T(8,128)(2,1)S(1)}, u32[]{:S(2)}, u32[]{:S(2)}) %all-to-all-start.6) | async-done | bytes 262176 | tf_op jit(solution)/shard_map/all_to_all | solution.py:411
  175.1 0.8 lay.1
  (9 shorter events, 0.1 us)
Async XLA Ops:
  0.6 12.4 %copy-start.3 = (f32[64]{0:T(128)S(1)}, f32[64]{0:T(128)}, u32[]{:S(2)}) copy-start(f32[64]{0:T(128)} %param.12) | copy-start | bytes 772
  0.6 12.4 %copy-start.2 = (f32[128,2]{0,1:T(2,128)S(1)}, f32[128,2]{0,1:T(2,128)}, u32[]{:S(2)}) copy-start(f32[128,2]{0,1:T(2,128)} %param.16) | copy-start | bytes 3076
  2.1 17.9 %all-to-all-start = ((bf16[16,64,128]{2,1,0:T(8,128)(2,1)}), bf16[16,64,128]{2,1,0:T(8,128)(2,1)S(1)}, u32[]{:S(2)}, u32[]{:S(2)}) async-start(bf16[16,64,128]{2,1,0:T(8,128)(2,1)} %broadcast_in_dim.6), calls=%async_computation | async-start | bytes 524288 | tf_op jit(solution)/shard_map/all_to_all | solution.py:411
  52.5 20.9 %copy-start.1 = (bf16[2,256,2048]{2,1,0:T(8,128)(2,1)S(1)}, bf16[2,256,2048]{2,1,0:T(8,128)(2,1)}, u32[]{:S(2)}) copy-start(bf16[2,256,2048]{2,1,0:T(8,128)(2,1)} %down_ref.5) | copy-start | bytes 6291460
  53.4 20.0 %copy-start = (bf16[2,2048,256]{2,1,0:T(8,128)(2,1)S(1)}, bf16[2,2048,256]{2,1,0:T(8,128)(2,1)}, u32[]{:S(2)}) copy-start(bf16[2,2048,256]{2,1,0:T(8,128)(2,1)} %up_ref.5) | copy-start | bytes 6291460
  71.5 4.8 %collective-permute-start = (bf16[4,4,304,128]{3,2,1,0:T(8,128)(2,1)S(1)}, bf16[4,4,304,128]{3,2,1,0:T(8,128)(2,1)S(1)}, u32[]{:S(2)}, u32[]{:S(2)}) collective-permute-start(bf16[4,4,304,128]{3,2,1,0:T(8,128)(2,1)S(1)} %all_to_all.36.in_ref), channel_id=1, source_target_pairs={{0,1},{1,0},{2,3},{3,2},{4,5},{5,4},{6,7},{7,6},{8,9},{9,8},{10,11... | collective-permute-start | bytes 3735560 | tf_op jit(solution)/shard_map/ppermute | solution.py:462
  79.0 4.8 %collective-permute-start.1 = (bf16[4,4,304,128]{3,2,1,0:T(8,128)(2,1)S(1)}, bf16[4,4,304,128]{3,2,1,0:T(8,128)(2,1)S(1)}, u32[]{:S(2)}, u32[]{:S(2)}) collective-permute-start(bf16[4,4,304,128]{3,2,1,0:T(8,128)(2,1)S(1)} %both_ways.1), channel_id=1, source_target_pairs={{0,1},{1,0},{2,3},{3,2},{4,5},{5,4},{6,7},{7,6},{8,9},{9,8},{10,11... | collective-permute-start | bytes 3735560 | tf_op jit(solution)/shard_map/ppermute | solution.py:479
  131.1 7.4 %collective-permute-start.2 = (bf16[2,4,64,128]{3,2,1,0:T(8,128)(2,1)S(1)}, bf16[2,4,64,128]{3,2,1,0:T(8,128)(2,1)S(1)}, u32[]{:S(2)}, u32[]{:S(2)}) collective-permute-start(bf16[2,4,64,128]{3,2,1,0:T(8,128)(2,1)S(1)} %get-tuple-element.46), channel_id=1, source_target_pairs={{0,2},{2,0},{4,6},{6,4},{1,3},{3,1},{5,7},{7,5},{8,10},{10,8},{12,... | collective-permute-start | bytes 393224 | tf_op jit(solution)/shard_map/ppermute | solution.py:415
  134.5 16.5 %all-to-all-start.5 = ((bf16[16,64,128]{2,1,0:T(8,128)(2,1)}), bf16[16,64,128]{2,1,0:T(8,128)(2,1)S(1)}, u32[]{:S(2)}, u32[]{:S(2)}) async-start(bf16[16,64,128]{2,1,0:T(8,128)(2,1)} %get-tuple-element.47), calls=%async_computation.5 | async-start | bytes 524288 | tf_op jit(solution)/shard_map/all_to_all | solution.py:411
  138.6 7.7 %collective-permute-start.3 = (bf16[4,64,128]{2,1,0:T(8,128)(2,1)S(1)}, bf16[4,64,128]{2,1,0:T(8,128)(2,1)S(1)}, u32[]{:S(2)}, u32[]{:S(2)}) collective-permute-start(bf16[4,64,128]{2,1,0:T(8,128)(2,1)S(1)} %fusion.2), channel_id=1, source_target_pairs={{0,4},{2,6},{4,0},{6,2},{1,5},{3,7},{5,1},{7,3},{8,12},{10,14},{12... | collective-permute-start | bytes 196616 | tf_op jit(solution)/shard_map/ppermute | solution.py:417
  146.3 15.5 %collective-permute-start.4 = (bf16[2,64,128]{2,1,0:T(8,128)(2,1)S(1)}, bf16[2,64,128]{2,1,0:T(8,128)(2,1)S(1)}, u32[]{:S(2)}, u32[]{:S(2)}) collective-permute-start(bf16[2,64,128]{2,1,0:T(8,128)(2,1)S(1)} %slice.29), channel_id=1, source_target_pairs={{0,8},{8,0},{16,24},{24,16},{1,9},{9,1},{17,25},{25,17},{2,10},{10... | collective-permute-start | bytes 98312 | tf_op jit(solution)/shard_map/ppermute | solution.py:415
  151.8 23.3 %all-to-all-start.6 = ((bf16[16,64,128]{2,1,0:T(8,128)(2,1)}), bf16[16,64,128]{2,1,0:T(8,128)(2,1)S(1)}, u32[]{:S(2)}, u32[]{:S(2)}) async-start(bf16[16,64,128]{2,1,0:T(8,128)(2,1)} %broadcast_in_dim.7), calls=%async_computation.6 | async-start | bytes 524288 | tf_op jit(solution)/shard_map/all_to_all | solution.py:411
  161.8 6.8 %collective-permute-start.5 = (bf16[64,128]{1,0:T(8,128)(2,1)S(1)}, bf16[64,128]{1,0:T(8,128)(2,1)S(1)}, u32[]{:S(2)}, u32[]{:S(2)}) collective-permute-start(bf16[64,128]{1,0:T(8,128)(2,1)S(1)} %fusion.6), channel_id=1, source_target_pairs={{0,16},{8,24},{16,0},{24,8},{1,17},{9,25},{17,1},{25,9},{2,18},{10... | collective-permute-start | bytes 49160 | tf_op jit(solution)/shard_map/ppermute | solution.py:417

commit v6 on v5

--- a/solution.py
+++ b/solution.py
@@ -12,7 +12,8 @@
 BLOCKS = 16
 CAP = 9
 MSG = 20
-ORDER = (0, 2, 1, 3)
+ORDER_X = (0, 3, 1, 2)
+ORDER_Y = (0, 2, 1, 3)
 PACK = 304
 SLOTS = BLOCKS * CAP
 SIDE = 2432
@@ -153,12 +154,14 @@
         out_ref[chip] = jnp.where(core_ref[0] == 0, turned[0:64], turned[64:128]).astype(BF16)
 
 
-def dispatch(block_ref, heads_ref, side_ref, place_ref, gate_ref, stream_ref, out_ref):
+def dispatch(block_ref, heads_ref, side_ref, place_ref, gate_ref, stream_ref, whole_ref, out_ref):
     pieces = []
     for chip in range(16):
         pieces.append(heads_ref[0, chip])
         pieces.append(heads_ref[1, chip])
-    mixed = dot_nn(side_ref[:, 0:2048], jnp.concatenate(pieces, axis=0))
+    heads = jnp.concatenate(pieces, axis=0)
+    whole_ref[...] = heads
+    mixed = dot_nn(side_ref[:, 0:2048], heads)
     stream = side_ref[:, 2048:2176].astype(F32) + mixed
     stream_ref[...] = stream
     shift = jnp.mean(stream, axis=0, keepdims=True)
@@ -389,15 +392,15 @@
     own = jnp.where(low, grad[0:64], grad[64:128]).astype(BF16)
     grad_ref[...] = own
     pair_ref[...] = grad.astype(BF16)
+    product = dot_nt(own, heads_ref[...]).astype(BF16)
     for chip in range(16):
-        heads = jnp.concatenate([heads_ref[0, chip], heads_ref[1, chip]], axis=0)
-        gw_ref[chip] = dot_nt(own, heads).astype(BF16)
+        gw_ref[chip] = product[:, chip * 128 : chip * 128 + 128]
 
 
 def heads_back(at_ref, pair_ref, weight_ref, keep_ref, send_ref):
     for k in range(4):
         for j in range(4):
-            chip = (at_ref[1] ^ ORDER[j]) * 4 + (at_ref[0] ^ ORDER[k])
+            chip = (at_ref[1] ^ ORDER_Y[j]) * 4 + (at_ref[0] ^ ORDER_X[k])
             out_ref = keep_ref if k < 2 else send_ref
             out_ref[k % 2, j] = dot_nn(weight_ref[chip], pair_ref[...]).astype(BF16)
 
@@ -411,10 +414,10 @@
     return lax.all_to_all(value, axes, split_axis=0, concat_axis=0, tiled=True)
 
 
-def halve(keep, send, axis):
+def halve(keep, send, axis, far):
     came = lax.ppermute(send, axis, [(i, i ^ 1) for i in range(4)])
     half = keep.astype(F32) + came.astype(F32)
-    came = lax.ppermute(half[1].astype(BF16), axis, [(i, i ^ 2) for i in range(4)])
+    came = lax.ppermute(half[1].astype(BF16), axis, [(i, i ^ far) for i in range(4)])
     return half[0], came
 
 
@@ -451,8 +454,16 @@
     at = jnp.stack([lax.axis_index("x"), lax.axis_index("yl")]).astype(jnp.int32)
     heads_t, turned, at = lax.optimization_barrier((heads_t, turned, at))
     heads_t = lax.all_gather(heads_t, "c", axis=0)
-    stream, message = call(
-        dispatch, (shape((128, 128), F32), shape((BLOCKS, 4, 2, MSG * 64), BF16)), "dispatch", 1, 4
+    stream, heads_t, message = call(
+        dispatch,
+        (
+            shape((128, 128), F32),
+            shape((WIDTH, 128), BF16),
+            shape((BLOCKS, 4, 2, MSG * 64), BF16),
+        ),
+        "dispatch",
+        1,
+        4,
     )(block, heads_t, side, place, gate)
     message = a2a(message.reshape(64, 2, MSG * 64), ("yh", "z", "yl"))
     packed = call(repack, shape((4, 4, PACK, 128), BF16), "repack", 0, 2)(
@@ -506,12 +517,12 @@
     keep, send = call(heads_back, (shape((2, 4, 64, 128), BF16),) * 2, "heads_back", 1, 2)(
         at, grad_pair, turned
     )
-    pieces = halve(keep, send, "x")
+    pieces = halve(keep, send, "x", 3)
     grad_weight = jnp.broadcast_to(grad_weight, (16, 64, 128))
     grad_weight = a2a(grad_weight, EXPERT)
     grad_weight = call(lay, shape((64, WIDTH), BF16), "lay", 0, 1)(grad_weight)
     heads_sum = (pieces[0] + pieces[1].astype(F32)).astype(BF16)
-    pieces = halve(heads_sum[0:2], heads_sum[2:4], "yl")
+    pieces = halve(heads_sum[0:2], heads_sum[2:4], "yl", 2)
     grad_heads = (pieces[0] + pieces[1].astype(F32)).astype(BF16).T
     return (result.T, grad_residual.T, grad_heads, grad_weight.T)
 

time: 177 us -> 176 us (level)
  the two profiles are of different devices: /device:TPU:2 before, /device:TPU:16 now
where the time goes in v6:
time: 176 us; the launch traced here: 175 us
  blocking collectives  96.4 us (55%)
  starting transfers between devices  35.3 us (20%)
  waiting for transfers between devices  25.2 us (14%)
  Pallas kernels  12.7 us (7%)
  other arithmetic  2.49 us (1%)
  local copies, waits for them, and re-layouts  2.28 us (1%)
    all_to_all x4, blocking collectives, a2a(): return lax.all_to_all(value, axes, split_axis=0, concat_axis=0, tiled=True)  90 us
    all_to_all x3, starting transfers between devices, a2a(): return lax.all_to_all(value, axes, split_axis=0, concat_axis=0, tiled=True)  20.4 us
    all_to_all x3, waiting for transfers between devices, a2a(): return lax.all_to_all(value, axes, split_axis=0, concat_axis=0, tiled=True)  13.6 us
    ppermute x2, waiting for transfers between devices, halve(): lax.ppermute(half[1].astype(BF16), axis, [(i, i ^ far) for i in range(4)])  8.08 us
    ppermute x2, starting transfers between devices, halve(): lax.ppermute(half[1].astype(BF16), axis, [(i, i ^ far) for i in range(4)])  5.82 us
    ppermute x2, starting transfers between devices, halve(): came = lax.ppermute(send, axis, [(i, i ^ 1) for i in range(4)])  5.11 us
  transfers between devices with their start and end apart: 9, of which 8 were waited for; matrix products, arithmetic and copies ran while one was open for 2% of the time, Pallas kernels for 2%

profile of v6, /device:TPU:16, one launch (start us, length us, event | category | flops | bytes accessed | tf_op | source)
XLA Modules:
  0.0 175.4 jit_solution(11945830282912879135)
XLA Ops:
  0.6 0.0 copy-start.3
  0.6 0.0 copy-start.2
  0.7 1.5 broadcast_in_dim.6
  2.1 9.1 %all-to-all-start = ((bf16[16,64,128]{2,1,0:T(8,128)(2,1)}), bf16[16,64,128]{2,1,0:T(8,128)(2,1)S(1)}, u32[]{:S(2)}, u32[]{:S(2)}) async-start(bf16[16,64,128]{2,1,0:T(8,128)(2,1)} %broadcast_in_dim.6), calls=%async_computation | async-start | bytes 524288 | tf_op jit(solution)/shard_map/all_to_all | solution.py:414
  11.2 0.7 convert_bitcast_fusion
  11.9 1.0 pad_maximum_fusion.wide_ref
  12.9 0.0 copy-done.3
  12.9 0.0 copy-done.2
  13.0 0.2 prepare.1
  13.2 2.3 %all_gather.15.side_ref = bf16[128,2432]{1,0:T(8,128)(2,1)S(1)} all-gather(bf16[64,2432]{1,0:T(8,128)(2,1)S(1)} %get-tuple-element.27), channel_id=1, replica_groups=mesh['yh'=2,'z'=8,'yl'=4,'x'=4,'c'=2] {'c'}, dimensions={0}, use_global_device_ids=true | all-gather | bytes 933888 | tf_op jit(solution)/shard_map/all_gather | solution.py:452
  15.5 0.5 turn_weight.1.weight_ref
  15.9 0.1 pad_add_fusion.at_ref
  16.0 2.8 %all-to-all-done = bf16[16,64,128]{2,1,0:T(8,128)(2,1)S(1)} async-done(((bf16[16,64,128]{2,1,0:T(8,128)(2,1)}), bf16[16,64,128]{2,1,0:T(8,128)(2,1)S(1)}, u32[]{:S(2)}, u32[]{:S(2)}) %all-to-all-start) | async-done | bytes 262176 | tf_op jit(solution)/shard_map/all_to_all | solution.py:414
  18.8 2.2 %all-gather = bf16[32,64,128]{2,1,0:T(8,128)(2,1)S(1)} all-gather(bf16[16,64,128]{2,1,0:T(8,128)(2,1)S(1)} %all-to-all-done), channel_id=2, replica_groups=mesh['yh'=2,'z'=8,'yl'=4,'x'=4,'c'=2] {'c'}, dimensions={0}, use_global_device_ids=true | all-gather | bytes 786432 | tf_op jit(solution)/shard_map/all_gather | solution.py:456
  21.0 0.8 dispatch.1
  21.8 30.6 %all_to_all.35 = bf16[64,2,1280]{2,1,0:T(2,128)(2,1)S(1)} all-to-all(bf16[64,2,1280]{2,1,0:T(2,128)(2,1)S(1)} %bitcast.47), channel_id=1, replica_groups=mesh['yh'=2,'z'=8,'yl'=4,'x'=4,'c'=2] {'yh','z','yl'}, dimensions={0} | all-to-all | bytes 655360 | tf_op jit(solution)/shard_map/all_to_all | solution.py:414
  52.4 0.0 copy-start.1
  52.4 0.9 repack.1
  53.3 0.0 copy-start
  53.3 18.4 %all_to_all.36.in_ref = bf16[4,4,304,128]{3,2,1,0:T(8,128)(2,1)S(1)} all-to-all(bf16[4,4,304,128]{3,2,1,0:T(8,128)(2,1)S(1)} %repack.1), channel_id=1, replica_groups=mesh['yh'=2,'z'=8,'yl'=4,'x'=4,'c'=2] {'x'}, dimensions={0} | all-to-all | bytes 2490368 | tf_op jit(solution)/shard_map/all_to_all | solution.py:414
  71.7 1.9 %collective-permute-start = (bf16[4,4,304,128]{3,2,1,0:T(8,128)(2,1)S(1)}, bf16[4,4,304,128]{3,2,1,0:T(8,128)(2,1)S(1)}, u32[]{:S(2)}, u32[]{:S(2)}) collective-permute-start(bf16[4,4,304,128]{3,2,1,0:T(8,128)(2,1)S(1)} %all_to_all.36.in_ref), channel_id=1, source_target_pairs={{0,1},{1,0},{2,3},{3,2},{4,5},{5,4},{6,7},{7,6},{8,9},{9,8},{10,11... | collective-permute-start | bytes 3735560 | tf_op jit(solution)/shard_map/ppermute | solution.py:473
  73.6 0.0 copy-done.1
  73.6 0.0 copy-done
  73.6 1.6 only_ahead.1
  75.2 1.3 collective-permute-done.in_ref
  76.5 2.7 %both_ways.1 = bf16[4,4,304,128]{3,2,1,0:T(8,128)(2,1)S(1)} custom-call(s32[1]{0:T(128)S(6)} %sub.3.which_ref, bf16[4,4,304,128]{3,2,1,0:T(8,128)(2,1)S(1)} %collective-permute-done.in_ref, bf16[2,2048,256]{2,1,0:T(8,128)(2,1)S(1)} %copy-done, bf16[2,256,2048]{2,1,0:T(8,128)(2,1)S(1)} %copy-done.1), custom_call_target="tpu_custom_call" | custom-call | tf_op jit(solution)/shard_map/both_ways/pallas_call | solution.py:486
  79.2 2.0 %collective-permute-start.1 = (bf16[4,4,304,128]{3,2,1,0:T(8,128)(2,1)S(1)}, bf16[4,4,304,128]{3,2,1,0:T(8,128)(2,1)S(1)}, u32[]{:S(2)}, u32[]{:S(2)}) collective-permute-start(bf16[4,4,304,128]{3,2,1,0:T(8,128)(2,1)S(1)} %both_ways.1), channel_id=1, source_target_pairs={{0,1},{1,0},{2,3},{3,2},{4,5},{5,4},{6,7},{7,6},{8,9},{9,8},{10,11... | collective-permute-start | bytes 3735560 | tf_op jit(solution)/shard_map/ppermute | solution.py:490
  81.2 1.5 only_behind.1.grad_ref
  82.8 1.2 collective-permute-done.1.came_ref
  84.0 0.3 add_pair.1
  84.3 20.2 %all_to_all.37.in_ref = bf16[4,4,304,128]{3,2,1,0:T(8,128)(2,1)S(1)} all-to-all(bf16[4,4,304,128]{3,2,1,0:T(8,128)(2,1)S(1)} %add_pair.1), channel_id=1, replica_groups=mesh['yh'=2,'z'=8,'yl'=4,'x'=4,'c'=2] {'x'}, dimensions={0} | all-to-all | bytes 2490368 | tf_op jit(solution)/shard_map/all_to_all | solution.py:414
  104.5 0.8 add_four.1
  105.4 20.8 %all_to_all.38 = bf16[64,2,1280]{2,1,0:T(2,128)(2,1)S(1)} all-to-all(bf16[64,2,1280]{2,1,0:T(2,128)(2,1)S(1)} %bitcast.44), channel_id=1, replica_groups=mesh['yh'=2,'z'=8,'yl'=4,'x'=4,'c'=2] {'yh','z','yl'}, dimensions={0} | all-to-all | bytes 655360 | tf_op jit(solution)/shard_map/all_to_all | solution.py:414
  126.2 0.7 combine.1
  126.9 2.0 %all-gather.1 = f32[528,128]{1,0:T(8,128)S(1)} all-gather(f32[264,128]{1,0:T(8,128)S(1)} %combine.1), channel_id=3, replica_groups=mesh['yh'=2,'z'=8,'yl'=4,'x'=4,'c'=2] {'c'}, dimensions={0}, use_global_device_ids=true | all-gather | bytes 405504 | tf_op jit(solution)/shard_map/all_gather | solution.py:503
  128.9 1.1 finish.1
  130.0 0.8 heads_back.1
  130.8 2.5 %collective-permute-start.2 = (bf16[2,4,64,128]{3,2,1,0:T(8,128)(2,1)S(1)}, bf16[2,4,64,128]{3,2,1,0:T(8,128)(2,1)S(1)}, u32[]{:S(2)}, u32[]{:S(2)}) collective-permute-start(bf16[2,4,64,128]{3,2,1,0:T(8,128)(2,1)S(1)} %get-tuple-element.48), channel_id=1, source_target_pairs={{0,2},{2,0},{4,6},{6,4},{1,3},{3,1},{5,7},{7,5},{8,10},{10,8},{12,... | collective-permute-start | bytes 393224 | tf_op jit(solution)/shard_map/ppermute | solution.py:418
  133.3 3.9 %all-to-all-start.5 = ((bf16[16,64,128]{2,1,0:T(8,128)(2,1)}), bf16[16,64,128]{2,1,0:T(8,128)(2,1)S(1)}, u32[]{:S(2)}, u32[]{:S(2)}) async-start(bf16[16,64,128]{2,1,0:T(8,128)(2,1)} %get-tuple-element.49), calls=%async_computation.5 | async-start | bytes 524288 | tf_op jit(solution)/shard_map/all_to_all | solution.py:414
  137.2 1.0 collective-permute-done.2
  138.3 3.1 %collective-permute-start.3 = (bf16[4,64,128]{2,1,0:T(8,128)(2,1)S(1)}, bf16[4,64,128]{2,1,0:T(8,128)(2,1)S(1)}, u32[]{:S(2)}, u32[]{:S(2)}) collective-permute-start(bf16[4,64,128]{2,1,0:T(8,128)(2,1)S(1)} %fusion.2), channel_id=1, source_target_pairs={{0,6},{2,4},{4,2},{6,0},{1,7},{3,5},{5,3},{7,1},{8,14},{10,12},{12... | collective-permute-start | bytes 196616 | tf_op jit(solution)/shard_map/ppermute | solution.py:420
  141.4 4.3 %collective-permute-done.3 = bf16[4,64,128]{2,1,0:T(8,128)(2,1)S(1)} collective-permute-done((bf16[4,64,128]{2,1,0:T(8,128)(2,1)S(1)}, bf16[4,64,128]{2,1,0:T(8,128)(2,1)S(1)}, u32[]{:S(2)}, u32[]{:S(2)}) %collective-permute-start.3) | collective-permute-done | bytes 65568 | tf_op jit(solution)/shard_map/ppermute | solution.py:420
  145.7 2.6 %collective-permute-start.4 = (bf16[2,64,128]{2,1,0:T(8,128)(2,1)S(1)}, bf16[2,64,128]{2,1,0:T(8,128)(2,1)S(1)}, u32[]{:S(2)}, u32[]{:S(2)}) collective-permute-start(bf16[2,64,128]{2,1,0:T(8,128)(2,1)S(1)} %slice.29), channel_id=1, source_target_pairs={{0,8},{8,0},{16,24},{24,16},{1,9},{9,1},{17,25},{25,17},{2,10},{10... | collective-permute-start | bytes 98312 | tf_op jit(solution)/shard_map/ppermute | solution.py:418
  148.4 4.3 %all-to-all-done.5 = bf16[16,64,128]{2,1,0:T(8,128)(2,1)S(1)} async-done(((bf16[16,64,128]{2,1,0:T(8,128)(2,1)}), bf16[16,64,128]{2,1,0:T(8,128)(2,1)S(1)}, u32[]{:S(2)}, u32[]{:S(2)}) %all-to-all-start.5) | async-done | bytes 262176 | tf_op jit(solution)/shard_map/all_to_all | solution.py:414
  152.7 0.8 broadcast_in_dim.7
  153.4 7.5 %all-to-all-start.6 = ((bf16[16,64,128]{2,1,0:T(8,128)(2,1)}), bf16[16,64,128]{2,1,0:T(8,128)(2,1)S(1)}, u32[]{:S(2)}, u32[]{:S(2)}) async-start(bf16[16,64,128]{2,1,0:T(8,128)(2,1)} %broadcast_in_dim.7), calls=%async_computation.6 | async-start | bytes 524288 | tf_op jit(solution)/shard_map/all_to_all | solution.py:414
  160.9 0.0 collective-permute-done.4
  160.9 2.7 %collective-permute-start.5 = (bf16[64,128]{1,0:T(8,128)(2,1)S(1)}, bf16[64,128]{1,0:T(8,128)(2,1)S(1)}, u32[]{:S(2)}, u32[]{:S(2)}) collective-permute-start(bf16[64,128]{1,0:T(8,128)(2,1)S(1)} %fusion.6), channel_id=1, source_target_pairs={{0,16},{8,24},{16,0},{24,8},{1,17},{9,25},{17,1},{25,9},{2,18},{10... | collective-permute-start | bytes 49160 | tf_op jit(solution)/shard_map/ppermute | solution.py:420
  163.7 3.8 %collective-permute-done.5 = bf16[64,128]{1,0:T(8,128)(2,1)S(1)} collective-permute-done((bf16[64,128]{1,0:T(8,128)(2,1)S(1)}, bf16[64,128]{1,0:T(8,128)(2,1)S(1)}, u32[]{:S(2)}, u32[]{:S(2)}) %collective-permute-start.5) | collective-permute-done | bytes 16416 | tf_op jit(solution)/shard_map/ppermute | solution.py:420
  167.5 0.6 fusion.5
  168.1 6.5 %all-to-all-done.6.in_ref = bf16[16,64,128]{2,1,0:T(8,128)(2,1)S(1)} async-done(((bf16[16,64,128]{2,1,0:T(8,128)(2,1)}), bf16[16,64,128]{2,1,0:T(8,128)(2,1)S(1)}, u32[]{:S(2)}, u32[]{:S(2)}) %all-to-all-start.6) | async-done | bytes 262176 | tf_op jit(solution)/shard_map/all_to_all | solution.py:414
  174.6 0.8 lay.1
  (9 shorter events, 0.1 us)
Async XLA Ops:
  0.6 12.3 %copy-start.3 = (f32[64]{0:T(128)S(1)}, f32[64]{0:T(128)}, u32[]{:S(2)}) copy-start(f32[64]{0:T(128)} %param.12) | copy-start | bytes 772
  0.6 12.3 %copy-start.2 = (f32[128,2]{0,1:T(2,128)S(1)}, f32[128,2]{0,1:T(2,128)}, u32[]{:S(2)}) copy-start(f32[128,2]{0,1:T(2,128)} %param.16) | copy-start | bytes 3076
  2.1 16.7 %all-to-all-start = ((bf16[16,64,128]{2,1,0:T(8,128)(2,1)}), bf16[16,64,128]{2,1,0:T(8,128)(2,1)S(1)}, u32[]{:S(2)}, u32[]{:S(2)}) async-start(bf16[16,64,128]{2,1,0:T(8,128)(2,1)} %broadcast_in_dim.6), calls=%async_computation | async-start | bytes 524288 | tf_op jit(solution)/shard_map/all_to_all | solution.py:414
  52.4 21.2 %copy-start.1 = (bf16[2,256,2048]{2,1,0:T(8,128)(2,1)S(1)}, bf16[2,256,2048]{2,1,0:T(8,128)(2,1)}, u32[]{:S(2)}) copy-start(bf16[2,256,2048]{2,1,0:T(8,128)(2,1)} %down_ref.5) | copy-start | bytes 6291460
  53.3 20.3 %copy-start = (bf16[2,2048,256]{2,1,0:T(8,128)(2,1)S(1)}, bf16[2,2048,256]{2,1,0:T(8,128)(2,1)}, u32[]{:S(2)}) copy-start(bf16[2,2048,256]{2,1,0:T(8,128)(2,1)} %up_ref.5) | copy-start | bytes 6291460
  71.7 4.8 %collective-permute-start = (bf16[4,4,304,128]{3,2,1,0:T(8,128)(2,1)S(1)}, bf16[4,4,304,128]{3,2,1,0:T(8,128)(2,1)S(1)}, u32[]{:S(2)}, u32[]{:S(2)}) collective-permute-start(bf16[4,4,304,128]{3,2,1,0:T(8,128)(2,1)S(1)} %all_to_all.36.in_ref), channel_id=1, source_target_pairs={{0,1},{1,0},{2,3},{3,2},{4,5},{5,4},{6,7},{7,6},{8,9},{9,8},{10,11... | collective-permute-start | bytes 3735560 | tf_op jit(solution)/shard_map/ppermute | solution.py:473
  79.2 4.8 %collective-permute-start.1 = (bf16[4,4,304,128]{3,2,1,0:T(8,128)(2,1)S(1)}, bf16[4,4,304,128]{3,2,1,0:T(8,128)(2,1)S(1)}, u32[]{:S(2)}, u32[]{:S(2)}) collective-permute-start(bf16[4,4,304,128]{3,2,1,0:T(8,128)(2,1)S(1)} %both_ways.1), channel_id=1, source_target_pairs={{0,1},{1,0},{2,3},{3,2},{4,5},{5,4},{6,7},{7,6},{8,9},{9,8},{10,11... | collective-permute-start | bytes 3735560 | tf_op jit(solution)/shard_map/ppermute | solution.py:490
  130.8 7.4 %collective-permute-start.2 = (bf16[2,4,64,128]{3,2,1,0:T(8,128)(2,1)S(1)}, bf16[2,4,64,128]{3,2,1,0:T(8,128)(2,1)S(1)}, u32[]{:S(2)}, u32[]{:S(2)}) collective-permute-start(bf16[2,4,64,128]{3,2,1,0:T(8,128)(2,1)S(1)} %get-tuple-element.48), channel_id=1, source_target_pairs={{0,2},{2,0},{4,6},{6,4},{1,3},{3,1},{5,7},{7,5},{8,10},{10,8},{12,... | collective-permute-start | bytes 393224 | tf_op jit(solution)/shard_map/ppermute | solution.py:418
  133.3 19.3 %all-to-all-start.5 = ((bf16[16,64,128]{2,1,0:T(8,128)(2,1)}), bf16[16,64,128]{2,1,0:T(8,128)(2,1)S(1)}, u32[]{:S(2)}, u32[]{:S(2)}) async-start(bf16[16,64,128]{2,1,0:T(8,128)(2,1)} %get-tuple-element.49), calls=%async_computation.5 | async-start | bytes 524288 | tf_op jit(solution)/shard_map/all_to_all | solution.py:414
  138.3 7.4 %collective-permute-start.3 = (bf16[4,64,128]{2,1,0:T(8,128)(2,1)S(1)}, bf16[4,64,128]{2,1,0:T(8,128)(2,1)S(1)}, u32[]{:S(2)}, u32[]{:S(2)}) collective-permute-start(bf16[4,64,128]{2,1,0:T(8,128)(2,1)S(1)} %fusion.2), channel_id=1, source_target_pairs={{0,6},{2,4},{4,2},{6,0},{1,7},{3,5},{5,3},{7,1},{8,14},{10,12},{12... | collective-permute-start | bytes 196616 | tf_op jit(solution)/shard_map/ppermute | solution.py:420
  145.7 15.2 %collective-permute-start.4 = (bf16[2,64,128]{2,1,0:T(8,128)(2,1)S(1)}, bf16[2,64,128]{2,1,0:T(8,128)(2,1)S(1)}, u32[]{:S(2)}, u32[]{:S(2)}) collective-permute-start(bf16[2,64,128]{2,1,0:T(8,128)(2,1)S(1)} %slice.29), channel_id=1, source_target_pairs={{0,8},{8,0},{16,24},{24,16},{1,9},{9,1},{17,25},{25,17},{2,10},{10... | collective-permute-start | bytes 98312 | tf_op jit(solution)/shard_map/ppermute | solution.py:418
  153.4 21.2 %all-to-all-start.6 = ((bf16[16,64,128]{2,1,0:T(8,128)(2,1)}), bf16[16,64,128]{2,1,0:T(8,128)(2,1)S(1)}, u32[]{:S(2)}, u32[]{:S(2)}) async-start(bf16[16,64,128]{2,1,0:T(8,128)(2,1)} %broadcast_in_dim.7), calls=%async_computation.6 | async-start | bytes 524288 | tf_op jit(solution)/shard_map/all_to_all | solution.py:414
  160.9 6.5 %collective-permute-start.5 = (bf16[64,128]{1,0:T(8,128)(2,1)S(1)}, bf16[64,128]{1,0:T(8,128)(2,1)S(1)}, u32[]{:S(2)}, u32[]{:S(2)}) collective-permute-start(bf16[64,128]{1,0:T(8,128)(2,1)S(1)} %fusion.6), channel_id=1, source_target_pairs={{0,16},{8,24},{16,0},{24,8},{1,17},{9,25},{17,1},{25,9},{2,18},{10... | collective-permute-start | bytes 49160 | tf_op jit(solution)/shard_map/ppermute | solution.py:420

commit v7 on v6

--- a/solution.py
+++ b/solution.py
@@ -92,13 +92,14 @@
 
 
 def row_place(row):
-    return row & 15, lax.shift_right_logical(row, 4)
+    pair = lax.shift_right_logical(row, 5)
+    return lax.shift_right_logical(row & 31, 1), 2 * pair + (row & 1)
 
 
 def write_messages(out_ref, value, ways):
     for i in range(MSG // 2):
         at = i * 32
-        pair = jnp.stack([value[at : at + 16], value[at + 16 : at + 32]], axis=1).astype(BF16)
+        pair = value[at : at + 32].reshape(BLOCKS, 2, 128).astype(BF16)
         for y in ways:
             out_ref[:, y, :, i * 128 : i * 128 + 128] = pair
 
@@ -110,7 +111,7 @@
         for y in ways:
             came = in_ref[:, y, :, i * 128 : i * 128 + 128].astype(F32)
             pair = came if pair is None else pair + came
-        rows.extend([pair[:, 0], pair[:, 1]])
+        rows.append(pair.reshape(32, 128))
     return jnp.concatenate(rows, axis=0)
 
 
@@ -354,7 +355,10 @@
 
 def combine(in_ref, place_ref, gate_ref, out_ref):
     value = read_messages(in_ref, range(4))
-    stats = jnp.concatenate([join(value[288:304])] * MSG, axis=0)
+    stats = join(value[288:320])
+    odd = (iota((32, 128), 0) & 1) == 1
+    above = jnp.concatenate([stats[31:32], stats[0:31]], axis=0)
+    stats = jnp.concatenate([jnp.where(odd, above, stats)] * (MSG // 2), axis=0)
     value = value.astype(BF16)
     row = iota((ROWS, 128), 0)
     lane = iota((ROWS, 128), 1)

time: 176 us -> 176 us (level)
  no operation moved by 1% of the time
where the time goes in v7:
time: 176 us; the launch traced here: 175 us
  blocking collectives  96.4 us (55%)
  starting transfers between devices  35.3 us (20%)
  waiting for transfers between devices  25.1 us (14%)
  Pallas kernels  12.1 us (7%)
  other arithmetic  2.49 us (1%)
  local copies, waits for them, and re-layouts  2.28 us (1%)
    all_to_all x4, blocking collectives, a2a(): return lax.all_to_all(value, axes, split_axis=0, concat_axis=0, tiled=True)  90 us
    all_to_all x3, starting transfers between devices, a2a(): return lax.all_to_all(value, axes, split_axis=0, concat_axis=0, tiled=True)  20.4 us
    all_to_all x3, waiting for transfers between devices, a2a(): return lax.all_to_all(value, axes, split_axis=0, concat_axis=0, tiled=True)  13.5 us
    ppermute x2, waiting for transfers between devices, halve(): lax.ppermute(half[1].astype(BF16), axis, [(i, i ^ far) for i in range(4)])  8.08 us
    ppermute x2, starting transfers between devices, halve(): lax.ppermute(half[1].astype(BF16), axis, [(i, i ^ far) for i in range(4)])  5.82 us
    ppermute x2, starting transfers between devices, halve(): came = lax.ppermute(send, axis, [(i, i ^ 1) for i in range(4)])  5.14 us
  transfers between devices with their start and end apart: 9, of which 8 were waited for; matrix products, arithmetic and copies ran while one was open for 2% of the time, Pallas kernels for 2%

profile of v7, /device:TPU:16, one launch (start us, length us, event | category | flops | bytes accessed | tf_op | source)
XLA Modules:
  0.0 174.7 jit_solution(2968737630343021904)
XLA Ops:
  0.6 0.0 copy-start.3
  0.6 0.0 copy-start.2
  0.7 1.5 broadcast_in_dim.6
  2.1 9.1 %all-to-all-start = ((bf16[16,64,128]{2,1,0:T(8,128)(2,1)}), bf16[16,64,128]{2,1,0:T(8,128)(2,1)S(1)}, u32[]{:S(2)}, u32[]{:S(2)}) async-start(bf16[16,64,128]{2,1,0:T(8,128)(2,1)} %broadcast_in_dim.6), calls=%async_computation | async-start | bytes 524288 | tf_op jit(solution)/shard_map/all_to_all | solution.py:418
  11.2 0.7 convert_bitcast_fusion
  11.9 1.0 pad_maximum_fusion.wide_ref
  12.9 0.0 copy-done.3
  12.9 0.0 copy-done.2
  13.0 0.4 prepare.1
  13.3 2.3 %all_gather.15.side_ref = bf16[128,2432]{1,0:T(8,128)(2,1)S(1)} all-gather(bf16[64,2432]{1,0:T(8,128)(2,1)S(1)} %get-tuple-element.27), channel_id=1, replica_groups=mesh['yh'=2,'z'=8,'yl'=4,'x'=4,'c'=2] {'c'}, dimensions={0}, use_global_device_ids=true | all-gather | bytes 933888 | tf_op jit(solution)/shard_map/all_gather | solution.py:456
  15.6 0.5 turn_weight.1.weight_ref
  16.0 0.1 pad_add_fusion.at_ref
  16.1 2.7 %all-to-all-done = bf16[16,64,128]{2,1,0:T(8,128)(2,1)S(1)} async-done(((bf16[16,64,128]{2,1,0:T(8,128)(2,1)}), bf16[16,64,128]{2,1,0:T(8,128)(2,1)S(1)}, u32[]{:S(2)}, u32[]{:S(2)}) %all-to-all-start) | async-done | bytes 262176 | tf_op jit(solution)/shard_map/all_to_all | solution.py:418
  18.8 2.2 %all-gather = bf16[32,64,128]{2,1,0:T(8,128)(2,1)S(1)} all-gather(bf16[16,64,128]{2,1,0:T(8,128)(2,1)S(1)} %all-to-all-done), channel_id=2, replica_groups=mesh['yh'=2,'z'=8,'yl'=4,'x'=4,'c'=2] {'c'}, dimensions={0}, use_global_device_ids=true | all-gather | bytes 786432 | tf_op jit(solution)/shard_map/all_gather | solution.py:460
  21.0 0.8 dispatch.1
  21.8 30.6 %all_to_all.35 = bf16[64,2,1280]{2,1,0:T(2,128)(2,1)S(1)} all-to-all(bf16[64,2,1280]{2,1,0:T(2,128)(2,1)S(1)} %bitcast.47), channel_id=1, replica_groups=mesh['yh'=2,'z'=8,'yl'=4,'x'=4,'c'=2] {'yh','z','yl'}, dimensions={0} | all-to-all | bytes 655360 | tf_op jit(solution)/shard_map/all_to_all | solution.py:418
  52.4 0.0 copy-start.1
  52.4 0.6 repack.1
  53.0 0.0 copy-start
  53.0 18.4 %all_to_all.36.in_ref = bf16[4,4,304,128]{3,2,1,0:T(8,128)(2,1)S(1)} all-to-all(bf16[4,4,304,128]{3,2,1,0:T(8,128)(2,1)S(1)} %repack.1), channel_id=1, replica_groups=mesh['yh'=2,'z'=8,'yl'=4,'x'=4,'c'=2] {'x'}, dimensions={0} | all-to-all | bytes 2490368 | tf_op jit(solution)/shard_map/all_to_all | solution.py:418
  71.3 1.9 %collective-permute-start = (bf16[4,4,304,128]{3,2,1,0:T(8,128)(2,1)S(1)}, bf16[4,4,304,128]{3,2,1,0:T(8,128)(2,1)S(1)}, u32[]{:S(2)}, u32[]{:S(2)}) collective-permute-start(bf16[4,4,304,128]{3,2,1,0:T(8,128)(2,1)S(1)} %all_to_all.36.in_ref), channel_id=1, source_target_pairs={{0,1},{1,0},{2,3},{3,2},{4,5},{5,4},{6,7},{7,6},{8,9},{9,8},{10,11... | collective-permute-start | bytes 3735560 | tf_op jit(solution)/shard_map/ppermute | solution.py:477
  73.2 0.0 copy-done.1
  73.2 0.0 copy-done
  73.3 1.6 only_ahead.1
  74.9 1.3 collective-permute-done.in_ref
  76.1 2.7 %both_ways.1 = bf16[4,4,304,128]{3,2,1,0:T(8,128)(2,1)S(1)} custom-call(s32[1]{0:T(128)S(6)} %sub.3.which_ref, bf16[4,4,304,128]{3,2,1,0:T(8,128)(2,1)S(1)} %collective-permute-done.in_ref, bf16[2,2048,256]{2,1,0:T(8,128)(2,1)S(1)} %copy-done, bf16[2,256,2048]{2,1,0:T(8,128)(2,1)S(1)} %copy-done.1), custom_call_target="tpu_custom_call" | custom-call | tf_op jit(solution)/shard_map/both_ways/pallas_call | solution.py:490
  78.8 2.0 %collective-permute-start.1 = (bf16[4,4,304,128]{3,2,1,0:T(8,128)(2,1)S(1)}, bf16[4,4,304,128]{3,2,1,0:T(8,128)(2,1)S(1)}, u32[]{:S(2)}, u32[]{:S(2)}) collective-permute-start(bf16[4,4,304,128]{3,2,1,0:T(8,128)(2,1)S(1)} %both_ways.1), channel_id=1, source_target_pairs={{0,1},{1,0},{2,3},{3,2},{4,5},{5,4},{6,7},{7,6},{8,9},{9,8},{10,11... | collective-permute-start | bytes 3735560 | tf_op jit(solution)/shard_map/ppermute | solution.py:494
  80.9 1.5 only_behind.1.grad_ref
  82.4 1.2 collective-permute-done.1.came_ref
  83.6 0.3 add_pair.1
  84.0 20.2 %all_to_all.37.in_ref = bf16[4,4,304,128]{3,2,1,0:T(8,128)(2,1)S(1)} all-to-all(bf16[4,4,304,128]{3,2,1,0:T(8,128)(2,1)S(1)} %add_pair.1), channel_id=1, replica_groups=mesh['yh'=2,'z'=8,'yl'=4,'x'=4,'c'=2] {'x'}, dimensions={0} | all-to-all | bytes 2490368 | tf_op jit(solution)/shard_map/all_to_all | solution.py:418
  104.2 0.5 add_four.1
  104.7 20.9 %all_to_all.38 = bf16[64,2,1280]{2,1,0:T(2,128)(2,1)S(1)} all-to-all(bf16[64,2,1280]{2,1,0:T(2,128)(2,1)S(1)} %bitcast.44), channel_id=1, replica_groups=mesh['yh'=2,'z'=8,'yl'=4,'x'=4,'c'=2] {'yh','z','yl'}, dimensions={0} | all-to-all | bytes 655360 | tf_op jit(solution)/shard_map/all_to_all | solution.py:418
  125.6 0.6 combine.1
  126.2 2.0 %all-gather.1 = f32[528,128]{1,0:T(8,128)S(1)} all-gather(f32[264,128]{1,0:T(8,128)S(1)} %combine.1), channel_id=3, replica_groups=mesh['yh'=2,'z'=8,'yl'=4,'x'=4,'c'=2] {'c'}, dimensions={0}, use_global_device_ids=true | all-gather | bytes 405504 | tf_op jit(solution)/shard_map/all_gather | solution.py:507
  128.2 1.1 finish.1
  129.3 0.8 heads_back.1
  130.1 2.5 %collective-permute-start.2 = (bf16[2,4,64,128]{3,2,1,0:T(8,128)(2,1)S(1)}, bf16[2,4,64,128]{3,2,1,0:T(8,128)(2,1)S(1)}, u32[]{:S(2)}, u32[]{:S(2)}) collective-permute-start(bf16[2,4,64,128]{3,2,1,0:T(8,128)(2,1)S(1)} %get-tuple-element.48), channel_id=1, source_target_pairs={{0,2},{2,0},{4,6},{6,4},{1,3},{3,1},{5,7},{7,5},{8,10},{10,8},{12,... | collective-permute-start | bytes 393224 | tf_op jit(solution)/shard_map/ppermute | solution.py:422
  132.6 3.9 %all-to-all-start.5 = ((bf16[16,64,128]{2,1,0:T(8,128)(2,1)}), bf16[16,64,128]{2,1,0:T(8,128)(2,1)S(1)}, u32[]{:S(2)}, u32[]{:S(2)}) async-start(bf16[16,64,128]{2,1,0:T(8,128)(2,1)} %get-tuple-element.49), calls=%async_computation.5 | async-start | bytes 524288 | tf_op jit(solution)/shard_map/all_to_all | solution.py:418
  136.5 1.0 collective-permute-done.2
  137.6 3.1 %collective-permute-start.3 = (bf16[4,64,128]{2,1,0:T(8,128)(2,1)S(1)}, bf16[4,64,128]{2,1,0:T(8,128)(2,1)S(1)}, u32[]{:S(2)}, u32[]{:S(2)}) collective-permute-start(bf16[4,64,128]{2,1,0:T(8,128)(2,1)S(1)} %fusion.2), channel_id=1, source_target_pairs={{0,6},{2,4},{4,2},{6,0},{1,7},{3,5},{5,3},{7,1},{8,14},{10,12},{12... | collective-permute-start | bytes 196616 | tf_op jit(solution)/shard_map/ppermute | solution.py:424
  140.7 4.3 %collective-permute-done.3 = bf16[4,64,128]{2,1,0:T(8,128)(2,1)S(1)} collective-permute-done((bf16[4,64,128]{2,1,0:T(8,128)(2,1)S(1)}, bf16[4,64,128]{2,1,0:T(8,128)(2,1)S(1)}, u32[]{:S(2)}, u32[]{:S(2)}) %collective-permute-start.3) | collective-permute-done | bytes 65568 | tf_op jit(solution)/shard_map/ppermute | solution.py:424
  145.0 2.6 %collective-permute-start.4 = (bf16[2,64,128]{2,1,0:T(8,128)(2,1)S(1)}, bf16[2,64,128]{2,1,0:T(8,128)(2,1)S(1)}, u32[]{:S(2)}, u32[]{:S(2)}) collective-permute-start(bf16[2,64,128]{2,1,0:T(8,128)(2,1)S(1)} %slice.29), channel_id=1, source_target_pairs={{0,8},{8,0},{16,24},{24,16},{1,9},{9,1},{17,25},{25,17},{2,10},{10... | collective-permute-start | bytes 98312 | tf_op jit(solution)/shard_map/ppermute | solution.py:422
  147.7 4.3 %all-to-all-done.5 = bf16[16,64,128]{2,1,0:T(8,128)(2,1)S(1)} async-done(((bf16[16,64,128]{2,1,0:T(8,128)(2,1)}), bf16[16,64,128]{2,1,0:T(8,128)(2,1)S(1)}, u32[]{:S(2)}, u32[]{:S(2)}) %all-to-all-start.5) | async-done | bytes 262176 | tf_op jit(solution)/shard_map/all_to_all | solution.py:418
  152.0 0.8 broadcast_in_dim.7
  152.7 7.4 %all-to-all-start.6 = ((bf16[16,64,128]{2,1,0:T(8,128)(2,1)}), bf16[16,64,128]{2,1,0:T(8,128)(2,1)S(1)}, u32[]{:S(2)}, u32[]{:S(2)}) async-start(bf16[16,64,128]{2,1,0:T(8,128)(2,1)} %broadcast_in_dim.7), calls=%async_computation.6 | async-start | bytes 524288 | tf_op jit(solution)/shard_map/all_to_all | solution.py:418
  160.2 0.0 collective-permute-done.4
  160.2 2.7 %collective-permute-start.5 = (bf16[64,128]{1,0:T(8,128)(2,1)S(1)}, bf16[64,128]{1,0:T(8,128)(2,1)S(1)}, u32[]{:S(2)}, u32[]{:S(2)}) collective-permute-start(bf16[64,128]{1,0:T(8,128)(2,1)S(1)} %fusion.6), channel_id=1, source_target_pairs={{0,16},{8,24},{16,0},{24,8},{1,17},{9,25},{17,1},{25,9},{2,18},{10... | collective-permute-start | bytes 49160 | tf_op jit(solution)/shard_map/ppermute | solution.py:424
  163.0 3.8 %collective-permute-done.5 = bf16[64,128]{1,0:T(8,128)(2,1)S(1)} collective-permute-done((bf16[64,128]{1,0:T(8,128)(2,1)S(1)}, bf16[64,128]{1,0:T(8,128)(2,1)S(1)}, u32[]{:S(2)}, u32[]{:S(2)}) %collective-permute-start.5) | collective-permute-done | bytes 16416 | tf_op jit(solution)/shard_map/ppermute | solution.py:424
  166.8 0.6 fusion.5
  167.4 6.5 %all-to-all-done.6.in_ref = bf16[16,64,128]{2,1,0:T(8,128)(2,1)S(1)} async-done(((bf16[16,64,128]{2,1,0:T(8,128)(2,1)}), bf16[16,64,128]{2,1,0:T(8,128)(2,1)S(1)}, u32[]{:S(2)}, u32[]{:S(2)}) %all-to-all-start.6) | async-done | bytes 262176 | tf_op jit(solution)/shard_map/all_to_all | solution.py:418
  173.9 0.8 lay.1
  (9 shorter events, 0.1 us)
Async XLA Ops:
  0.6 12.3 %copy-start.3 = (f32[64]{0:T(128)S(1)}, f32[64]{0:T(128)}, u32[]{:S(2)}) copy-start(f32[64]{0:T(128)} %param.12) | copy-start | bytes 772
  0.6 12.3 %copy-start.2 = (f32[128,2]{0,1:T(2,128)S(1)}, f32[128,2]{0,1:T(2,128)}, u32[]{:S(2)}) copy-start(f32[128,2]{0,1:T(2,128)} %param.16) | copy-start | bytes 3076
  2.1 16.7 %all-to-all-start = ((bf16[16,64,128]{2,1,0:T(8,128)(2,1)}), bf16[16,64,128]{2,1,0:T(8,128)(2,1)S(1)}, u32[]{:S(2)}, u32[]{:S(2)}) async-start(bf16[16,64,128]{2,1,0:T(8,128)(2,1)} %broadcast_in_dim.6), calls=%async_computation | async-start | bytes 524288 | tf_op jit(solution)/shard_map/all_to_all | solution.py:418
  52.4 20.8 %copy-start.1 = (bf16[2,256,2048]{2,1,0:T(8,128)(2,1)S(1)}, bf16[2,256,2048]{2,1,0:T(8,128)(2,1)}, u32[]{:S(2)}) copy-start(bf16[2,256,2048]{2,1,0:T(8,128)(2,1)} %down_ref.5) | copy-start | bytes 6291460
  53.0 20.3 %copy-start = (bf16[2,2048,256]{2,1,0:T(8,128)(2,1)S(1)}, bf16[2,2048,256]{2,1,0:T(8,128)(2,1)}, u32[]{:S(2)}) copy-start(bf16[2,2048,256]{2,1,0:T(8,128)(2,1)} %up_ref.5) | copy-start | bytes 6291460
  71.3 4.8 %collective-permute-start = (bf16[4,4,304,128]{3,2,1,0:T(8,128)(2,1)S(1)}, bf16[4,4,304,128]{3,2,1,0:T(8,128)(2,1)S(1)}, u32[]{:S(2)}, u32[]{:S(2)}) collective-permute-start(bf16[4,4,304,128]{3,2,1,0:T(8,128)(2,1)S(1)} %all_to_all.36.in_ref), channel_id=1, source_target_pairs={{0,1},{1,0},{2,3},{3,2},{4,5},{5,4},{6,7},{7,6},{8,9},{9,8},{10,11... | collective-permute-start | bytes 3735560 | tf_op jit(solution)/shard_map/ppermute | solution.py:477
  78.8 4.8 %collective-permute-start.1 = (bf16[4,4,304,128]{3,2,1,0:T(8,128)(2,1)S(1)}, bf16[4,4,304,128]{3,2,1,0:T(8,128)(2,1)S(1)}, u32[]{:S(2)}, u32[]{:S(2)}) collective-permute-start(bf16[4,4,304,128]{3,2,1,0:T(8,128)(2,1)S(1)} %both_ways.1), channel_id=1, source_target_pairs={{0,1},{1,0},{2,3},{3,2},{4,5},{5,4},{6,7},{7,6},{8,9},{9,8},{10,11... | collective-permute-start | bytes 3735560 | tf_op jit(solution)/shard_map/ppermute | solution.py:494
  130.1 7.4 %collective-permute-start.2 = (bf16[2,4,64,128]{3,2,1,0:T(8,128)(2,1)S(1)}, bf16[2,4,64,128]{3,2,1,0:T(8,128)(2,1)S(1)}, u32[]{:S(2)}, u32[]{:S(2)}) collective-permute-start(bf16[2,4,64,128]{3,2,1,0:T(8,128)(2,1)S(1)} %get-tuple-element.48), channel_id=1, source_target_pairs={{0,2},{2,0},{4,6},{6,4},{1,3},{3,1},{5,7},{7,5},{8,10},{10,8},{12,... | collective-permute-start | bytes 393224 | tf_op jit(solution)/shard_map/ppermute | solution.py:422
  132.6 19.3 %all-to-all-start.5 = ((bf16[16,64,128]{2,1,0:T(8,128)(2,1)}), bf16[16,64,128]{2,1,0:T(8,128)(2,1)S(1)}, u32[]{:S(2)}, u32[]{:S(2)}) async-start(bf16[16,64,128]{2,1,0:T(8,128)(2,1)} %get-tuple-element.49), calls=%async_computation.5 | async-start | bytes 524288 | tf_op jit(solution)/shard_map/all_to_all | solution.py:418
  137.6 7.4 %collective-permute-start.3 = (bf16[4,64,128]{2,1,0:T(8,128)(2,1)S(1)}, bf16[4,64,128]{2,1,0:T(8,128)(2,1)S(1)}, u32[]{:S(2)}, u32[]{:S(2)}) collective-permute-start(bf16[4,64,128]{2,1,0:T(8,128)(2,1)S(1)} %fusion.2), channel_id=1, source_target_pairs={{0,6},{2,4},{4,2},{6,0},{1,7},{3,5},{5,3},{7,1},{8,14},{10,12},{12... | collective-permute-start | bytes 196616 | tf_op jit(solution)/shard_map/ppermute | solution.py:424
  145.0 15.2 %collective-permute-start.4 = (bf16[2,64,128]{2,1,0:T(8,128)(2,1)S(1)}, bf16[2,64,128]{2,1,0:T(8,128)(2,1)S(1)}, u32[]{:S(2)}, u32[]{:S(2)}) collective-permute-start(bf16[2,64,128]{2,1,0:T(8,128)(2,1)S(1)} %slice.29), channel_id=1, source_target_pairs={{0,8},{8,0},{16,24},{24,16},{1,9},{9,1},{17,25},{25,17},{2,10},{10... | collective-permute-start | bytes 98312 | tf_op jit(solution)/shard_map/ppermute | solution.py:422
  152.7 21.2 %all-to-all-start.6 = ((bf16[16,64,128]{2,1,0:T(8,128)(2,1)}), bf16[16,64,128]{2,1,0:T(8,128)(2,1)S(1)}, u32[]{:S(2)}, u32[]{:S(2)}) async-start(bf16[16,64,128]{2,1,0:T(8,128)(2,1)} %broadcast_in_dim.7), calls=%async_computation.6 | async-start | bytes 524288 | tf_op jit(solution)/shard_map/all_to_all | solution.py:418
  160.2 6.5 %collective-permute-start.5 = (bf16[64,128]{1,0:T(8,128)(2,1)S(1)}, bf16[64,128]{1,0:T(8,128)(2,1)S(1)}, u32[]{:S(2)}, u32[]{:S(2)}) collective-permute-start(bf16[64,128]{1,0:T(8,128)(2,1)S(1)} %fusion.6), channel_id=1, source_target_pairs={{0,16},{8,24},{16,0},{24,8},{1,17},{9,25},{17,1},{25,9},{2,18},{10... | collective-permute-start | bytes 49160 | tf_op jit(solution)/shard_map/ppermute | solution.py:424

commit v8 on v7

--- a/solution.py
+++ b/solution.py
@@ -204,7 +204,8 @@
 def repack(in_ref, pick_ref, out_ref):
     pick = pick_ref[...]
     for y in range(4):
-        rows = read_messages(in_ref, (y,)).astype(BF16)
+        rows = [in_ref[:, y, :, i * 128 : i * 128 + 128] for i in range(MSG // 2)]
+        rows = jnp.concatenate([pair.reshape(32, 128) for pair in rows], axis=0)
         packed = dot_nn(pick, rows).astype(BF16)
         for x in range(4):
             out_ref[x, y] = packed

time: 176 us -> 176 us (level)
  no operation moved by 1% of the time
where the time goes in v8:
time: 176 us; the launch traced here: 175 us
  blocking collectives  96.4 us (55%)
  starting transfers between devices  35.3 us (20%)
  waiting for transfers between devices  25.1 us (14%)
  Pallas kernels  12 us (7%)
  other arithmetic  2.49 us (1%)
  local copies, waits for them, and re-layouts  2.28 us (1%)
    all_to_all x4, blocking collectives, a2a(): return lax.all_to_all(value, axes, split_axis=0, concat_axis=0, tiled=True)  90 us
    all_to_all x3, starting transfers between devices, a2a(): return lax.all_to_all(value, axes, split_axis=0, concat_axis=0, tiled=True)  20.4 us
    all_to_all x3, waiting for transfers between devices, a2a(): return lax.all_to_all(value, axes, split_axis=0, concat_axis=0, tiled=True)  13.5 us
    ppermute x2, waiting for transfers between devices, halve(): lax.ppermute(half[1].astype(BF16), axis, [(i, i ^ far) for i in range(4)])  8.08 us
    ppermute x2, starting transfers between devices, halve(): lax.ppermute(half[1].astype(BF16), axis, [(i, i ^ far) for i in range(4)])  5.82 us
    ppermute x2, starting transfers between devices, halve(): came = lax.ppermute(send, axis, [(i, i ^ 1) for i in range(4)])  5.14 us
  transfers between devices with their start and end apart: 9, of which 8 were waited for; matrix products, arithmetic and copies ran while one was open for 2% of the time, Pallas kernels for 2%

profile of v8, /device:TPU:16, one launch (start us, length us, event | category | flops | bytes accessed | tf_op | source)
XLA Modules:
  0.0 174.6 jit_solution(11888132014674796811)
XLA Ops:
  0.6 0.0 copy-start.3
  0.6 0.0 copy-start.2
  0.7 1.5 broadcast_in_dim.6
  2.1 9.1 %all-to-all-start = ((bf16[16,64,128]{2,1,0:T(8,128)(2,1)}), bf16[16,64,128]{2,1,0:T(8,128)(2,1)S(1)}, u32[]{:S(2)}, u32[]{:S(2)}) async-start(bf16[16,64,128]{2,1,0:T(8,128)(2,1)} %broadcast_in_dim.6), calls=%async_computation | async-start | bytes 524288 | tf_op jit(solution)/shard_map/all_to_all | solution.py:419
  11.2 0.7 convert_bitcast_fusion
  11.9 1.0 pad_maximum_fusion.wide_ref
  12.9 0.0 copy-done.3
  12.9 0.0 copy-done.2
  13.0 0.4 prepare.1
  13.3 2.3 %all_gather.15.side_ref = bf16[128,2432]{1,0:T(8,128)(2,1)S(1)} all-gather(bf16[64,2432]{1,0:T(8,128)(2,1)S(1)} %get-tuple-element.27), channel_id=1, replica_groups=mesh['yh'=2,'z'=8,'yl'=4,'x'=4,'c'=2] {'c'}, dimensions={0}, use_global_device_ids=true | all-gather | bytes 933888 | tf_op jit(solution)/shard_map/all_gather | solution.py:457
  15.6 0.5 turn_weight.1.weight_ref
  16.0 0.1 pad_add_fusion.at_ref
  16.1 2.7 %all-to-all-done = bf16[16,64,128]{2,1,0:T(8,128)(2,1)S(1)} async-done(((bf16[16,64,128]{2,1,0:T(8,128)(2,1)}), bf16[16,64,128]{2,1,0:T(8,128)(2,1)S(1)}, u32[]{:S(2)}, u32[]{:S(2)}) %all-to-all-start) | async-done | bytes 262176 | tf_op jit(solution)/shard_map/all_to_all | solution.py:419
  18.8 2.2 %all-gather = bf16[32,64,128]{2,1,0:T(8,128)(2,1)S(1)} all-gather(bf16[16,64,128]{2,1,0:T(8,128)(2,1)S(1)} %all-to-all-done), channel_id=2, replica_groups=mesh['yh'=2,'z'=8,'yl'=4,'x'=4,'c'=2] {'c'}, dimensions={0}, use_global_device_ids=true | all-gather | bytes 786432 | tf_op jit(solution)/shard_map/all_gather | solution.py:461
  21.0 0.8 dispatch.1
  21.8 30.6 %all_to_all.35 = bf16[64,2,1280]{2,1,0:T(2,128)(2,1)S(1)} all-to-all(bf16[64,2,1280]{2,1,0:T(2,128)(2,1)S(1)} %bitcast.47), channel_id=1, replica_groups=mesh['yh'=2,'z'=8,'yl'=4,'x'=4,'c'=2] {'yh','z','yl'}, dimensions={0} | all-to-all | bytes 655360 | tf_op jit(solution)/shard_map/all_to_all | solution.py:419
  52.4 0.0 copy-start.1
  52.4 0.5 repack.1
  52.9 0.0 copy-start
  52.9 18.4 %all_to_all.36.in_ref = bf16[4,4,304,128]{3,2,1,0:T(8,128)(2,1)S(1)} all-to-all(bf16[4,4,304,128]{3,2,1,0:T(8,128)(2,1)S(1)} %repack.1), channel_id=1, replica_groups=mesh['yh'=2,'z'=8,'yl'=4,'x'=4,'c'=2] {'x'}, dimensions={0} | all-to-all | bytes 2490368 | tf_op jit(solution)/shard_map/all_to_all | solution.py:419
  71.3 1.9 %collective-permute-start = (bf16[4,4,304,128]{3,2,1,0:T(8,128)(2,1)S(1)}, bf16[4,4,304,128]{3,2,1,0:T(8,128)(2,1)S(1)}, u32[]{:S(2)}, u32[]{:S(2)}) collective-permute-start(bf16[4,4,304,128]{3,2,1,0:T(8,128)(2,1)S(1)} %all_to_all.36.in_ref), channel_id=1, source_target_pairs={{0,1},{1,0},{2,3},{3,2},{4,5},{5,4},{6,7},{7,6},{8,9},{9,8},{10,11... | collective-permute-start | bytes 3735560 | tf_op jit(solution)/shard_map/ppermute | solution.py:478
  73.2 0.0 copy-done.1
  73.2 0.0 copy-done
  73.2 1.6 only_ahead.1
  74.8 1.3 collective-permute-done.in_ref
  76.1 2.7 %both_ways.1 = bf16[4,4,304,128]{3,2,1,0:T(8,128)(2,1)S(1)} custom-call(s32[1]{0:T(128)S(6)} %sub.3.which_ref, bf16[4,4,304,128]{3,2,1,0:T(8,128)(2,1)S(1)} %collective-permute-done.in_ref, bf16[2,2048,256]{2,1,0:T(8,128)(2,1)S(1)} %copy-done, bf16[2,256,2048]{2,1,0:T(8,128)(2,1)S(1)} %copy-done.1), custom_call_target="tpu_custom_call" | custom-call | tf_op jit(solution)/shard_map/both_ways/pallas_call | solution.py:491
  78.8 2.0 %collective-permute-start.1 = (bf16[4,4,304,128]{3,2,1,0:T(8,128)(2,1)S(1)}, bf16[4,4,304,128]{3,2,1,0:T(8,128)(2,1)S(1)}, u32[]{:S(2)}, u32[]{:S(2)}) collective-permute-start(bf16[4,4,304,128]{3,2,1,0:T(8,128)(2,1)S(1)} %both_ways.1), channel_id=1, source_target_pairs={{0,1},{1,0},{2,3},{3,2},{4,5},{5,4},{6,7},{7,6},{8,9},{9,8},{10,11... | collective-permute-start | bytes 3735560 | tf_op jit(solution)/shard_map/ppermute | solution.py:495
  80.8 1.5 only_behind.1.grad_ref
  82.3 1.2 collective-permute-done.1.came_ref
  83.6 0.3 add_pair.1
  83.9 20.2 %all_to_all.37.in_ref = bf16[4,4,304,128]{3,2,1,0:T(8,128)(2,1)S(1)} all-to-all(bf16[4,4,304,128]{3,2,1,0:T(8,128)(2,1)S(1)} %add_pair.1), channel_id=1, replica_groups=mesh['yh'=2,'z'=8,'yl'=4,'x'=4,'c'=2] {'x'}, dimensions={0} | all-to-all | bytes 2490368 | tf_op jit(solution)/shard_map/all_to_all | solution.py:419
  104.1 0.5 add_four.1
  104.6 20.9 %all_to_all.38 = bf16[64,2,1280]{2,1,0:T(2,128)(2,1)S(1)} all-to-all(bf16[64,2,1280]{2,1,0:T(2,128)(2,1)S(1)} %bitcast.44), channel_id=1, replica_groups=mesh['yh'=2,'z'=8,'yl'=4,'x'=4,'c'=2] {'yh','z','yl'}, dimensions={0} | all-to-all | bytes 655360 | tf_op jit(solution)/shard_map/all_to_all | solution.py:419
  125.5 0.6 combine.1
  126.1 2.0 %all-gather.1 = f32[528,128]{1,0:T(8,128)S(1)} all-gather(f32[264,128]{1,0:T(8,128)S(1)} %combine.1), channel_id=3, replica_groups=mesh['yh'=2,'z'=8,'yl'=4,'x'=4,'c'=2] {'c'}, dimensions={0}, use_global_device_ids=true | all-gather | bytes 405504 | tf_op jit(solution)/shard_map/all_gather | solution.py:508
  128.1 1.1 finish.1
  129.2 0.8 heads_back.1
  130.0 2.5 %collective-permute-start.2 = (bf16[2,4,64,128]{3,2,1,0:T(8,128)(2,1)S(1)}, bf16[2,4,64,128]{3,2,1,0:T(8,128)(2,1)S(1)}, u32[]{:S(2)}, u32[]{:S(2)}) collective-permute-start(bf16[2,4,64,128]{3,2,1,0:T(8,128)(2,1)S(1)} %get-tuple-element.48), channel_id=1, source_target_pairs={{0,2},{2,0},{4,6},{6,4},{1,3},{3,1},{5,7},{7,5},{8,10},{10,8},{12,... | collective-permute-start | bytes 393224 | tf_op jit(solution)/shard_map/ppermute | solution.py:423
  132.5 3.9 %all-to-all-start.5 = ((bf16[16,64,128]{2,1,0:T(8,128)(2,1)}), bf16[16,64,128]{2,1,0:T(8,128)(2,1)S(1)}, u32[]{:S(2)}, u32[]{:S(2)}) async-start(bf16[16,64,128]{2,1,0:T(8,128)(2,1)} %get-tuple-element.49), calls=%async_computation.5 | async-start | bytes 524288 | tf_op jit(solution)/shard_map/all_to_all | solution.py:419
  136.5 1.0 collective-permute-done.2
  137.5 3.1 %collective-permute-start.3 = (bf16[4,64,128]{2,1,0:T(8,128)(2,1)S(1)}, bf16[4,64,128]{2,1,0:T(8,128)(2,1)S(1)}, u32[]{:S(2)}, u32[]{:S(2)}) collective-permute-start(bf16[4,64,128]{2,1,0:T(8,128)(2,1)S(1)} %fusion.2), channel_id=1, source_target_pairs={{0,6},{2,4},{4,2},{6,0},{1,7},{3,5},{5,3},{7,1},{8,14},{10,12},{12... | collective-permute-start | bytes 196616 | tf_op jit(solution)/shard_map/ppermute | solution.py:425
  140.6 4.3 %collective-permute-done.3 = bf16[4,64,128]{2,1,0:T(8,128)(2,1)S(1)} collective-permute-done((bf16[4,64,128]{2,1,0:T(8,128)(2,1)S(1)}, bf16[4,64,128]{2,1,0:T(8,128)(2,1)S(1)}, u32[]{:S(2)}, u32[]{:S(2)}) %collective-permute-start.3) | collective-permute-done | bytes 65568 | tf_op jit(solution)/shard_map/ppermute | solution.py:425
  144.9 2.6 %collective-permute-start.4 = (bf16[2,64,128]{2,1,0:T(8,128)(2,1)S(1)}, bf16[2,64,128]{2,1,0:T(8,128)(2,1)S(1)}, u32[]{:S(2)}, u32[]{:S(2)}) collective-permute-start(bf16[2,64,128]{2,1,0:T(8,128)(2,1)S(1)} %slice.29), channel_id=1, source_target_pairs={{0,8},{8,0},{16,24},{24,16},{1,9},{9,1},{17,25},{25,17},{2,10},{10... | collective-permute-start | bytes 98312 | tf_op jit(solution)/shard_map/ppermute | solution.py:423
  147.6 4.3 %all-to-all-done.5 = bf16[16,64,128]{2,1,0:T(8,128)(2,1)S(1)} async-done(((bf16[16,64,128]{2,1,0:T(8,128)(2,1)}), bf16[16,64,128]{2,1,0:T(8,128)(2,1)S(1)}, u32[]{:S(2)}, u32[]{:S(2)}) %all-to-all-start.5) | async-done | bytes 262176 | tf_op jit(solution)/shard_map/all_to_all | solution.py:419
  151.9 0.8 broadcast_in_dim.7
  152.7 7.4 %all-to-all-start.6 = ((bf16[16,64,128]{2,1,0:T(8,128)(2,1)}), bf16[16,64,128]{2,1,0:T(8,128)(2,1)S(1)}, u32[]{:S(2)}, u32[]{:S(2)}) async-start(bf16[16,64,128]{2,1,0:T(8,128)(2,1)} %broadcast_in_dim.7), calls=%async_computation.6 | async-start | bytes 524288 | tf_op jit(solution)/shard_map/all_to_all | solution.py:419
  160.1 0.0 collective-permute-done.4
  160.2 2.7 %collective-permute-start.5 = (bf16[64,128]{1,0:T(8,128)(2,1)S(1)}, bf16[64,128]{1,0:T(8,128)(2,1)S(1)}, u32[]{:S(2)}, u32[]{:S(2)}) collective-permute-start(bf16[64,128]{1,0:T(8,128)(2,1)S(1)} %fusion.6), channel_id=1, source_target_pairs={{0,16},{8,24},{16,0},{24,8},{1,17},{9,25},{17,1},{25,9},{2,18},{10... | collective-permute-start | bytes 49160 | tf_op jit(solution)/shard_map/ppermute | solution.py:425
  162.9 3.8 %collective-permute-done.5 = bf16[64,128]{1,0:T(8,128)(2,1)S(1)} collective-permute-done((bf16[64,128]{1,0:T(8,128)(2,1)S(1)}, bf16[64,128]{1,0:T(8,128)(2,1)S(1)}, u32[]{:S(2)}, u32[]{:S(2)}) %collective-permute-start.5) | collective-permute-done | bytes 16416 | tf_op jit(solution)/shard_map/ppermute | solution.py:425
  166.7 0.6 fusion.5
  167.3 6.5 %all-to-all-done.6.in_ref = bf16[16,64,128]{2,1,0:T(8,128)(2,1)S(1)} async-done(((bf16[16,64,128]{2,1,0:T(8,128)(2,1)}), bf16[16,64,128]{2,1,0:T(8,128)(2,1)S(1)}, u32[]{:S(2)}, u32[]{:S(2)}) %all-to-all-start.6) | async-done | bytes 262176 | tf_op jit(solution)/shard_map/all_to_all | solution.py:419
  173.8 0.8 lay.1
  (9 shorter events, 0.1 us)
Async XLA Ops:
  0.6 12.3 %copy-start.3 = (f32[64]{0:T(128)S(1)}, f32[64]{0:T(128)}, u32[]{:S(2)}) copy-start(f32[64]{0:T(128)} %param.12) | copy-start | bytes 772
  0.6 12.3 %copy-start.2 = (f32[128,2]{0,1:T(2,128)S(1)}, f32[128,2]{0,1:T(2,128)}, u32[]{:S(2)}) copy-start(f32[128,2]{0,1:T(2,128)} %param.16) | copy-start | bytes 3076
  2.1 16.7 %all-to-all-start = ((bf16[16,64,128]{2,1,0:T(8,128)(2,1)}), bf16[16,64,128]{2,1,0:T(8,128)(2,1)S(1)}, u32[]{:S(2)}, u32[]{:S(2)}) async-start(bf16[16,64,128]{2,1,0:T(8,128)(2,1)} %broadcast_in_dim.6), calls=%async_computation | async-start | bytes 524288 | tf_op jit(solution)/shard_map/all_to_all | solution.py:419
  52.4 20.8 %copy-start.1 = (bf16[2,256,2048]{2,1,0:T(8,128)(2,1)S(1)}, bf16[2,256,2048]{2,1,0:T(8,128)(2,1)}, u32[]{:S(2)}) copy-start(bf16[2,256,2048]{2,1,0:T(8,128)(2,1)} %down_ref.5) | copy-start | bytes 6291460
  52.9 20.3 %copy-start = (bf16[2,2048,256]{2,1,0:T(8,128)(2,1)S(1)}, bf16[2,2048,256]{2,1,0:T(8,128)(2,1)}, u32[]{:S(2)}) copy-start(bf16[2,2048,256]{2,1,0:T(8,128)(2,1)} %up_ref.5) | copy-start | bytes 6291460
  71.3 4.8 %collective-permute-start = (bf16[4,4,304,128]{3,2,1,0:T(8,128)(2,1)S(1)}, bf16[4,4,304,128]{3,2,1,0:T(8,128)(2,1)S(1)}, u32[]{:S(2)}, u32[]{:S(2)}) collective-permute-start(bf16[4,4,304,128]{3,2,1,0:T(8,128)(2,1)S(1)} %all_to_all.36.in_ref), channel_id=1, source_target_pairs={{0,1},{1,0},{2,3},{3,2},{4,5},{5,4},{6,7},{7,6},{8,9},{9,8},{10,11... | collective-permute-start | bytes 3735560 | tf_op jit(solution)/shard_map/ppermute | solution.py:478
  78.8 4.8 %collective-permute-start.1 = (bf16[4,4,304,128]{3,2,1,0:T(8,128)(2,1)S(1)}, bf16[4,4,304,128]{3,2,1,0:T(8,128)(2,1)S(1)}, u32[]{:S(2)}, u32[]{:S(2)}) collective-permute-start(bf16[4,4,304,128]{3,2,1,0:T(8,128)(2,1)S(1)} %both_ways.1), channel_id=1, source_target_pairs={{0,1},{1,0},{2,3},{3,2},{4,5},{5,4},{6,7},{7,6},{8,9},{9,8},{10,11... | collective-permute-start | bytes 3735560 | tf_op jit(solution)/shard_map/ppermute | solution.py:495
  130.0 7.4 %collective-permute-start.2 = (bf16[2,4,64,128]{3,2,1,0:T(8,128)(2,1)S(1)}, bf16[2,4,64,128]{3,2,1,0:T(8,128)(2,1)S(1)}, u32[]{:S(2)}, u32[]{:S(2)}) collective-permute-start(bf16[2,4,64,128]{3,2,1,0:T(8,128)(2,1)S(1)} %get-tuple-element.48), channel_id=1, source_target_pairs={{0,2},{2,0},{4,6},{6,4},{1,3},{3,1},{5,7},{7,5},{8,10},{10,8},{12,... | collective-permute-start | bytes 393224 | tf_op jit(solution)/shard_map/ppermute | solution.py:423
  132.5 19.3 %all-to-all-start.5 = ((bf16[16,64,128]{2,1,0:T(8,128)(2,1)}), bf16[16,64,128]{2,1,0:T(8,128)(2,1)S(1)}, u32[]{:S(2)}, u32[]{:S(2)}) async-start(bf16[16,64,128]{2,1,0:T(8,128)(2,1)} %get-tuple-element.49), calls=%async_computation.5 | async-start | bytes 524288 | tf_op jit(solution)/shard_map/all_to_all | solution.py:419
  137.5 7.4 %collective-permute-start.3 = (bf16[4,64,128]{2,1,0:T(8,128)(2,1)S(1)}, bf16[4,64,128]{2,1,0:T(8,128)(2,1)S(1)}, u32[]{:S(2)}, u32[]{:S(2)}) collective-permute-start(bf16[4,64,128]{2,1,0:T(8,128)(2,1)S(1)} %fusion.2), channel_id=1, source_target_pairs={{0,6},{2,4},{4,2},{6,0},{1,7},{3,5},{5,3},{7,1},{8,14},{10,12},{12... | collective-permute-start | bytes 196616 | tf_op jit(solution)/shard_map/ppermute | solution.py:425
  144.9 15.2 %collective-permute-start.4 = (bf16[2,64,128]{2,1,0:T(8,128)(2,1)S(1)}, bf16[2,64,128]{2,1,0:T(8,128)(2,1)S(1)}, u32[]{:S(2)}, u32[]{:S(2)}) collective-permute-start(bf16[2,64,128]{2,1,0:T(8,128)(2,1)S(1)} %slice.29), channel_id=1, source_target_pairs={{0,8},{8,0},{16,24},{24,16},{1,9},{9,1},{17,25},{25,17},{2,10},{10... | collective-permute-start | bytes 98312 | tf_op jit(solution)/shard_map/ppermute | solution.py:423
  152.7 21.2 %all-to-all-start.6 = ((bf16[16,64,128]{2,1,0:T(8,128)(2,1)}), bf16[16,64,128]{2,1,0:T(8,128)(2,1)S(1)}, u32[]{:S(2)}, u32[]{:S(2)}) async-start(bf16[16,64,128]{2,1,0:T(8,128)(2,1)} %broadcast_in_dim.7), calls=%async_computation.6 | async-start | bytes 524288 | tf_op jit(solution)/shard_map/all_to_all | solution.py:419
  160.2 6.5 %collective-permute-start.5 = (bf16[64,128]{1,0:T(8,128)(2,1)S(1)}, bf16[64,128]{1,0:T(8,128)(2,1)S(1)}, u32[]{:S(2)}, u32[]{:S(2)}) collective-permute-start(bf16[64,128]{1,0:T(8,128)(2,1)S(1)} %fusion.6), channel_id=1, source_target_pairs={{0,16},{8,24},{16,0},{24,8},{1,17},{9,25},{17,1},{25,9},{2,18},{10... | collective-permute-start | bytes 49160 | tf_op jit(solution)/shard_map/ppermute | solution.py:425
